TPU v7x, 32 devices: a whole 2x2x4 slice. The times are simulated.
32 devices in a mesh: tm: 8 (over z, y), head: 4 (over x, core).
Axes of the slice: x: 2, y: 2, z: 4, core: 2. Of those that a mesh axis runs over, the one named last changes fastest.
Arguments:
- series: bfloat16 [2048, 512], P('tm'), may hold values from -6 to 6
- in_weight: bfloat16 [512, 3, 1024], P(None, None, 'head'), may hold values from -0.25 to 0.25
- step_weight: bfloat16 [512, 16], P(None, 'head'), may hold values from -0.25 to 0.25
- step_bias: float32 [16], P('head'), may hold values from -7 to -6
- log_rate: float32 [16], P('head'), as said below
- conv_weight: float32 [4, 2, 1024], P(None, None, 'head'), may hold values from -3 to 3
- conv_bias: float32 [2, 1024], P(None, 'head'), may hold values from -3 to 3
- skip_gain: float32 [16], P('head'), may hold values from 0.5 to 1.5
- norm_gain: float32 [1024], P('head'), may hold values from 0.1 to 1.9
- out_weight: bfloat16 [512, 1024], P(None, 'head'), may hold values from -0.1875 to 0.1875
- cotangent: bfloat16 [2048, 512], P('tm'), may hold values from -6 to 6
Outputs:
- layer_out: bfloat16 [2048, 512], P(('tm', 'head'))
- series_grad: float32 [2048, 512], P(('tm', 'head'))
- w_in_grad: float32 [512, 3, 1024], P('tm', None, 'head')
- w_dt_grad: float32 [512, 16], P('tm', 'head')
- w_out_grad: float32 [512, 1024], P('tm', 'head')
Inputs may be any that keep to these rules, and one draw needn't show every extreme that they name: `log_rate`: each head's logarithm of its decay rate.
All inputs are finite; a program needn't handle non-finite values.
Results may differ from a plain program's by a relative error of at most 0.0076.
Values may be sent and summed in bfloat16 or wider, within the bound.
No kernel may reach another device: no remote copies, remote signals or barrier semaphores. Data moves between devices by JAX's collectives and lax.ppermute only.
A program may use at most 64 MiB of HBM per device.

v0:
```python
import functools

import jax
import jax.numpy as jnp
from jax import lax
from jax.experimental import pallas as pl
from jax.experimental.pallas import tpu as pltpu
from jax.sharding import PartitionSpec as P

N = 128
KW = 4
RIM = 16
LIMIT = 12 * 2**20
SPARE = 4
SKIP, GAIN, BIAS, TAPS, SCALARS = 16, 17, 18, 20, 32
LOGS = 16
NORM_EPSILON = 1e-05

F32 = jnp.float32
BF16 = jnp.bfloat16
NN = (((1,), (0,)), ((), ()))
NT = (((1,), (1,)), ((), ()))
TN = (((0,), (0,)), ((), ()))


def mm(a, b, dims=NN):
    return lax.dot_general(a.astype(BF16), b.astype(BF16), dims, preferred_element_type=F32)


def mm_exact(a, b, dims=NN):
    return lax.dot_general(
        a, b, dims, precision=lax.Precision.HIGHEST, preferred_element_type=F32
    )


def lanes_of(shape):
    return lax.broadcasted_iota(jnp.int32, shape, len(shape) - 1)


def rows_of(shape):
    return lax.broadcasted_iota(jnp.int32, shape, len(shape) - 2)


def per_row(ref, shape):
    rows = rows_of(shape)
    out = jnp.full(shape, ref[0], F32)
    for h in range(1, shape[0]):
        out = jnp.where(rows == h, ref[h], out)
    return out


def per_lane(ref, heads, width):
    head = lanes_of((1, width)) // (width // heads)
    out = jnp.full((1, width), ref[0], F32)
    for h in range(1, heads):
        out = jnp.where(head == h, ref[h], out)
    return out


def widen(cols, heads, width):
    head = lanes_of((cols.shape[0], width)) // (width // heads)
    out = jnp.broadcast_to(cols[:, 0:1], (cols.shape[0], width))
    for h in range(1, heads):
        out = jnp.where(head == h, cols[:, h : h + 1], out)
    return out


def head_mask(heads, width):
    shape = (8, width)
    return jnp.where(lanes_of(shape) // (width // heads) == rows_of(shape), 1.0, 0.0)


def only_head(x, h, heads):
    width = x.shape[1]
    return jnp.where(lanes_of(x.shape) // (width // heads) == h, x, jnp.zeros_like(x))


def tap(scal, k, slot):
    return scal[TAPS + 2 * k + slot : TAPS + 2 * k + slot + 1, :]


def columns(rows):
    short = -rows.shape[0] % 8
    if short:
        rows = jnp.concatenate([rows, jnp.zeros((short, rows.shape[1]), F32)], axis=0)
    return jnp.transpose(rows)


def sigmoid(v):
    return 1.0 / (1.0 + jnp.exp(-v))


def running_sum(x):
    width = x.shape[1]
    lanes = lanes_of(x.shape)
    hop = 1
    while hop < width:
        x = x + jnp.where(lanes >= hop, pltpu.roll(x, hop, 1), 0.0)
        hop *= 2
    return x


def running_sum_back(x):
    width = x.shape[1]
    lanes = lanes_of(x.shape)
    hop = 1
    while hop < width:
        x = x + jnp.where(lanes < width - hop, pltpu.roll(x, width - hop, 1), 0.0)
        hop *= 2
    return x


def decay_of(cols, rows, h):
    length = cols.shape[0]
    gap = cols[:, h : h + 1] - rows[h : h + 1, :]
    shape = (length, length)
    return jnp.exp(jnp.where(lanes_of(shape) <= rows_of(shape), gap, -1e30))


def logs_of(msg, heads):
    logs = msg[msg.shape[0] - LOGS :].astype(F32)
    return logs[0:heads] + logs[heads : 2 * heads] + logs[2 * heads : 3 * heads]


def spread_rows(logs, heads, size):
    return jnp.concatenate(
        [jnp.broadcast_to(logs[h : h + 1], (size // heads, N)) for h in range(heads)], axis=0
    )


def state_of(msg):
    return msg[0 : msg.shape[0] - LOGS].astype(F32)


def packed(state, logs):
    high = logs.astype(BF16).astype(F32)
    middle = (logs - high).astype(BF16).astype(F32)
    low = logs - high - middle
    logs = jnp.concatenate([high, middle, low, jnp.zeros_like(low)], axis=0)
    return jnp.concatenate([state.astype(BF16), logs.astype(BF16)], axis=0)


def carried(own_turn, partner, far, near, heads):
    state = state_of(far)
    size = state.shape[0]
    if near is not None:
        state = near[0:size, 0:N] + near[0:size, N:] * state
    with_partner = jnp.exp(spread_rows(logs_of(partner, heads), heads, size)) * state
    return jnp.where(own_turn, with_partner + state_of(partner), state)


def project_kernel(
    heads, series, w, dtw, bias, rate, skip, gain, cw, cb, gate, pre, scal, w_xbc,
):
    width = w.shape[2]
    s = series[...]
    gate[...] = mm(s, w[0]).astype(BF16)
    pre[:, 0:width] = mm(s, w[1]).astype(BF16)
    pre[:, width:] = mm(s, w[2]).astype(BF16)
    w_xbc[0] = w[1]
    w_xbc[1] = w[2]
    raw = mm(dtw[...], s, NT)
    shifted = raw + per_row(bias, raw.shape)
    step = jnp.maximum(shifted, 0.0) + jnp.log1p(jnp.exp(-jnp.abs(shifted)))
    rates = jnp.exp(per_row(rate, raw.shape))
    scal[0:heads, :] = running_sum(-step * rates)
    scal[heads : 2 * heads, :] = step
    scal[2 * heads : 3 * heads, :] = sigmoid(shifted)
    scal[3 * heads : SKIP, :] = rates
    scal[SKIP : SKIP + 1, :] = per_lane(skip, heads, width)
    scal[GAIN : GAIN + 1, :] = gain[...]
    scal[BIAS : BIAS + 2, :] = cb[...]
    for k in range(KW):
        scal[TAPS + 2 * k : TAPS + 2 * k + 2, :] = cw[k]
    scal[TAPS + 2 * KW :, :] = jnp.zeros((SCALARS - TAPS - 2 * KW, width), F32)


def conv_kernel(heads, pre, rim, w, scal, x, bc, conv, msg, wide):
    length, both = pre.shape
    width = both // 2
    for s in range(2):
        cut = slice(s * width, (s + 1) * width)
        rims = mm(rim[...], w[s]).astype(BF16).astype(F32)
        wide[0:8, cut] = rims[RIM - 8 :, :]
        wide[8:, cut] = pre[:, cut].astype(F32)
        acc = scal[BIAS + s : BIAS + s + 1, :] + tap(scal, 0, s) * wide[5 : 5 + length, cut]
        for k in range(1, KW):
            acc = acc + tap(scal, k, s) * wide[5 + k : 5 + k + length, cut]
        conv[:, cut] = acc
        act = (acc * sigmoid(acc)).astype(BF16)
        if s == 0:
            x[...] = act
        else:
            bc[...] = act
    running = scal[0:heads, :]
    last = running[:, length - 1 : length]
    remain = jnp.exp(last - running) * scal[heads : 2 * heads, :]
    scaled = x[...].astype(F32) * widen(columns(remain), heads, width)
    state = mm(scaled, bc[:, 0:N], TN)
    msg[...] = packed(state, jnp.broadcast_to(last, (heads, N)))


def pair_kernel(heads, back, low, mine, other, msg):
    mine, other = mine[...], other[...]
    size = mine.shape[0] - LOGS
    mine_first = low[0] == 0
    mine_logs, other_logs = logs_of(mine, heads), logs_of(other, heads)
    crossed = jnp.logical_not(mine_first) if back else mine_first
    mine_scale = jnp.where(crossed, jnp.exp(other_logs), 1.0)
    other_scale = jnp.where(crossed, 1.0, jnp.exp(mine_logs))
    state = spread_rows(mine_scale, heads, size) * state_of(mine)
    state = state + spread_rows(other_scale, heads, size) * state_of(other)
    msg[...] = packed(state, mine_logs + other_logs)


def link_kernel(heads, farther, nearer, *rest):
    *before, msg, near = rest
    farther, nearer = farther[...], nearer[...]
    size = nearer.shape[0] - LOGS
    logs, more = logs_of(nearer, heads), logs_of(farther, heads)
    state = state_of(farther)
    msg[...] = packed(
        jnp.exp(spread_rows(logs, heads, size)) * state + state_of(nearer), logs + more
    )
    scale = jnp.exp(spread_rows(more, heads, size))
    if before:
        state = before[0][0:size, 0:N] + before[0][0:size, N:] * state
        scale = before[0][0:size, N:] * scale
    near[0:size, 0:N] = state
    near[0:size, N:] = scale


def inside_kernel(heads, x, bc, scal, cot, ow, conv, y, gg, slope):
    length, width = x.shape
    xv = x[...].astype(F32)
    rows = scal[0 : 2 * heads, :]
    cols = columns(rows)
    scores = mm(bc[:, N:], bc[:, 0:N], NT)
    acc = scal[SKIP : SKIP + 1, :] * xv
    for h in range(heads):
        mixing = scores * decay_of(cols, rows, h) * rows[heads + h : heads + h + 1, :]
        acc = acc + mm(mixing, only_head(xv, h, heads))
    y[...] = acc
    gg[...] = scal[GAIN : GAIN + 1, :] * mm(cot[...], ow[...])
    v = conv[...]
    sig = sigmoid(v)
    slope[...] = sig * (1.0 + v * (1.0 - sig))


def join_kernel(heads, low, yi, gg, gate, bc, scal, partner, *rest):
    far, *near, y, sin, sums = rest
    length, width = yi.shape
    start = carried(low[0] == 1, partner[...], far[...], near[0] if near else None, heads)
    sin[...] = start
    grow = widen(columns(jnp.exp(scal[0:heads, :])), heads, width)
    yv = yi[...] + grow * mm(bc[:, N:], start, NT)
    y[...] = yv
    g = gate[...].astype(F32)
    gated = yv * (g * sigmoid(g))
    ones = jnp.ones((8, width), F32)
    square = mm_exact(ones, gated * gated, NT)
    inner = mm_exact(ones, gated * gg[...], NT)
    sums[...] = jnp.where(rows_of(square.shape) == 0, square, inner)


def norm_columns(total, every):
    inv = lax.rsqrt(total[0:1, :] / every + NORM_EPSILON)
    coef = inv * inv * inv * total[1:2, :] / every
    return columns(jnp.concatenate([inv, coef], axis=0))


def grad_y_kernel(heads, every, sums, other, y, gate, gg, bc, scal, gy, msg, total):
    length, width = y.shape
    total[...] = sums[...] + other[...]
    cols = norm_columns(total[...], every)
    g = gate[...].astype(F32)
    act = g * sigmoid(g)
    gated = y[...] * act
    grad = (cols[:, 0:1] * gg[...] - gated * cols[:, 1:2]) * act
    gy[...] = grad
    grow = widen(columns(jnp.exp(scal[0:heads, :])), heads, width)
    last = scal[0:heads, length - 1 : length]
    msg[...] = packed(mm(grad * grow, bc[:, N:], TN), jnp.broadcast_to(last, (heads, N)))


def conv_back(scal, wide, cut, length, slot, slot_cut):
    acc = tap(scal, 0, slot)[:, slot_cut] * wide[KW - 1 : KW - 1 + RIM + length, cut]
    for k in range(1, KW):
        at = KW - 1 - k
        acc = acc + tap(scal, k, slot)[:, slot_cut] * wide[at : at + RIM + length, cut]
    return acc.astype(BF16)


def clear_ends(wide, length):
    zeros = jnp.zeros((RIM, wide.shape[1]), F32)
    wide[0:RIM, :] = zeros
    wide[RIM + length :, :] = zeros[0:8]


def stack_columns(msg, grad, at, base, piece):
    for q in range(grad.shape[1] // N):
        msg[at, (base + q) * piece : (base + q + 1) * piece, :] = grad[
            at * piece : (at + 1) * piece, q * N : (q + 1) * N
        ]


def split_pair(low, every, keep, send):
    for at in range(send.shape[0]):
        keep[at] = every[2 * at + low]
        send[at] = every[2 * at + 1 - low]


def early_kernel(
    heads, count, every,
    low, total, y, gate, gg, gy, x, bc, scal, sin, cot, series, rim, slope,
    normed, grad_gate, gp, gb, edge, keep, send, wide, stage,
):
    length, width = y.shape
    depth = series.shape[1]
    rows = scal[0 : 2 * heads, :]
    cols = columns(rows)
    xv = x[...]
    gyv = gy[...].astype(BF16)
    b, c = bc[:, 0:N], bc[:, N:]
    group = jnp.zeros((length, length), F32)
    for h in range(heads):
        pairs = mm(only_head(gyv, h, heads), xv, NT)
        group = group + decay_of(cols, rows, h) * pairs * rows[heads + h : heads + h + 1, :]
    gb[...] = mm(group, c, TN)
    grow = widen(columns(jnp.exp(rows[0:heads])), heads, width)
    grad_c = mm(group, b) + mm(gy[...] * grow, sin[...])
    clear_ends(wide, length)
    wide[RIM : RIM + length, :] = grad_c * slope[:, 2 * width - N :]
    grad_pre = conv_back(scal, wide, slice(0, N), length, 1, slice(width - N, width))
    edge[...] = grad_pre[0:RIM]
    gp[...] = grad_pre[RIM:]
    cols = norm_columns(total[...], every)
    g = gate[...].astype(F32)
    sig = sigmoid(g)
    yv = y[...]
    gated = yv * (g * sig)
    normed[...] = (gated * cols[:, 0:1] * scal[GAIN : GAIN + 1, :]).astype(BF16)
    grad_gated = cols[:, 0:1] * gg[...] - gated * cols[:, 1:2]
    grad_gate[...] = (grad_gated * yv * (sig * (1.0 + g * (1.0 - sig)))).astype(BF16)
    w_out = mm(cot[...], normed[...], TN).astype(BF16)
    w_gate = mm(series[...], grad_gate[...], TN).astype(BF16)
    w_c = (mm(series[...], gp[...], TN) + mm(rim[...], edge[...], TN)).astype(BF16)
    piece = depth // count
    for at in range(count):
        stack_columns(stage, w_out, at, 0, piece)
        stack_columns(stage, w_gate, at, 2, piece)
        stack_columns(stage, w_c, at, 4, piece)
    split_pair(low[0], stage, keep, send)


def beside_kernel(
    heads, normed, grad_gate, gp, gb, y, gy, x, bc, scal, sin, ow, w, series,
    sg, held, yb, turned,
):
    length, width = y.shape
    rows = scal[0 : 2 * heads, :]
    cols = columns(rows)
    xv = x[...].astype(F32)
    gyv = gy[...]
    scores = mm(bc[:, N:], bc[:, 0:N], NT)
    back = jnp.zeros((length, width), F32)
    for h in range(heads):
        back = back + mm(scores * decay_of(cols, rows, h), only_head(gyv, h, heads), TN)
    held[:, 0:width] = back
    held[:, width : width + N] = gb[...]
    last = rows[0:heads, length - 1 : length]
    remain = jnp.exp(last - rows[0:heads]) * rows[heads:]
    own = mm(xv * widen(columns(remain), heads, width), bc[:, 0:N], TN)
    whole = jnp.exp(spread_rows(jnp.broadcast_to(last, (heads, N)), heads, width))
    held[:, width + N :] = whole * sin[...] + own
    turned[0 : series.shape[1], :] = jnp.transpose(series[...])
    skips = scal[SKIP : SKIP + 1, :]
    yb[...] = mm_exact(head_mask(heads, width), gyv * (y[...] - skips * xv), NT)
    depth = series.shape[1]
    sg[:, 0:depth] = mm(normed[...], ow[...], NT)
    sg[:, depth:] = mm(grad_gate[...], w[0], NT) + mm(gp[...], w[2, :, width - N :], NT)


def close_kernel(
    heads,
    low, x, bc, scal, gy, held, slope, edge_c, partner, *rest,
):
    far, *near, back, gp, lead, edge, wide = rest
    length, width = gy.shape
    state = carried(low[0] == 0, partner[...], far[...], near[0] if near else None, heads)
    back[0:width, width:] = state
    running, step = scal[0:heads, :], scal[heads : 2 * heads, :]
    remain = jnp.exp(running[:, length - 1 : length] - running)
    cols = columns(jnp.concatenate([remain, step, remain * step], axis=0))
    grown = held[:, 0:width] + widen(cols, heads, width) * mm(bc[:, 0:N], state, NT)
    back[0:length, 0:width] = grown
    grad_x = scal[SKIP : SKIP + 1, :] * gy[...] + widen(cols[:, heads:], heads, width) * grown
    grad_b = held[:, width : width + N] + mm(x[...].astype(F32) * widen(cols[:, 2 * heads :], heads, width), state)
    clear_ends(wide, length)
    wide[RIM : RIM + length, 0:width] = grad_x * slope[:, 0:width]
    wide[RIM : RIM + length, width:] = grad_b * slope[:, width : width + N]
    grad_x = conv_back(scal, wide, slice(0, width), length, 0, slice(0, width))
    grad_b = conv_back(scal, wide, slice(width, width + N), length, 1, slice(0, N))
    for out, cut in ((lead, slice(0, RIM)), (gp, slice(RIM, RIM + length))):
        out[:, 0:width] = grad_x[cut]
        out[:, width:] = grad_b[cut]
    edge[:, 0 : width + N] = lead[...]
    edge[:, width + N :] = edge_c[...]


def late_kernel(
    heads, count,
    low, x, scal, back, gp, lead, yb, held, turned, series, rim,
    keep, send, graw, stage,
):
    length, width = x.shape
    depth = series.shape[1]
    w_xb = (mm(turned[0:depth, :], gp[...]) + mm(rim[...], lead[...], TN)).astype(BF16)
    rows = scal[0 : 4 * heads, :]
    step = rows[heads : 2 * heads]
    mask = head_mask(heads, width)
    x_back = mm_exact(mask, x[...].astype(F32) * back[0:length, 0:width], NT)[0:heads]
    ends = jnp.sum(mm_exact(mask, back[0:width, width:] * held[:, width + N :]), axis=1, keepdims=True)[0:heads]
    grad_log = running_sum_back(yb[0:heads, :] - step * x_back) + ends
    grad_step = x_back - rows[3 * heads :] * grad_log
    grad_raw = grad_step * rows[2 * heads : 3 * heads]
    grad_raw = jnp.concatenate([grad_raw, jnp.zeros_like(grad_raw)], axis=0)
    graw[...] = grad_raw
    dt = mm(grad_raw, series[...])
    piece = depth // count
    blank = jnp.zeros((LOGS, N), F32)
    for at in range(count):
        stack_columns(stage, w_xb, at, 0, piece)
        dt_piece = jnp.concatenate(
            [dt[:, at * piece : (at + 1) * piece], blank[0 : 2 * heads, 0 : N - piece]], axis=1
        )
        dt_piece = jnp.concatenate([dt_piece, blank[0 : LOGS - 2 * heads]], axis=0)
        stage[at, 3 * piece :, :] = dt_piece.astype(BF16)
    split_pair(low[0], stage, keep, send)


def halve_kernel(high, keep, other, own, *parts):
    at = high[0]
    own[0 : other.shape[1], :] = keep[at].astype(F32) + other[at].astype(F32)
    for k, part in enumerate(parts):
        at = high[0] ^ (k + 1)
        part[...] = (keep[at].astype(F32) + other[at].astype(F32)).astype(BF16)


def rows_kernel(low, sg, gp, graw, edge, w, dtw, keep, send, stage):
    length, depth = sg.shape[0], sg.shape[1] // 2
    width = w.shape[2]
    heads = dtw.shape[0]
    total = sg[:, depth:] + mm(graw[0:heads, :], dtw[...], TN)
    total = total + mm(gp[:, 0:width], w[1], NT) + mm(gp[:, width:], w[2, :, 0:N], NT)
    late = mm(edge[:, 0:width], w[1], NT) + mm(edge[:, width:], w[2], NT)
    stage[:, 0:depth] = sg[:, 0:depth].astype(BF16)
    stage[:, depth:] = total.astype(BF16)
    stage[length - RIM :, depth:] = (total[length - RIM :, :] + late).astype(BF16)
    piece = keep.shape[1]
    for at in range(send.shape[0]):
        start = pl.multiple_of((2 * at + low[0]) * piece, piece)
        keep[at] = stage[pl.ds(start, piece), :]
        start = pl.multiple_of((2 * at + 1 - low[0]) * piece, piece)
        send[at] = stage[pl.ds(start, piece), :]


def sum_of(parts):
    rows = parts[-1].shape[0]
    total = parts[0][0:rows, :]
    for part in parts[1:]:
        total = total + part[...].astype(F32)
    return total


def outputs_kernel(*refs):
    *parts, layer, grad = refs
    depth = layer.shape[1]
    total = sum_of(parts)
    layer[...] = total[:, 0:depth].astype(BF16)
    grad[...] = total[:, depth:]


def early_sum_kernel(*refs):
    *parts, w_out, others = refs
    piece = w_out.shape[0]
    total = sum_of(parts)
    for q in range(2):
        w_out[:, q * N : (q + 1) * N] = total[q * piece : (q + 1) * piece, :]
    others[0 : 3 * piece, :] = total[2 * piece :, :]


def total_kernel(early, *refs):
    *parts, w_in, w_dt = refs
    piece = w_in.shape[1]
    late = sum_of(parts)
    for q in range(2):
        cut = slice(q * N, (q + 1) * N)
        w_in[0, :, cut] = early[q * piece : (q + 1) * piece, :]
        w_in[1, :, cut] = late[q * piece : (q + 1) * piece, :]
    w_in[2, :, 0:N] = late[2 * piece : 3 * piece, :]
    w_in[2, :, N:] = early[2 * piece : 3 * piece, :]
    w_dt[...] = late[3 * piece : 3 * piece + w_dt.shape[0], 0:piece]


VMEM = pl.BlockSpec(memory_space=pltpu.VMEM)
SMEM = pl.BlockSpec(memory_space=pltpu.SMEM)
HBM = pl.BlockSpec(memory_space=pltpu.HBM)


def run(kernel, name, outs, args, scalars=(), fetched=(), scratch=()):
    args = [
        pltpu.with_memory_space_constraint(a, pltpu.HBM) if i in fetched else a
        for i, a in enumerate(args)
    ]

    def place(i):
        if i in fetched:
            return HBM
        return SMEM if i in scalars else VMEM

    def whole(*refs):
        held, sems = refs[len(refs) - len(fetched) - 1 : -1], refs[-1]
        refs = list(refs[: len(refs) - len(fetched) - 1])
        copies = []
        for k, i in enumerate(fetched):
            copies.append(pltpu.make_async_copy(refs[i], held[k], sems.at[k]))
            refs[i] = held[k]
        for copy in copies:
            copy.start()
        for copy in copies:
            copy.wait()
        kernel(*refs)

    holders = []
    if fetched:
        for i in fetched:
            kind = pltpu.SMEM if i in scalars else pltpu.VMEM
            holders.append(kind(args[i].shape, args[i].dtype))
        holders.append(pltpu.SemaphoreType.DMA((len(fetched),)))
    return pl.pallas_call(
        whole if fetched else kernel,
        name=name,
        out_shape=[jax.ShapeDtypeStruct(shape, kind) for shape, kind in outs],
        in_specs=[place(i) for i in range(len(args))],
        out_specs=[VMEM] * len(outs),
        scratch_shapes=list(scratch) + holders,
        compiler_params=pltpu.CompilerParams(vmem_limit_bytes=LIMIT),
        cost_estimate=pl.CostEstimate(flops=10**6, bytes_accessed=2**14, transcendentals=0),
    )(*args)


def shifted(block, axis, distance):
    devices = range(lax.axis_size(axis))
    route = [(i - distance, i) for i in devices if i - distance in devices]
    return lax.ppermute(block, axis, route)


def swapped(block, axis, flip):
    return lax.ppermute(block, axis, [(i, i ^ flip) for i in range(lax.axis_size(axis))])


def body(
    series,
    in_weight,
    step_weight,
    step_bias,
    log_rate,
    conv_weight,
    conv_bias,
    skip_gain,
    norm_gain,
    out_weight,
    cotangent,
):
    length, depth = series.shape
    width = in_weight.shape[2]
    heads = step_weight.shape[1]
    count = lax.axis_size("tm")
    parts = lax.axis_size("head")
    every = width * parts
    assert width == 2 * N and heads == 4
    part = functools.partial
    w = in_weight.transpose(1, 0, 2)
    dtw = step_weight.T
    gain = norm_gain.reshape(1, width)
    hops = count // 2
    piece = depth // count
    position = lax.axis_index("tm").astype(jnp.int32)
    spot = lax.axis_index("head").astype(jnp.int32)
    low, high = (position % 2).reshape(1), (position // 2).reshape(1)
    low_spot, high_spot = (spot % 2).reshape(1), (spot // 2).reshape(1)
    rim = shifted(series[length - RIM :], "tm", 1)
    state_msg = ((width + LOGS, N), BF16)

    def passed(msg, back, during):
        made = []

        def meanwhile(k, block):
            if k < len(during):
                block, extra = lax.optimization_barrier((block, during[k](made)))
                made.append(extra)
            return block

        partner = meanwhile(0, swapped(msg, "tm", 1))
        (msg,) = run(part(pair_kernel, heads, back), "pair", [state_msg], [low, msg, partner], (0,))
        near = []
        hop = 1
        while hop < hops:
            far = meanwhile(len(made), shifted(msg, "tm", (-2 if back else 2) * hop))
            hop *= 2
            if hop < hops:
                msg, *near = run(
                    part(link_kernel, heads), "link",
                    [state_msg, ((SPARE * width, 2 * N), F32)], [far, msg] + near,
                )
        return [partner, far] + near, made

    def halved(keep, send, axis, where, name):
        most, rows, cols = send.shape
        return run(
            halve_kernel, name, [((SPARE * rows, cols), F32)] + [((rows, cols), BF16)] * (most - 1),
            [where, keep, swapped(send, axis, 1)], (0,),
        )

    def gathered(blocks, axis):
        return [blocks[0]] + [swapped(block, axis, 2 * k) for k, block in enumerate(blocks) if k]

    gate, pre, scal, w_xbc = run(
        part(project_kernel, heads), "project",
        [
            ((length, width), BF16),
            ((length, 2 * width), BF16),
            ((SCALARS, length), F32),
            ((2, depth, width), BF16),
        ],
        [series, w, dtw, step_bias, log_rate, skip_gain, gain, conv_weight, conv_bias],
        (3, 4, 5), tuple(range(9)),
    )
    x, bc, conv, msg = run(
        part(conv_kernel, heads), "conv",
        [((length, width), BF16), ((length, width), BF16), ((length, 2 * width), F32), state_msg],
        [pre, rim, w_xbc, scal],
        scratch=[pltpu.VMEM((length + 8, 2 * width), F32)],
    )

    def inner(made):
        return run(
            part(inside_kernel, heads), "inside",
            [((length, width), F32), ((length, width), F32), ((length, 2 * width), F32)],
            [x, bc, scal, cotangent, out_weight, conv],
        )

    ahead, ((inside, gg, slope),) = passed(msg, False, [inner])
    y, sin, sums = run(
        part(join_kernel, heads), "join",
        [((length, width), F32), ((width, N), F32), ((8, length), F32)],
        [low, inside, gg, gate, bc, scal] + ahead, (0,),
    )
    flip = 1
    while 2 * flip < parts:
        sums = sums + swapped(sums, "head", flip)
        flip *= 2
    gy, msg, total = run(
        part(grad_y_kernel, heads, every), "grad_y",
        [((length, width), F32), state_msg, ((8, length), F32)],
        [sums, swapped(sums, "head", flip), y, gate, gg, bc, scal],
    )
    early, late = 5 * piece, 3 * piece + LOGS

    def early_part(made):
        return run(
            part(early_kernel, heads, count, every), "early",
            [
                ((length, width), BF16),
                ((length, width), BF16),
                ((length, N), BF16),
                ((length, N), F32),
                ((RIM, N), BF16),
                ((SPARE * hops, early, N), BF16),
                ((hops, early, N), BF16),
            ],
            [
                low, total, y, gate, gg, gy, x, bc, scal, sin, cotangent, series, rim, slope,
            ],
            (0,),
            scratch=[
                pltpu.VMEM((length + RIM + 8, N), F32),
                pltpu.VMEM((count, early, N), BF16),
            ],
        )

    def beside_part(made):
        normed, grad_gate, gp_c, gb = made[0][0:4]
        return run(
            part(beside_kernel, heads), "beside",
            [
                ((length, 2 * depth), F32),
                ((length, 2 * width), F32),
                ((8, length), F32),
                ((SPARE * depth, length), BF16),
            ],
            [normed, grad_gate, gp_c, gb, y, gy, x, bc, scal, sin, out_weight, w, series],
        )

    behind, (firsts, (sg, held, yb, turned)) = passed(msg, True, [early_part, beside_part])
    edge_c, keep, send = firsts[4:]
    early_parts = halved(keep, send, "tm", high, "halve_early")
    early_parts = gathered(early_parts, "tm")
    back, gp, lead, edge = run(
        part(close_kernel, heads), "close",
        [
            ((SPARE * length, width + N), F32),
            ((length, width + N), BF16),
            ((RIM, width + N), BF16),
            ((RIM, 2 * width), BF16),
        ],
        [low, x, bc, scal, gy, held, slope, edge_c] + behind, (0,),
        scratch=[pltpu.VMEM((length + RIM + 8, width + N), F32)],
    )
    edge = shifted(edge, "tm", -1)
    keep, send, graw = run(
        part(late_kernel, heads, count), "late",
        [((SPARE * hops, late, N), BF16), ((hops, late, N), BF16), ((2 * heads, length), F32)],
        [low, x, scal, back, gp, lead, yb, held, turned, series, rim], (0,),
        scratch=[pltpu.VMEM((count, late, N), BF16)],
    )
    late_parts = halved(keep, send, "tm", high, "halve_late")
    late_parts = gathered(late_parts, "tm")
    rows = length // parts
    edge, early_parts = lax.optimization_barrier((edge, early_parts))
    w_out_grad, early_total = run(
        early_sum_kernel, "early_sum",
        [((piece, width), F32), ((SPARE * 3 * piece, N), F32)], early_parts,
    )
    keep, send = run(
        rows_kernel, "rows",
        [((SPARE * parts // 2, rows, 2 * depth), BF16), ((parts // 2, rows, 2 * depth), BF16)],
        [low_spot, sg, gp, graw, edge, w, dtw], (0,),
        scratch=[pltpu.VMEM((length, 2 * depth), BF16)],
    )
    both = gathered(halved(keep, send, "head", high_spot, "halve_rows"), "head")
    layer_out, series_grad = run(
        outputs_kernel, "outputs", [((rows, depth), BF16), ((rows, depth), F32)], both,
    )
    late_parts, layer_out = lax.optimization_barrier((late_parts, layer_out))
    w_in_grad, w_dt_grad = run(
        total_kernel, "total",
        [((3, piece, width), F32), ((heads, piece), F32)], [early_total] + late_parts,
    )
    return (layer_out, series_grad, w_in_grad.transpose(1, 0, 2), w_dt_grad.T, w_out_grad)


def solution(mesh):
    in_specs = (
        P("tm", None),
        P(None, None, "head"),
        P(None, "head"),
        P("head"),
        P("head"),
        P(None, None, "head"),
        P(None, "head"),
        P("head"),
        P("head"),
        P(None, "head"),
        P("tm", None),
    )
    out_specs = (
        P(("tm", "head"), None),
        P(("tm", "head"), None),
        P("tm", None, "head"),
        P("tm", "head"),
        P("tm", "head"),
    )
    return jax.shard_map(body, mesh=mesh, in_specs=in_specs, out_specs=out_specs, check_vma=False)
```

profile of v0, /device:TPU:0, one launch (start us, length us, event | category | flops | bytes accessed | tf_op | source)
XLA Modules:
  0.0 85.8 jit_solution(13716107758553849823)
XLA Ops:
  1.4 4.9 %collective-permute-start = (bf16[16,512]{1,0:T(8,128)(2,1)S(1)}, bf16[16,512]{1,0:T(8,128)(2,1)S(1)}, u32[]{:S(2)}, u32[]{:S(2)}) collective-permute-start(bf16[16,512]{1,0:T(8,128)(2,1)S(1)} %slice.3), channel_id=1, source_target_pairs={{0,4},{4,8},{8,12},{12,16},{16,20},{20,24},{24,28},{1,5},{5,9},{9,... | collective-permute-start | bytes 49160 | tf_op jit(solution)/shard_map/ppermute | solution.py:556
  6.3 2.3 %project.1 = (bf16[256,256]{1,0:T(8,128)(2,1)S(1)}, bf16[256,512]{1,0:T(8,128)(2,1)S(1)}, f32[32,256]{1,0:T(8,128)S(1)}, bf16[2,512,256]{2,1,0:T(8,128)(2,1)S(1)}) custom-call(bf16[256,512]{1,0:T(8,128)(2,1)} %series.5, bf16[3,512,256]{2,1,0:T(8,128)(2,1)} %bitcast.9, bf16[4,512]{1,0:T(4,128)(2,1)} %bitcast.12, f32[4]{0:T(128)} %refs_3_.1, f32[4]{0:T(128)} %refs_4_.1, ...), custom_call_target="tpu_custom_call" | custom-call | flops 1000000 | bytes 16384 | tf_op jit(solution)/shard_map/project/pallas_call | solution.py:541
  9.6 1.6 %collective-permute-start.1 = (bf16[272,128]{1,0:T(8,128)(2,1)S(1)}, bf16[272,128]{1,0:T(8,128)(2,1)S(1)}, u32[]{:S(2)}, u32[]{:S(2)}) collective-permute-start(bf16[272,128]{1,0:T(8,128)(2,1)S(1)} %get-tuple-element.94.mine), channel_id=1, source_target_pairs={{0,4},{4,0},{8,12},{12,8},{16,20},{20,16},{24,28},{28,24},{1,5},{5... | collective-permute-start | bytes 208904 | tf_op jit(solution)/shard_map/ppermute | solution.py:560
  12.0 2.0 %collective-permute-done.1.other.partner = bf16[272,128]{1,0:T(8,128)(2,1)S(1)} collective-permute-done((bf16[272,128]{1,0:T(8,128)(2,1)S(1)}, bf16[272,128]{1,0:T(8,128)(2,1)S(1)}, u32[]{:S(2)}, u32[]{:S(2)}) %collective-permute-start.1) | collective-permute-done | bytes 69664 | tf_op jit(solution)/shard_map/ppermute | solution.py:560
  14.0 4.4 %collective-permute-start.2 = (bf16[272,128]{1,0:T(8,128)(2,1)S(1)}, bf16[272,128]{1,0:T(8,128)(2,1)S(1)}, u32[]{:S(2)}, u32[]{:S(2)}) collective-permute-start(bf16[272,128]{1,0:T(8,128)(2,1)S(1)} %pair.2.nearer), channel_id=1, source_target_pairs={{0,8},{4,12},{8,16},{12,20},{16,24},{20,28},{1,9},{5,13},{9,17},{1... | collective-permute-start | bytes 208904 | tf_op jit(solution)/shard_map/ppermute | solution.py:556
  18.4 1.9 %collective-permute-done.2.farther = bf16[272,128]{1,0:T(8,128)(2,1)S(1)} collective-permute-done((bf16[272,128]{1,0:T(8,128)(2,1)S(1)}, bf16[272,128]{1,0:T(8,128)(2,1)S(1)}, u32[]{:S(2)}, u32[]{:S(2)}) %collective-permute-start.2) | collective-permute-done | bytes 69664 | tf_op jit(solution)/shard_map/ppermute | solution.py:556
  20.4 5.3 %collective-permute-start.3 = (bf16[272,128]{1,0:T(8,128)(2,1)S(1)}, bf16[272,128]{1,0:T(8,128)(2,1)S(1)}, u32[]{:S(2)}, u32[]{:S(2)}) collective-permute-start(bf16[272,128]{1,0:T(8,128)(2,1)S(1)} %get-tuple-element.103), channel_id=1, source_target_pairs={{0,16},{4,20},{8,24},{12,28},{1,17},{5,21},{9,25},{13,29},{2,18},{... | collective-permute-start | bytes 208904 | tf_op jit(solution)/shard_map/ppermute | solution.py:556
  25.7 1.9 %collective-permute-done.3.rest_0_ = bf16[272,128]{1,0:T(8,128)(2,1)S(1)} collective-permute-done((bf16[272,128]{1,0:T(8,128)(2,1)S(1)}, bf16[272,128]{1,0:T(8,128)(2,1)S(1)}, u32[]{:S(2)}, u32[]{:S(2)}) %collective-permute-start.3) | collective-permute-done | bytes 69664 | tf_op jit(solution)/shard_map/ppermute | solution.py:556
  29.6 1.5 %collective-permute-start.5 = (f32[8,256]{1,0:T(8,128)S(1)}, f32[8,256]{1,0:T(8,128)S(1)}, u32[]{:S(2)}, u32[]{:S(2)}) collective-permute-start(f32[8,256]{1,0:T(8,128)S(1)} %add.13.sums), channel_id=1, source_target_pairs={{0,2},{1,3},{2,0},{3,1},{4,6},{5,7},{6,4},{7,5},{8,10},{9,11},{10,... | collective-permute-start | bytes 24584 | tf_op jit(solution)/shard_map/ppermute | solution.py:560
  31.1 2.2 %collective-permute-done.5.other = f32[8,256]{1,0:T(8,128)S(1)} collective-permute-done((f32[8,256]{1,0:T(8,128)S(1)}, f32[8,256]{1,0:T(8,128)S(1)}, u32[]{:S(2)}, u32[]{:S(2)}) %collective-permute-start.5) | collective-permute-done | bytes 8224 | tf_op jit(solution)/shard_map/ppermute | solution.py:560
  34.8 2.1 %early.1 = (bf16[256,256]{1,0:T(8,128)(2,1)S(1)}, bf16[256,256]{1,0:T(8,128)(2,1)S(1)}, bf16[256,128]{1,0:T(8,128)(2,1)S(1)}, f32[256,128]{1,0:T(8,128)S(1)}, bf...) custom-call(s32[1]{0:T(128)} %bitcast.1.low, ...), custom_call_target="tpu_custom_call" | custom-call | flops 1000000 | bytes 16384 | tf_op jit(solution)/shard_map/early/pallas_call | solution.py:541
  40.7 1.5 %beside.1 = (f32[256,1024]{1,0:T(8,128)S(1)}, f32[256,512]{1,0:T(8,128)S(1)}, f32[8,256]{1,0:T(8,128)S(1)}, bf16[2048,256]{1,0:T(8,128)(2,1)S(1)}) custom-call(bf16[256,256]{1,0:T(8,128)(2,1)S(1)} %get-tuple-element.120.normed, bf16[256,256]{1,0:T(8,128)(2,1)S(1)} %get-tuple-element.121.grad_gate, bf16[256,128]{1,0:T(8,128)(2,1)S(1)} %get-tuple-element.122.gp, ...), custom_call_target="tpu_custom_call" | custom-call | flops 1000000 | bytes 16384 | tf_op jit(solution)/shard_map/beside/pallas_call | solution.py:541
  44.1 1.5 %collective-permute-done.7.farther = bf16[272,128]{1,0:T(8,128)(2,1)S(1)} collective-permute-done((bf16[272,128]{1,0:T(8,128)(2,1)S(1)}, bf16[272,128]{1,0:T(8,128)(2,1)S(1)}, u32[]{:S(2)}, u32[]{:S(2)}) %collective-permute-start.7) | collective-permute-done | bytes 69664 | tf_op jit(solution)/shard_map/ppermute | solution.py:556
  50.9 2.0 %collective-permute-start.15 = (bf16[320,128]{1,0:T(8,128)(2,1)}, bf16[320,128]{1,0:T(8,128)(2,1)S(1)}, u32[]{:S(2)}, u32[]{:S(2)}) collective-permute-start(bf16[320,128]{1,0:T(8,128)(2,1)} %get-tuple-element.150), channel_id=1, source_target_pairs={{0,8},{4,12},{8,0},{12,4},{16,24},{20,28},{24,16},{28,20},{1,9},{5... | collective-permute-start | bytes 245768 | tf_op jit(solution)/shard_map/ppermute | solution.py:560
  52.9 3.5 %collective-permute-start.16 = (bf16[320,128]{1,0:T(8,128)(2,1)}, bf16[320,128]{1,0:T(8,128)(2,1)S(1)}, u32[]{:S(2)}, u32[]{:S(2)}) collective-permute-start(bf16[320,128]{1,0:T(8,128)(2,1)} %get-tuple-element.151), channel_id=1, source_target_pairs={{0,16},{4,20},{8,24},{12,28},{16,0},{20,4},{24,8},{28,12},{1,17},{... | collective-permute-start | bytes 245768 | tf_op jit(solution)/shard_map/ppermute | solution.py:560
  59.9 1.4 %copy-done.3 = f32[1024,384]{1,0:T(8,128)S(1)} copy-done((f32[1024,384]{1,0:T(8,128)S(1)}, f32[1024,384]{1,0:T(8,128)}, u32[]{:S(2)}) %copy-start.3) | copy-done | bytes 1572888
  62.5 2.1 %late.1 = (bf16[16,208,128]{2,1,0:T(8,128)(2,1)S(1)}, bf16[4,208,128]{2,1,0:T(8,128)(2,1)}, f32[8,256]{1,0:T(8,128)S(1)}) custom-call(s32[1]{0:T(128)} %bitcast.1.low, bf16[256,256]{1,0:T(8,128)(2,1)S(1)} %get-tuple-element.92.x, f32[32,256]{1,0:T(8,128)S(1)} %get-tuple-element.91.scal, f32[1024,384]{1,0:T(8,128)S(1)} %copy-done.3, ...), custom_call_target="tpu_custom_call" | custom-call | flops 1000000 | bytes 16384 | tf_op jit(solution)/shard_map/late/pallas_call | solution.py:541
  65.9 2.6 %collective-permute-start.9 = (bf16[4,208,128]{2,1,0:T(8,128)(2,1)}, bf16[4,208,128]{2,1,0:T(8,128)(2,1)S(1)}, u32[]{:S(2)}, u32[]{:S(2)}) collective-permute-start(bf16[4,208,128]{2,1,0:T(8,128)(2,1)} %get-tuple-element.139), channel_id=1, source_target_pairs={{0,4},{4,0},{8,12},{12,8},{16,20},{20,16},{24,28},{28,24},{1,5},{5... | collective-permute-start | bytes 638984 | tf_op jit(solution)/shard_map/ppermute | solution.py:560
  68.6 1.6 %collective-permute-start.19 = (bf16[64,1024]{1,0:T(8,128)(2,1)S(1)}, bf16[64,1024]{1,0:T(8,128)(2,1)S(1)}, u32[]{:S(2)}, u32[]{:S(2)}) collective-permute-start(bf16[64,1024]{1,0:T(8,128)(2,1)S(1)} %get-tuple-element.157), channel_id=1, source_target_pairs={{0,2},{1,3},{2,0},{3,1},{4,6},{5,7},{6,4},{7,5},{8,10},{9,11},{10,... | collective-permute-start | bytes 393224 | tf_op jit(solution)/shard_map/ppermute | solution.py:560
  70.1 4.5 %collective-permute-done.9.other = bf16[4,208,128]{2,1,0:T(8,128)(2,1)S(1)} collective-permute-done((bf16[4,208,128]{2,1,0:T(8,128)(2,1)}, bf16[4,208,128]{2,1,0:T(8,128)(2,1)S(1)}, u32[]{:S(2)}, u32[]{:S(2)}) %collective-permute-start.9) | collective-permute-done | bytes 213024 | tf_op jit(solution)/shard_map/ppermute | solution.py:560
  74.7 2.3 %collective-permute-start.10 = (bf16[208,128]{1,0:T(8,128)(2,1)S(1)}, bf16[208,128]{1,0:T(8,128)(2,1)S(1)}, u32[]{:S(2)}, u32[]{:S(2)}) collective-permute-start(bf16[208,128]{1,0:T(8,128)(2,1)S(1)} %get-tuple-element.141), channel_id=1, source_target_pairs={{0,8},{4,12},{8,0},{12,4},{16,24},{20,28},{24,16},{28,20},{1,9},{5... | collective-permute-start | bytes 159752 | tf_op jit(solution)/shard_map/ppermute | solution.py:560
  77.0 2.1 %collective-permute-start.11 = (bf16[208,128]{1,0:T(8,128)(2,1)S(1)}, bf16[208,128]{1,0:T(8,128)(2,1)S(1)}, u32[]{:S(2)}, u32[]{:S(2)}) collective-permute-start(bf16[208,128]{1,0:T(8,128)(2,1)S(1)} %get-tuple-element.142), channel_id=1, source_target_pairs={{0,16},{4,20},{8,24},{12,28},{16,0},{20,4},{24,8},{28,12},{1,17},{... | collective-permute-start | bytes 159752 | tf_op jit(solution)/shard_map/ppermute | solution.py:560
  79.5 1.5 %early_sum.1 = (f32[64,256]{1,0:T(8,128)}, f32[768,128]{1,0:T(8,128)S(1)}) custom-call(f32[1280,128]{1,0:T(8,128)S(1)} %copy-done.15, bf16[320,128]{1,0:T(8,128)(2,1)S(1)} %collective-permute-done.15.refs_1_, bf16[320,128]{1,0:T(8,128)(2,1)S(1)} %collective-permute-done.16.refs_2_, bf16[320,128]{1,0:T(8,128)(2,1)} %collective-permute-done.17.refs_3_), custom_call_target="tpu_custom_call" | custom-call | flops 1000000 | bytes 16384 | tf_op jit(solution)/shard_map/early_sum/pallas_call | solution.py:541
  82.8 2.3 %collective-permute-done.12.refs_3_ = bf16[208,128]{1,0:T(8,128)(2,1)S(1)} collective-permute-done((bf16[208,128]{1,0:T(8,128)(2,1)S(1)}, bf16[208,128]{1,0:T(8,128)(2,1)S(1)}, u32[]{:S(2)}, u32[]{:S(2)}) %collective-permute-start.12) | collective-permute-done | bytes 53280 | tf_op jit(solution)/shard_map/ppermute | solution.py:560
  (72 shorter events, 25.8 us)
Async XLA Ops:
  0.6 10.5 %copy-start.13 = (bf16[512,256]{1,0:T(8,128)(2,1)S(1)}, bf16[512,256]{1,0:T(8,128)(2,1)}, u32[]{:S(2)}) copy-start(bf16[512,256]{1,0:T(8,128)(2,1)} %ow.3) | copy-start | bytes 786436
  0.6 10.5 %copy-start.12 = (bf16[256,512]{1,0:T(8,128)(2,1)S(1)}, bf16[256,512]{1,0:T(8,128)(2,1)}, u32[]{:S(2)}) copy-start(bf16[256,512]{1,0:T(8,128)(2,1)} %cot.3) | copy-start | bytes 786436
  1.4 7.2 %collective-permute-start = (bf16[16,512]{1,0:T(8,128)(2,1)S(1)}, bf16[16,512]{1,0:T(8,128)(2,1)S(1)}, u32[]{:S(2)}, u32[]{:S(2)}) collective-permute-start(bf16[16,512]{1,0:T(8,128)(2,1)S(1)} %slice.3), channel_id=1, source_target_pairs={{0,4},{4,8},{8,12},{12,16},{16,20},{20,24},{24,28},{1,5},{5,9},{9,... | collective-permute-start | bytes 49160 | tf_op jit(solution)/shard_map/ppermute | solution.py:556
  9.6 4.4 %collective-permute-start.1 = (bf16[272,128]{1,0:T(8,128)(2,1)S(1)}, bf16[272,128]{1,0:T(8,128)(2,1)S(1)}, u32[]{:S(2)}, u32[]{:S(2)}) collective-permute-start(bf16[272,128]{1,0:T(8,128)(2,1)S(1)} %get-tuple-element.94.mine), channel_id=1, source_target_pairs={{0,4},{4,0},{8,12},{12,8},{16,20},{20,16},{24,28},{28,24},{1,5},{5... | collective-permute-start | bytes 208904 | tf_op jit(solution)/shard_map/ppermute | solution.py:560
  14.0 20.9 %copy-start.1 = (bf16[256,512]{1,0:T(8,128)(2,1)S(1)}, bf16[256,512]{1,0:T(8,128)(2,1)}, u32[]{:S(2)}) copy-start(bf16[256,512]{1,0:T(8,128)(2,1)} %series.5) | copy-start | bytes 786436
  14.0 6.3 %collective-permute-start.2 = (bf16[272,128]{1,0:T(8,128)(2,1)S(1)}, bf16[272,128]{1,0:T(8,128)(2,1)S(1)}, u32[]{:S(2)}, u32[]{:S(2)}) collective-permute-start(bf16[272,128]{1,0:T(8,128)(2,1)S(1)} %pair.2.nearer), channel_id=1, source_target_pairs={{0,8},{4,12},{8,16},{12,20},{16,24},{20,28},{1,9},{5,13},{9,17},{1... | collective-permute-start | bytes 208904 | tf_op jit(solution)/shard_map/ppermute | solution.py:556
  20.4 7.2 %collective-permute-start.3 = (bf16[272,128]{1,0:T(8,128)(2,1)S(1)}, bf16[272,128]{1,0:T(8,128)(2,1)S(1)}, u32[]{:S(2)}, u32[]{:S(2)}) collective-permute-start(bf16[272,128]{1,0:T(8,128)(2,1)S(1)} %get-tuple-element.103), channel_id=1, source_target_pairs={{0,16},{4,20},{8,24},{12,28},{1,17},{5,21},{9,25},{13,29},{2,18},{... | collective-permute-start | bytes 208904 | tf_op jit(solution)/shard_map/ppermute | solution.py:556
  28.4 1.2 %collective-permute-start.4 = (f32[8,256]{1,0:T(8,128)S(1)}, f32[8,256]{1,0:T(8,128)S(1)}, u32[]{:S(2)}, u32[]{:S(2)}) collective-permute-start(f32[8,256]{1,0:T(8,128)S(1)} %get-tuple-element.105), channel_id=1, source_target_pairs={{0,1},{1,0},{2,3},{3,2},{4,5},{5,4},{6,7},{7,6},{8,9},{9,8},{10,11... | collective-permute-start | bytes 24584 | tf_op jit(solution)/shard_map/ppermute | solution.py:560
  29.6 3.7 %collective-permute-start.5 = (f32[8,256]{1,0:T(8,128)S(1)}, f32[8,256]{1,0:T(8,128)S(1)}, u32[]{:S(2)}, u32[]{:S(2)}) collective-permute-start(f32[8,256]{1,0:T(8,128)S(1)} %add.13.sums), channel_id=1, source_target_pairs={{0,2},{1,3},{2,0},{3,1},{4,6},{5,7},{6,4},{7,5},{8,10},{9,11},{10,... | collective-permute-start | bytes 24584 | tf_op jit(solution)/shard_map/ppermute | solution.py:560
  34.0 4.4 %collective-permute-start.6 = (bf16[272,128]{1,0:T(8,128)(2,1)S(1)}, bf16[272,128]{1,0:T(8,128)(2,1)S(1)}, u32[]{:S(2)}, u32[]{:S(2)}) collective-permute-start(bf16[272,128]{1,0:T(8,128)(2,1)S(1)} %get-tuple-element.108.mine), channel_id=1, source_target_pairs={{0,4},{4,0},{8,12},{12,8},{16,20},{20,16},{24,28},{28,24},{1,5},{5... | collective-permute-start | bytes 208904 | tf_op jit(solution)/shard_map/ppermute | solution.py:560
  38.4 9.6 %collective-permute-start.14 = (bf16[4,320,128]{2,1,0:T(8,128)(2,1)}, bf16[4,320,128]{2,1,0:T(8,128)(2,1)S(1)}, u32[]{:S(2)}, u32[]{:S(2)}) collective-permute-start(bf16[4,320,128]{2,1,0:T(8,128)(2,1)} %get-tuple-element.148), channel_id=1, source_target_pairs={{0,4},{4,0},{8,12},{12,8},{16,20},{20,16},{24,28},{28,24},{1,5},{5... | collective-permute-start | bytes 983048 | tf_op jit(solution)/shard_map/ppermute | solution.py:560
  39.4 6.3 %collective-permute-start.7 = (bf16[272,128]{1,0:T(8,128)(2,1)S(1)}, bf16[272,128]{1,0:T(8,128)(2,1)S(1)}, u32[]{:S(2)}, u32[]{:S(2)}) collective-permute-start(bf16[272,128]{1,0:T(8,128)(2,1)S(1)} %pair.3.nearer), channel_id=1, source_target_pairs={{8,0},{12,4},{16,8},{20,12},{24,16},{28,20},{9,1},{13,5},{17,9},{2... | collective-permute-start | bytes 208904 | tf_op jit(solution)/shard_map/ppermute | solution.py:556
  46.7 9.7 %collective-permute-start.8 = (bf16[272,128]{1,0:T(8,128)(2,1)S(1)}, bf16[272,128]{1,0:T(8,128)(2,1)S(1)}, u32[]{:S(2)}, u32[]{:S(2)}) collective-permute-start(bf16[272,128]{1,0:T(8,128)(2,1)S(1)} %get-tuple-element.131), channel_id=1, source_target_pairs={{16,0},{20,4},{24,8},{28,12},{17,1},{21,5},{25,9},{29,13},{18,2},{... | collective-permute-start | bytes 208904 | tf_op jit(solution)/shard_map/ppermute | solution.py:556
  50.9 13.7 %collective-permute-start.15 = (bf16[320,128]{1,0:T(8,128)(2,1)}, bf16[320,128]{1,0:T(8,128)(2,1)S(1)}, u32[]{:S(2)}, u32[]{:S(2)}) collective-permute-start(bf16[320,128]{1,0:T(8,128)(2,1)} %get-tuple-element.150), channel_id=1, source_target_pairs={{0,8},{4,12},{8,0},{12,4},{16,24},{20,28},{24,16},{28,20},{1,9},{5... | collective-permute-start | bytes 245768 | tf_op jit(solution)/shard_map/ppermute | solution.py:560
  52.9 11.7 %collective-permute-start.16 = (bf16[320,128]{1,0:T(8,128)(2,1)}, bf16[320,128]{1,0:T(8,128)(2,1)S(1)}, u32[]{:S(2)}, u32[]{:S(2)}) collective-permute-start(bf16[320,128]{1,0:T(8,128)(2,1)} %get-tuple-element.151), channel_id=1, source_target_pairs={{0,16},{4,20},{8,24},{12,28},{16,0},{20,4},{24,8},{28,12},{1,17},{... | collective-permute-start | bytes 245768 | tf_op jit(solution)/shard_map/ppermute | solution.py:560
  56.4 8.2 %collective-permute-start.17 = (bf16[320,128]{1,0:T(8,128)(2,1)}, bf16[320,128]{1,0:T(8,128)(2,1)}, u32[]{:S(2)}, u32[]{:S(2)}) collective-permute-start(bf16[320,128]{1,0:T(8,128)(2,1)} %get-tuple-element.152), channel_id=1, source_target_pairs={{0,24},{4,28},{8,16},{12,20},{16,8},{20,12},{24,0},{28,4},{1,25},{... | collective-permute-start | bytes 245768 | tf_op jit(solution)/shard_map/ppermute | solution.py:560
  58.6 6.1 %collective-permute-start.13 = (bf16[16,512]{1,0:T(8,128)(2,1)S(1)}, bf16[16,512]{1,0:T(8,128)(2,1)S(1)}, u32[]{:S(2)}, u32[]{:S(2)}) collective-permute-start(bf16[16,512]{1,0:T(8,128)(2,1)S(1)} %get-tuple-element.146), channel_id=1, source_target_pairs={{4,0},{8,4},{12,8},{16,12},{20,16},{24,20},{28,24},{5,1},{9,5},{13... | collective-permute-start | bytes 49160 | tf_op jit(solution)/shard_map/ppermute | solution.py:556
  65.9 13.6 %copy-start.15 = (f32[1280,128]{1,0:T(8,128)S(1)}, f32[1280,128]{1,0:T(8,128)}, u32[]{:S(2)}) copy-start(f32[1280,128]{1,0:T(8,128)} %copy-done.14) | copy-start | bytes 1966084
  65.9 2.6 %collective-permute-start.18 = (bf16[2,64,1024]{2,1,0:T(8,128)(2,1)}, bf16[2,64,1024]{2,1,0:T(8,128)(2,1)S(1)}, u32[]{:S(2)}, u32[]{:S(2)}) collective-permute-start(bf16[2,64,1024]{2,1,0:T(8,128)(2,1)} %get-tuple-element.155), channel_id=1, source_target_pairs={{0,1},{1,0},{2,3},{3,2},{4,5},{5,4},{6,7},{7,6},{8,9},{9,8},{10,11... | collective-permute-start | bytes 786440 | tf_op jit(solution)/shard_map/ppermute | solution.py:560
  65.9 8.8 %collective-permute-start.9 = (bf16[4,208,128]{2,1,0:T(8,128)(2,1)}, bf16[4,208,128]{2,1,0:T(8,128)(2,1)S(1)}, u32[]{:S(2)}, u32[]{:S(2)}) collective-permute-start(bf16[4,208,128]{2,1,0:T(8,128)(2,1)} %get-tuple-element.139), channel_id=1, source_target_pairs={{0,4},{4,0},{8,12},{12,8},{16,20},{20,16},{24,28},{28,24},{1,5},{5... | collective-permute-start | bytes 638984 | tf_op jit(solution)/shard_map/ppermute | solution.py:560
  68.6 12.4 %collective-permute-start.19 = (bf16[64,1024]{1,0:T(8,128)(2,1)S(1)}, bf16[64,1024]{1,0:T(8,128)(2,1)S(1)}, u32[]{:S(2)}, u32[]{:S(2)}) collective-permute-start(bf16[64,1024]{1,0:T(8,128)(2,1)S(1)} %get-tuple-element.157), channel_id=1, source_target_pairs={{0,2},{1,3},{2,0},{3,1},{4,6},{5,7},{6,4},{7,5},{8,10},{9,11},{10,... | collective-permute-start | bytes 393224 | tf_op jit(solution)/shard_map/ppermute | solution.py:560
  74.7 7.0 %collective-permute-start.10 = (bf16[208,128]{1,0:T(8,128)(2,1)S(1)}, bf16[208,128]{1,0:T(8,128)(2,1)S(1)}, u32[]{:S(2)}, u32[]{:S(2)}) collective-permute-start(bf16[208,128]{1,0:T(8,128)(2,1)S(1)} %get-tuple-element.141), channel_id=1, source_target_pairs={{0,8},{4,12},{8,0},{12,4},{16,24},{20,28},{24,16},{28,20},{1,9},{5... | collective-permute-start | bytes 159752 | tf_op jit(solution)/shard_map/ppermute | solution.py:560
  77.0 5.7 %collective-permute-start.11 = (bf16[208,128]{1,0:T(8,128)(2,1)S(1)}, bf16[208,128]{1,0:T(8,128)(2,1)S(1)}, u32[]{:S(2)}, u32[]{:S(2)}) collective-permute-start(bf16[208,128]{1,0:T(8,128)(2,1)S(1)} %get-tuple-element.142), channel_id=1, source_target_pairs={{0,16},{4,20},{8,24},{12,28},{16,0},{20,4},{24,8},{28,12},{1,17},{... | collective-permute-start | bytes 159752 | tf_op jit(solution)/shard_map/ppermute | solution.py:560
  79.1 5.9 %collective-permute-start.12 = (bf16[208,128]{1,0:T(8,128)(2,1)S(1)}, bf16[208,128]{1,0:T(8,128)(2,1)S(1)}, u32[]{:S(2)}, u32[]{:S(2)}) collective-permute-start(bf16[208,128]{1,0:T(8,128)(2,1)S(1)} %get-tuple-element.143), channel_id=1, source_target_pairs={{0,24},{4,28},{8,16},{12,20},{16,8},{20,12},{24,0},{28,4},{1,25},{... | collective-permute-start | bytes 159752 | tf_op jit(solution)/shard_map/ppermute | solution.py:560
  (13 other events, 28.8 us)
where the time goes:
time: 86.2 us; the launch traced here: 85.8 us
  starting transfers between devices  37.8 us (44%)
  waiting for transfers between devices  18.9 us (22%)
  Pallas kernels  17.4 us (20%)
  local copies, waits for them, and re-layouts  10.8 us (13%)
  between operations  0.92 us (1%)
    ppermute x14, starting transfers between devices, swapped(): lax.ppermute(block, axis, [(i, i ^ flip) for i in range(lax.axis_size(axi...  19.4 us
    ppermute x6, starting transfers between devices, shifted(): return lax.ppermute(block, axis, route)  18.4 us
    pallas_call x20, Pallas kernels, run(): pl.pallas_call(whole if fetched else kernel, name=name, out_shape=[jax.Sh...  17.4 us
    ppermute x14, waiting for transfers between devices, swapped(): lax.ppermute(block, axis, [(i, i ^ flip) for i in range(lax.axis_size(axi...  13.5 us
    unnamed x34, local copies, waits for them, and re-layouts  10 us
    ppermute x6, waiting for transfers between devices, shifted(): return lax.ppermute(block, axis, route)  5.38 us
  transfers between devices with their start and end apart: 20, of which 10 were waited for; matrix products, arithmetic and copies ran while one was open for 0% of the time, Pallas kernels for 15%

commit v1 on v0

--- a/solution.py
+++ b/solution.py
@@ -10,8 +10,7 @@
 N = 128
 KW = 4
 RIM = 16
-LIMIT = 12 * 2**20
-SPARE = 4
+LIMIT = 6 * 2**20
 SKIP, GAIN, BIAS, TAPS, SCALARS = 16, 17, 18, 20, 32
 LOGS = 16
 NORM_EPSILON = 1e-05
@@ -244,7 +243,7 @@
     gg[...] = scal[GAIN : GAIN + 1, :] * mm(cot[...], ow[...])
     v = conv[...]
     sig = sigmoid(v)
-    slope[...] = sig * (1.0 + v * (1.0 - sig))
+    slope[...] = (sig * (1.0 + v * (1.0 - sig))).astype(BF16)
 
 
 def join_kernel(heads, low, yi, gg, gate, bc, scal, partner, *rest):
@@ -330,7 +329,7 @@
     grow = widen(columns(jnp.exp(rows[0:heads])), heads, width)
     grad_c = mm(group, b) + mm(gy[...] * grow, sin[...])
     clear_ends(wide, length)
-    wide[RIM : RIM + length, :] = grad_c * slope[:, 2 * width - N :]
+    wide[RIM : RIM + length, :] = grad_c * slope[:, 2 * width - N :].astype(F32)
     grad_pre = conv_back(scal, wide, slice(0, N), length, 1, slice(width - N, width))
     edge[...] = grad_pre[0:RIM]
     gp[...] = grad_pre[RIM:]
@@ -354,8 +353,8 @@
 
 
 def beside_kernel(
-    heads, normed, grad_gate, gp, gb, y, gy, x, bc, scal, sin, ow, w, series,
-    sg, held, yb, turned,
+    heads, normed, grad_gate, gp, gb, y, gy, x, bc, scal, sin, ow, w,
+    sg, held, yb,
 ):
     length, width = y.shape
     rows = scal[0 : 2 * heads, :]
@@ -373,12 +372,12 @@
     own = mm(xv * widen(columns(remain), heads, width), bc[:, 0:N], TN)
     whole = jnp.exp(spread_rows(jnp.broadcast_to(last, (heads, N)), heads, width))
     held[:, width + N :] = whole * sin[...] + own
-    turned[0 : series.shape[1], :] = jnp.transpose(series[...])
     skips = scal[SKIP : SKIP + 1, :]
     yb[...] = mm_exact(head_mask(heads, width), gyv * (y[...] - skips * xv), NT)
-    depth = series.shape[1]
-    sg[:, 0:depth] = mm(normed[...], ow[...], NT)
-    sg[:, depth:] = mm(grad_gate[...], w[0], NT) + mm(gp[...], w[2, :, width - N :], NT)
+    depth = ow.shape[0]
+    sg[:, 0:depth] = mm(normed[...], ow[...], NT).astype(BF16)
+    late = mm(grad_gate[...], w[0], NT) + mm(gp[...], w[2, :, width - N :], NT)
+    sg[:, depth:] = late.astype(BF16)
 
 
 def close_kernel(
@@ -397,8 +396,8 @@
     grad_x = scal[SKIP : SKIP + 1, :] * gy[...] + widen(cols[:, heads:], heads, width) * grown
     grad_b = held[:, width : width + N] + mm(x[...].astype(F32) * widen(cols[:, 2 * heads :], heads, width), state)
     clear_ends(wide, length)
-    wide[RIM : RIM + length, 0:width] = grad_x * slope[:, 0:width]
-    wide[RIM : RIM + length, width:] = grad_b * slope[:, width : width + N]
+    wide[RIM : RIM + length, 0:width] = grad_x * slope[:, 0:width].astype(F32)
+    wide[RIM : RIM + length, width:] = grad_b * slope[:, width : width + N].astype(F32)
     grad_x = conv_back(scal, wide, slice(0, width), length, 0, slice(0, width))
     grad_b = conv_back(scal, wide, slice(width, width + N), length, 1, slice(0, N))
     for out, cut in ((lead, slice(0, RIM)), (gp, slice(RIM, RIM + length))):
@@ -410,12 +409,12 @@
 
 def late_kernel(
     heads, count,
-    low, x, scal, back, gp, lead, yb, held, turned, series, rim,
+    low, x, scal, back, gp, lead, yb, held, series, rim,
     keep, send, graw, stage,
 ):
     length, width = x.shape
     depth = series.shape[1]
-    w_xb = (mm(turned[0:depth, :], gp[...]) + mm(rim[...], lead[...], TN)).astype(BF16)
+    w_xb = (mm(series[...], gp[...], TN) + mm(rim[...], lead[...], TN)).astype(BF16)
     rows = scal[0 : 4 * heads, :]
     step = rows[heads : 2 * heads]
     mask = head_mask(heads, width)
@@ -451,10 +450,10 @@
     length, depth = sg.shape[0], sg.shape[1] // 2
     width = w.shape[2]
     heads = dtw.shape[0]
-    total = sg[:, depth:] + mm(graw[0:heads, :], dtw[...], TN)
+    total = sg[:, depth:].astype(F32) + mm(graw[0:heads, :], dtw[...], TN)
     total = total + mm(gp[:, 0:width], w[1], NT) + mm(gp[:, width:], w[2, :, 0:N], NT)
     late = mm(edge[:, 0:width], w[1], NT) + mm(edge[:, width:], w[2], NT)
-    stage[:, 0:depth] = sg[:, 0:depth].astype(BF16)
+    stage[:, 0:depth] = sg[:, 0:depth]
     stage[:, depth:] = total.astype(BF16)
     stage[length - RIM :, depth:] = (total[length - RIM :, :] + late).astype(BF16)
     piece = keep.shape[1]
@@ -612,14 +611,14 @@
             if hop < hops:
                 msg, *near = run(
                     part(link_kernel, heads), "link",
-                    [state_msg, ((SPARE * width, 2 * N), F32)], [far, msg] + near,
+                    [state_msg, ((width, 2 * N), F32)], [far, msg] + near,
                 )
         return [partner, far] + near, made
 
     def halved(keep, send, axis, where, name):
         most, rows, cols = send.shape
         return run(
-            halve_kernel, name, [((SPARE * rows, cols), F32)] + [((rows, cols), BF16)] * (most - 1),
+            halve_kernel, name, [((rows, cols), F32)] + [((rows, cols), BF16)] * (most - 1),
             [where, keep, swapped(send, axis, 1)], (0,),
         )
 
@@ -647,7 +646,7 @@
     def inner(made):
         return run(
             part(inside_kernel, heads), "inside",
-            [((length, width), F32), ((length, width), F32), ((length, 2 * width), F32)],
+            [((length, width), F32), ((length, width), F32), ((length, 2 * width), BF16)],
             [x, bc, scal, cotangent, out_weight, conv],
         )
 
@@ -677,7 +676,7 @@
                 ((length, N), BF16),
                 ((length, N), F32),
                 ((RIM, N), BF16),
-                ((SPARE * hops, early, N), BF16),
+                ((hops, early, N), BF16),
                 ((hops, early, N), BF16),
             ],
             [
@@ -695,22 +694,21 @@
         return run(
             part(beside_kernel, heads), "beside",
             [
-                ((length, 2 * depth), F32),
+                ((length, 2 * depth), BF16),
                 ((length, 2 * width), F32),
                 ((8, length), F32),
-                ((SPARE * depth, length), BF16),
             ],
-            [normed, grad_gate, gp_c, gb, y, gy, x, bc, scal, sin, out_weight, w, series],
+            [normed, grad_gate, gp_c, gb, y, gy, x, bc, scal, sin, out_weight, w],
         )
 
-    behind, (firsts, (sg, held, yb, turned)) = passed(msg, True, [early_part, beside_part])
+    behind, (firsts, (sg, held, yb)) = passed(msg, True, [early_part, beside_part])
     edge_c, keep, send = firsts[4:]
     early_parts = halved(keep, send, "tm", high, "halve_early")
     early_parts = gathered(early_parts, "tm")
     back, gp, lead, edge = run(
         part(close_kernel, heads), "close",
         [
-            ((SPARE * length, width + N), F32),
+            ((length, width + N), F32),
             ((length, width + N), BF16),
             ((RIM, width + N), BF16),
             ((RIM, 2 * width), BF16),
@@ -721,8 +719,8 @@
     edge = shifted(edge, "tm", -1)
     keep, send, graw = run(
         part(late_kernel, heads, count), "late",
-        [((SPARE * hops, late, N), BF16), ((hops, late, N), BF16), ((2 * heads, length), F32)],
-        [low, x, scal, back, gp, lead, yb, held, turned, series, rim], (0,),
+        [((hops, late, N), BF16), ((hops, late, N), BF16), ((2 * heads, length), F32)],
+        [low, x, scal, back, gp, lead, yb, held, series, rim], (0,),
         scratch=[pltpu.VMEM((count, late, N), BF16)],
     )
     late_parts = halved(keep, send, "tm", high, "halve_late")
@@ -731,11 +729,11 @@
     edge, early_parts = lax.optimization_barrier((edge, early_parts))
     w_out_grad, early_total = run(
         early_sum_kernel, "early_sum",
-        [((piece, width), F32), ((SPARE * 3 * piece, N), F32)], early_parts,
+        [((piece, width), F32), ((3 * piece, N), F32)], early_parts,
     )
     keep, send = run(
         rows_kernel, "rows",
-        [((SPARE * parts // 2, rows, 2 * depth), BF16), ((parts // 2, rows, 2 * depth), BF16)],
+        [((parts // 2, rows, 2 * depth), BF16), ((parts // 2, rows, 2 * depth), BF16)],
         [low_spot, sg, gp, graw, edge, w, dtw], (0,),
         scratch=[pltpu.VMEM((length, 2 * depth), BF16)],
     )

time: 86.2 us -> 84.9 us (0.985)
  local copies, waits for them, and re-layouts: 10.8 us -> 4.09 us
  waiting for transfers between devices: 18.9 us -> 24.2 us
    unnamed x34 -> x26, local copies, waits for them, and re-layouts: 10 us -> 3.37 us
    ppermute x6, waiting for transfers between devices: 5.38 us -> 9.05 us  [shifted(): return lax.ppermute(block, axis, route)]
    ppermute x14, waiting for transfers between devices: 13.5 us -> 15.1 us  [swapped(): lax.ppermute(block, axis, [(i, i ^ flip) for i in range(lax.axis_size(axi...]
  transfers between devices with their start and end apart: 20 -> 20, of which waited for: 10 -> 11; matrix products, arithmetic and copies ran while one was open for 0% -> 0% of each run, Pallas kernels for 15% -> 17%
where the time goes in v1:
time: 84.9 us; the launch traced here: 84.4 us
  starting transfers between devices  37.4 us (44%)
  waiting for transfers between devices  24.2 us (29%)
  Pallas kernels  17.9 us (21%)
  local copies, waits for them, and re-layouts  4.09 us (5%)
  between operations  0.93 us (1%)
    ppermute x14, starting transfers between devices, swapped(): lax.ppermute(block, axis, [(i, i ^ flip) for i in range(lax.axis_size(axi...  19.1 us
    ppermute x6, starting transfers between devices, shifted(): return lax.ppermute(block, axis, route)  18.2 us
    pallas_call x20, Pallas kernels, run(): pl.pallas_call(whole if fetched else kernel, name=name, out_shape=[jax.Sh...  17.9 us
    ppermute x14, waiting for transfers between devices, swapped(): lax.ppermute(block, axis, [(i, i ^ flip) for i in range(lax.axis_size(axi...  15.1 us
    ppermute x6, waiting for transfers between devices, shifted(): return lax.ppermute(block, axis, route)  9.05 us
    unnamed x26, local copies, waits for them, and re-layouts  3.37 us
  transfers between devices with their start and end apart: 20, of which 11 were waited for; matrix products, arithmetic and copies ran while one was open for 0% of the time, Pallas kernels for 17%

profile of v1, /device:TPU:0, one launch (start us, length us, event | category | flops | bytes accessed | tf_op | source)
XLA Modules:
  0.0 84.4 jit_solution(16251292131177947871)
XLA Ops:
  1.4 4.9 %collective-permute-start = (bf16[16,512]{1,0:T(8,128)(2,1)S(1)}, bf16[16,512]{1,0:T(8,128)(2,1)S(1)}, u32[]{:S(2)}, u32[]{:S(2)}) collective-permute-start(bf16[16,512]{1,0:T(8,128)(2,1)S(1)} %slice.3), channel_id=1, source_target_pairs={{0,4},{4,8},{8,12},{12,16},{16,20},{20,24},{24,28},{1,5},{5,9},{9,... | collective-permute-start | bytes 49160 | tf_op jit(solution)/shard_map/ppermute | solution.py:555
  6.2 2.3 %project.1 = (bf16[256,256]{1,0:T(8,128)(2,1)S(1)}, bf16[256,512]{1,0:T(8,128)(2,1)S(1)}, f32[32,256]{1,0:T(8,128)S(1)}, bf16[2,512,256]{2,1,0:T(8,128)(2,1)S(1)}) custom-call(bf16[256,512]{1,0:T(8,128)(2,1)} %series.3, bf16[3,512,256]{2,1,0:T(8,128)(2,1)} %bitcast.9, bf16[4,512]{1,0:T(4,128)(2,1)} %bitcast.12, f32[4]{0:T(128)} %refs_3_.1, f32[4]{0:T(128)} %refs_4_.1, ...), custom_call_target="tpu_custom_call" | custom-call | flops 1000000 | bytes 16384 | tf_op jit(solution)/shard_map/project/pallas_call | solution.py:540
  9.5 1.6 %collective-permute-start.1 = (bf16[272,128]{1,0:T(8,128)(2,1)S(1)}, bf16[272,128]{1,0:T(8,128)(2,1)S(1)}, u32[]{:S(2)}, u32[]{:S(2)}) collective-permute-start(bf16[272,128]{1,0:T(8,128)(2,1)S(1)} %get-tuple-element.92.mine), channel_id=1, source_target_pairs={{0,4},{4,0},{8,12},{12,8},{16,20},{20,16},{24,28},{28,24},{1,5},{5... | collective-permute-start | bytes 208904 | tf_op jit(solution)/shard_map/ppermute | solution.py:559
  12.0 1.9 %collective-permute-done.1.other.partner = bf16[272,128]{1,0:T(8,128)(2,1)S(1)} collective-permute-done((bf16[272,128]{1,0:T(8,128)(2,1)S(1)}, bf16[272,128]{1,0:T(8,128)(2,1)S(1)}, u32[]{:S(2)}, u32[]{:S(2)}) %collective-permute-start.1) | collective-permute-done | bytes 69664 | tf_op jit(solution)/shard_map/ppermute | solution.py:559
  13.9 4.2 %collective-permute-start.2 = (bf16[272,128]{1,0:T(8,128)(2,1)S(1)}, bf16[272,128]{1,0:T(8,128)(2,1)S(1)}, u32[]{:S(2)}, u32[]{:S(2)}) collective-permute-start(bf16[272,128]{1,0:T(8,128)(2,1)S(1)} %pair.2.nearer), channel_id=1, source_target_pairs={{0,8},{4,12},{8,16},{12,20},{16,24},{20,28},{1,9},{5,13},{9,17},{1... | collective-permute-start | bytes 208904 | tf_op jit(solution)/shard_map/ppermute | solution.py:555
  18.2 1.9 %collective-permute-done.2.farther = bf16[272,128]{1,0:T(8,128)(2,1)S(1)} collective-permute-done((bf16[272,128]{1,0:T(8,128)(2,1)S(1)}, bf16[272,128]{1,0:T(8,128)(2,1)S(1)}, u32[]{:S(2)}, u32[]{:S(2)}) %collective-permute-start.2) | collective-permute-done | bytes 69664 | tf_op jit(solution)/shard_map/ppermute | solution.py:555
  20.2 5.3 %collective-permute-start.3 = (bf16[272,128]{1,0:T(8,128)(2,1)S(1)}, bf16[272,128]{1,0:T(8,128)(2,1)S(1)}, u32[]{:S(2)}, u32[]{:S(2)}) collective-permute-start(bf16[272,128]{1,0:T(8,128)(2,1)S(1)} %get-tuple-element.101), channel_id=1, source_target_pairs={{0,16},{4,20},{8,24},{12,28},{1,17},{5,21},{9,25},{13,29},{2,18},{... | collective-permute-start | bytes 208904 | tf_op jit(solution)/shard_map/ppermute | solution.py:555
  25.5 1.9 %collective-permute-done.3.rest_0_ = bf16[272,128]{1,0:T(8,128)(2,1)S(1)} collective-permute-done((bf16[272,128]{1,0:T(8,128)(2,1)S(1)}, bf16[272,128]{1,0:T(8,128)(2,1)S(1)}, u32[]{:S(2)}, u32[]{:S(2)}) %collective-permute-start.3) | collective-permute-done | bytes 69664 | tf_op jit(solution)/shard_map/ppermute | solution.py:555
  30.9 2.2 %collective-permute-done.5.other = f32[8,256]{1,0:T(8,128)S(1)} collective-permute-done((f32[8,256]{1,0:T(8,128)S(1)}, f32[8,256]{1,0:T(8,128)S(1)}, u32[]{:S(2)}, u32[]{:S(2)}) %collective-permute-start.5) | collective-permute-done | bytes 8224 | tf_op jit(solution)/shard_map/ppermute | solution.py:559
  34.7 2.1 %early.1 = (bf16[256,256]{1,0:T(8,128)(2,1)S(1)}, bf16[256,256]{1,0:T(8,128)(2,1)S(1)}, bf16[256,128]{1,0:T(8,128)(2,1)S(1)}, f32[256,128]{1,0:T(8,128)S(1)}, bf...) custom-call(s32[1]{0:T(128)} %bitcast.1.low, ...), custom_call_target="tpu_custom_call" | custom-call | flops 1000000 | bytes 16384 | tf_op jit(solution)/shard_map/early/pallas_call | solution.py:540
  40.3 1.6 %beside.1 = (bf16[256,1024]{1,0:T(8,128)(2,1)S(1)}, f32[256,512]{1,0:T(8,128)S(1)}, f32[8,256]{1,0:T(8,128)S(1)}) custom-call(bf16[256,256]{1,0:T(8,128)(2,1)S(1)} %get-tuple-element.118.normed, bf16[256,256]{1,0:T(8,128)(2,1)S(1)} %get-tuple-element.119.grad_gate, bf16[256,128]{1,0:T(8,128)(2,1)S(1)} %get-tuple-element.120.gp, ...), custom_call_target="tpu_custom_call" | custom-call | flops 1000000 | bytes 16384 | tf_op jit(solution)/shard_map/beside/pallas_call | solution.py:540
  42.0 3.3 %collective-permute-done.7.farther = bf16[272,128]{1,0:T(8,128)(2,1)S(1)} collective-permute-done((bf16[272,128]{1,0:T(8,128)(2,1)S(1)}, bf16[272,128]{1,0:T(8,128)(2,1)S(1)}, u32[]{:S(2)}, u32[]{:S(2)}) %collective-permute-start.7) | collective-permute-done | bytes 69664 | tf_op jit(solution)/shard_map/ppermute | solution.py:555
  47.3 1.7 %halve_early.1 = (f32[320,128]{1,0:T(8,128)S(1)}, bf16[320,128]{1,0:T(8,128)(2,1)}, bf16[320,128]{1,0:T(8,128)(2,1)}, bf16[320,128]{1,0:T(8,128)(2,1)}) custom-call(s32[1]{0:T(128)} %bitcast.high, bf16[4,320,128]{2,1,0:T(8,128)(2,1)S(1)} %get-tuple-element.143.keep, bf16[4,320,128]{2,1,0:T(8,128)(2,1)} %collective-permute-done.14.other), custom_call_target="tpu_custom_call" | custom-call | flops 1000000 | bytes 16384 | tf_op jit(solution)/shard_map/halve_early/pallas_call | solution.py:540
  49.7 2.0 %collective-permute-start.15 = (bf16[320,128]{1,0:T(8,128)(2,1)}, bf16[320,128]{1,0:T(8,128)(2,1)S(1)}, u32[]{:S(2)}, u32[]{:S(2)}) collective-permute-start(bf16[320,128]{1,0:T(8,128)(2,1)} %get-tuple-element.146), channel_id=1, source_target_pairs={{0,8},{4,12},{8,0},{12,4},{16,24},{20,28},{24,16},{28,20},{1,9},{5... | collective-permute-start | bytes 245768 | tf_op jit(solution)/shard_map/ppermute | solution.py:559
  51.7 4.1 %collective-permute-start.16 = (bf16[320,128]{1,0:T(8,128)(2,1)}, bf16[320,128]{1,0:T(8,128)(2,1)S(1)}, u32[]{:S(2)}, u32[]{:S(2)}) collective-permute-start(bf16[320,128]{1,0:T(8,128)(2,1)} %get-tuple-element.147), channel_id=1, source_target_pairs={{0,16},{4,20},{8,24},{12,28},{16,0},{20,4},{24,8},{28,12},{1,17},{... | collective-permute-start | bytes 245768 | tf_op jit(solution)/shard_map/ppermute | solution.py:559
  56.8 1.8 %close.1 = (f32[256,384]{1,0:T(8,128)S(1)}, bf16[256,384]{1,0:T(8,128)(2,1)S(1)}, bf16[16,384]{1,0:T(8,128)(2,1)S(1)}, bf16[16,512]{1,0:T(8,128)(2,1)S(1)}) custom-call(s32[1]{0:T(128)} %bitcast.1.low, bf16[256,256]{1,0:T(8,128)(2,1)S(1)} %get-tuple-element.90.x, bf16[256,256]{1,0:T(8,128)(2,1)S(1)} %get-tuple-element.91.bc, ...), custom_call_target="tpu_custom_call" | custom-call | flops 1000000 | bytes 16384 | tf_op jit(solution)/shard_map/close/pallas_call | solution.py:540
  63.1 1.9 %collective-permute-done.13.edge = bf16[16,512]{1,0:T(8,128)(2,1)S(1)} collective-permute-done((bf16[16,512]{1,0:T(8,128)(2,1)S(1)}, bf16[16,512]{1,0:T(8,128)(2,1)S(1)}, u32[]{:S(2)}, u32[]{:S(2)}) %collective-permute-start.13) | collective-permute-done | bytes 16416 | tf_op jit(solution)/shard_map/ppermute | solution.py:555
  65.6 2.2 %collective-permute-start.9 = (bf16[4,208,128]{2,1,0:T(8,128)(2,1)S(1)}, bf16[4,208,128]{2,1,0:T(8,128)(2,1)S(1)}, u32[]{:S(2)}, u32[]{:S(2)}) collective-permute-start(bf16[4,208,128]{2,1,0:T(8,128)(2,1)S(1)} %get-tuple-element.135), channel_id=1, source_target_pairs={{0,4},{4,0},{8,12},{12,8},{16,20},{20,16},{24,28},{28,24},{1,5},{5... | collective-permute-start | bytes 638984 | tf_op jit(solution)/shard_map/ppermute | solution.py:559
  67.9 1.6 %collective-permute-start.19 = (bf16[64,1024]{1,0:T(8,128)(2,1)S(1)}, bf16[64,1024]{1,0:T(8,128)(2,1)S(1)}, u32[]{:S(2)}, u32[]{:S(2)}) collective-permute-start(bf16[64,1024]{1,0:T(8,128)(2,1)S(1)} %get-tuple-element.153), channel_id=1, source_target_pairs={{0,2},{1,3},{2,0},{3,1},{4,6},{5,7},{6,4},{7,5},{8,10},{9,11},{10,... | collective-permute-start | bytes 393224 | tf_op jit(solution)/shard_map/ppermute | solution.py:559
  69.5 4.2 %collective-permute-done.9.other = bf16[4,208,128]{2,1,0:T(8,128)(2,1)S(1)} collective-permute-done((bf16[4,208,128]{2,1,0:T(8,128)(2,1)S(1)}, bf16[4,208,128]{2,1,0:T(8,128)(2,1)S(1)}, u32[]{:S(2)}, u32[]{:S(2)}) %collective-permute-start.9) | collective-permute-done | bytes 213024 | tf_op jit(solution)/shard_map/ppermute | solution.py:559
  73.7 1.8 %collective-permute-start.10 = (bf16[208,128]{1,0:T(8,128)(2,1)S(1)}, bf16[208,128]{1,0:T(8,128)(2,1)S(1)}, u32[]{:S(2)}, u32[]{:S(2)}) collective-permute-start(bf16[208,128]{1,0:T(8,128)(2,1)S(1)} %get-tuple-element.137), channel_id=1, source_target_pairs={{0,8},{4,12},{8,0},{12,4},{16,24},{20,28},{24,16},{28,20},{1,9},{5... | collective-permute-start | bytes 159752 | tf_op jit(solution)/shard_map/ppermute | solution.py:559
  75.5 2.3 %collective-permute-start.11 = (bf16[208,128]{1,0:T(8,128)(2,1)S(1)}, bf16[208,128]{1,0:T(8,128)(2,1)S(1)}, u32[]{:S(2)}, u32[]{:S(2)}) collective-permute-start(bf16[208,128]{1,0:T(8,128)(2,1)S(1)} %get-tuple-element.138), channel_id=1, source_target_pairs={{0,16},{4,20},{8,24},{12,28},{16,0},{20,4},{24,8},{28,12},{1,17},{... | collective-permute-start | bytes 159752 | tf_op jit(solution)/shard_map/ppermute | solution.py:559
  79.5 1.6 %collective-permute-done.11.refs_2_ = bf16[208,128]{1,0:T(8,128)(2,1)S(1)} collective-permute-done((bf16[208,128]{1,0:T(8,128)(2,1)S(1)}, bf16[208,128]{1,0:T(8,128)(2,1)S(1)}, u32[]{:S(2)}, u32[]{:S(2)}) %collective-permute-start.11) | collective-permute-done | bytes 53280 | tf_op jit(solution)/shard_map/ppermute | solution.py:559
  81.2 2.5 %collective-permute-done.12.refs_3_ = bf16[208,128]{1,0:T(8,128)(2,1)S(1)} collective-permute-done((bf16[208,128]{1,0:T(8,128)(2,1)S(1)}, bf16[208,128]{1,0:T(8,128)(2,1)S(1)}, u32[]{:S(2)}, u32[]{:S(2)}) %collective-permute-start.12) | collective-permute-done | bytes 53280 | tf_op jit(solution)/shard_map/ppermute | solution.py:559
  (64 shorter events, 22.4 us)
Async XLA Ops:
  1.4 7.2 %collective-permute-start = (bf16[16,512]{1,0:T(8,128)(2,1)S(1)}, bf16[16,512]{1,0:T(8,128)(2,1)S(1)}, u32[]{:S(2)}, u32[]{:S(2)}) collective-permute-start(bf16[16,512]{1,0:T(8,128)(2,1)S(1)} %slice.3), channel_id=1, source_target_pairs={{0,4},{4,8},{8,12},{12,16},{16,20},{20,24},{24,28},{1,5},{5,9},{9,... | collective-permute-start | bytes 49160 | tf_op jit(solution)/shard_map/ppermute | solution.py:555
  9.5 4.4 %collective-permute-start.1 = (bf16[272,128]{1,0:T(8,128)(2,1)S(1)}, bf16[272,128]{1,0:T(8,128)(2,1)S(1)}, u32[]{:S(2)}, u32[]{:S(2)}) collective-permute-start(bf16[272,128]{1,0:T(8,128)(2,1)S(1)} %get-tuple-element.92.mine), channel_id=1, source_target_pairs={{0,4},{4,0},{8,12},{12,8},{16,20},{20,16},{24,28},{28,24},{1,5},{5... | collective-permute-start | bytes 208904 | tf_op jit(solution)/shard_map/ppermute | solution.py:559
  13.9 6.2 %collective-permute-start.2 = (bf16[272,128]{1,0:T(8,128)(2,1)S(1)}, bf16[272,128]{1,0:T(8,128)(2,1)S(1)}, u32[]{:S(2)}, u32[]{:S(2)}) collective-permute-start(bf16[272,128]{1,0:T(8,128)(2,1)S(1)} %pair.2.nearer), channel_id=1, source_target_pairs={{0,8},{4,12},{8,16},{12,20},{16,24},{20,28},{1,9},{5,13},{9,17},{1... | collective-permute-start | bytes 208904 | tf_op jit(solution)/shard_map/ppermute | solution.py:555
  20.2 7.2 %collective-permute-start.3 = (bf16[272,128]{1,0:T(8,128)(2,1)S(1)}, bf16[272,128]{1,0:T(8,128)(2,1)S(1)}, u32[]{:S(2)}, u32[]{:S(2)}) collective-permute-start(bf16[272,128]{1,0:T(8,128)(2,1)S(1)} %get-tuple-element.101), channel_id=1, source_target_pairs={{0,16},{4,20},{8,24},{12,28},{1,17},{5,21},{9,25},{13,29},{2,18},{... | collective-permute-start | bytes 208904 | tf_op jit(solution)/shard_map/ppermute | solution.py:555
  28.2 1.2 %collective-permute-start.4 = (f32[8,256]{1,0:T(8,128)S(1)}, f32[8,256]{1,0:T(8,128)S(1)}, u32[]{:S(2)}, u32[]{:S(2)}) collective-permute-start(f32[8,256]{1,0:T(8,128)S(1)} %get-tuple-element.103), channel_id=1, source_target_pairs={{0,1},{1,0},{2,3},{3,2},{4,5},{5,4},{6,7},{7,6},{8,9},{9,8},{10,11... | collective-permute-start | bytes 24584 | tf_op jit(solution)/shard_map/ppermute | solution.py:559
  29.4 3.7 %collective-permute-start.5 = (f32[8,256]{1,0:T(8,128)S(1)}, f32[8,256]{1,0:T(8,128)S(1)}, u32[]{:S(2)}, u32[]{:S(2)}) collective-permute-start(f32[8,256]{1,0:T(8,128)S(1)} %add.13.sums), channel_id=1, source_target_pairs={{0,2},{1,3},{2,0},{3,1},{4,6},{5,7},{6,4},{7,5},{8,10},{9,11},{10,... | collective-permute-start | bytes 24584 | tf_op jit(solution)/shard_map/ppermute | solution.py:559
  33.8 4.4 %collective-permute-start.6 = (bf16[272,128]{1,0:T(8,128)(2,1)S(1)}, bf16[272,128]{1,0:T(8,128)(2,1)S(1)}, u32[]{:S(2)}, u32[]{:S(2)}) collective-permute-start(bf16[272,128]{1,0:T(8,128)(2,1)S(1)} %get-tuple-element.106.mine), channel_id=1, source_target_pairs={{0,4},{4,0},{8,12},{12,8},{16,20},{20,16},{24,28},{28,24},{1,5},{5... | collective-permute-start | bytes 208904 | tf_op jit(solution)/shard_map/ppermute | solution.py:559
  34.7 5.7 %copy-start = (bf16[512,3,256]{2,0,1:T(8,128)(2,1)S(1)}, bf16[512,3,256]{2,0,1:T(8,128)(2,1)}, u32[]{:S(2)}) copy-start(bf16[512,3,256]{2,0,1:T(8,128)(2,1)} %param.12) | copy-start | bytes 2359300
  38.2 9.1 %collective-permute-start.14 = (bf16[4,320,128]{2,1,0:T(8,128)(2,1)}, bf16[4,320,128]{2,1,0:T(8,128)(2,1)}, u32[]{:S(2)}, u32[]{:S(2)}) collective-permute-start(bf16[4,320,128]{2,1,0:T(8,128)(2,1)} %get-tuple-element.144), channel_id=1, source_target_pairs={{0,4},{4,0},{8,12},{12,8},{16,20},{20,16},{24,28},{28,24},{1,5},{5... | collective-permute-start | bytes 983048 | tf_op jit(solution)/shard_map/ppermute | solution.py:559
  39.0 6.3 %collective-permute-start.7 = (bf16[272,128]{1,0:T(8,128)(2,1)S(1)}, bf16[272,128]{1,0:T(8,128)(2,1)S(1)}, u32[]{:S(2)}, u32[]{:S(2)}) collective-permute-start(bf16[272,128]{1,0:T(8,128)(2,1)S(1)} %pair.3.nearer), channel_id=1, source_target_pairs={{8,0},{12,4},{16,8},{20,12},{24,16},{28,20},{9,1},{13,5},{17,9},{2... | collective-permute-start | bytes 208904 | tf_op jit(solution)/shard_map/ppermute | solution.py:555
  46.0 3.0 %copy-start.8 = (f32[256,256]{1,0:T(8,128)}, f32[256,256]{1,0:T(8,128)S(1)}, u32[]{:S(2)}) copy-start(f32[256,256]{1,0:T(8,128)S(1)} %get-tuple-element.129.rest_1_) | copy-start | bytes 786436
  46.0 9.8 %collective-permute-start.8 = (bf16[272,128]{1,0:T(8,128)(2,1)}, bf16[272,128]{1,0:T(8,128)(2,1)}, u32[]{:S(2)}, u32[]{:S(2)}) collective-permute-start(bf16[272,128]{1,0:T(8,128)(2,1)} %get-tuple-element.128), channel_id=1, source_target_pairs={{16,0},{20,4},{24,8},{28,12},{17,1},{21,5},{25,9},{29,13},{18,2},{... | collective-permute-start | bytes 208904 | tf_op jit(solution)/shard_map/ppermute | solution.py:555
  47.3 8.5 %copy-start.7 = (bf16[272,128]{1,0:T(8,128)(2,1)S(1)}, bf16[272,128]{1,0:T(8,128)(2,1)}, u32[]{:S(2)}) copy-start(bf16[272,128]{1,0:T(8,128)(2,1)} %copy-done.6) | copy-start | bytes 208900
  49.7 15.3 %collective-permute-start.15 = (bf16[320,128]{1,0:T(8,128)(2,1)}, bf16[320,128]{1,0:T(8,128)(2,1)S(1)}, u32[]{:S(2)}, u32[]{:S(2)}) collective-permute-start(bf16[320,128]{1,0:T(8,128)(2,1)} %get-tuple-element.146), channel_id=1, source_target_pairs={{0,8},{4,12},{8,0},{12,4},{16,24},{20,28},{24,16},{28,20},{1,9},{5... | collective-permute-start | bytes 245768 | tf_op jit(solution)/shard_map/ppermute | solution.py:559
  51.7 13.3 %collective-permute-start.16 = (bf16[320,128]{1,0:T(8,128)(2,1)}, bf16[320,128]{1,0:T(8,128)(2,1)S(1)}, u32[]{:S(2)}, u32[]{:S(2)}) collective-permute-start(bf16[320,128]{1,0:T(8,128)(2,1)} %get-tuple-element.147), channel_id=1, source_target_pairs={{0,16},{4,20},{8,24},{12,28},{16,0},{20,4},{24,8},{28,12},{1,17},{... | collective-permute-start | bytes 245768 | tf_op jit(solution)/shard_map/ppermute | solution.py:559
  55.8 9.2 %collective-permute-start.17 = (bf16[320,128]{1,0:T(8,128)(2,1)}, bf16[320,128]{1,0:T(8,128)(2,1)S(1)}, u32[]{:S(2)}, u32[]{:S(2)}) collective-permute-start(bf16[320,128]{1,0:T(8,128)(2,1)} %get-tuple-element.148), channel_id=1, source_target_pairs={{0,24},{4,28},{8,16},{12,20},{16,8},{20,12},{24,0},{28,4},{1,25},{... | collective-permute-start | bytes 245768 | tf_op jit(solution)/shard_map/ppermute | solution.py:559
  59.4 5.6 %collective-permute-start.13 = (bf16[16,512]{1,0:T(8,128)(2,1)S(1)}, bf16[16,512]{1,0:T(8,128)(2,1)S(1)}, u32[]{:S(2)}, u32[]{:S(2)}) collective-permute-start(bf16[16,512]{1,0:T(8,128)(2,1)S(1)} %get-tuple-element.142), channel_id=1, source_target_pairs={{4,0},{8,4},{12,8},{16,12},{20,16},{24,20},{28,24},{5,1},{9,5},{13... | collective-permute-start | bytes 49160 | tf_op jit(solution)/shard_map/ppermute | solution.py:555
  65.5 2.3 %collective-permute-start.18 = (bf16[2,64,1024]{2,1,0:T(8,128)(2,1)S(1)}, bf16[2,64,1024]{2,1,0:T(8,128)(2,1)S(1)}, u32[]{:S(2)}, u32[]{:S(2)}) collective-permute-start(bf16[2,64,1024]{2,1,0:T(8,128)(2,1)S(1)} %get-tuple-element.151), channel_id=1, source_target_pairs={{0,1},{1,0},{2,3},{3,2},{4,5},{5,4},{6,7},{7,6},{8,9},{9,8},{10,11... | collective-permute-start | bytes 786440 | tf_op jit(solution)/shard_map/ppermute | solution.py:559
  65.6 8.1 %collective-permute-start.9 = (bf16[4,208,128]{2,1,0:T(8,128)(2,1)S(1)}, bf16[4,208,128]{2,1,0:T(8,128)(2,1)S(1)}, u32[]{:S(2)}, u32[]{:S(2)}) collective-permute-start(bf16[4,208,128]{2,1,0:T(8,128)(2,1)S(1)} %get-tuple-element.135), channel_id=1, source_target_pairs={{0,4},{4,0},{8,12},{12,8},{16,20},{20,16},{24,28},{28,24},{1,5},{5... | collective-permute-start | bytes 638984 | tf_op jit(solution)/shard_map/ppermute | solution.py:559
  67.9 10.9 %collective-permute-start.19 = (bf16[64,1024]{1,0:T(8,128)(2,1)S(1)}, bf16[64,1024]{1,0:T(8,128)(2,1)S(1)}, u32[]{:S(2)}, u32[]{:S(2)}) collective-permute-start(bf16[64,1024]{1,0:T(8,128)(2,1)S(1)} %get-tuple-element.153), channel_id=1, source_target_pairs={{0,2},{1,3},{2,0},{3,1},{4,6},{5,7},{6,4},{7,5},{8,10},{9,11},{10,... | collective-permute-start | bytes 393224 | tf_op jit(solution)/shard_map/ppermute | solution.py:559
  73.7 4.5 %copy-start.11 = (f32[320,128]{1,0:T(8,128)S(1)}, f32[320,128]{1,0:T(8,128)}, u32[]{:S(2)}) copy-start(f32[320,128]{1,0:T(8,128)} %copy-done.10) | copy-start | bytes 491524
  73.7 5.8 %collective-permute-start.10 = (bf16[208,128]{1,0:T(8,128)(2,1)S(1)}, bf16[208,128]{1,0:T(8,128)(2,1)S(1)}, u32[]{:S(2)}, u32[]{:S(2)}) collective-permute-start(bf16[208,128]{1,0:T(8,128)(2,1)S(1)} %get-tuple-element.137), channel_id=1, source_target_pairs={{0,8},{4,12},{8,0},{12,4},{16,24},{20,28},{24,16},{28,20},{1,9},{5... | collective-permute-start | bytes 159752 | tf_op jit(solution)/shard_map/ppermute | solution.py:559
  75.5 5.7 %collective-permute-start.11 = (bf16[208,128]{1,0:T(8,128)(2,1)S(1)}, bf16[208,128]{1,0:T(8,128)(2,1)S(1)}, u32[]{:S(2)}, u32[]{:S(2)}) collective-permute-start(bf16[208,128]{1,0:T(8,128)(2,1)S(1)} %get-tuple-element.138), channel_id=1, source_target_pairs={{0,16},{4,20},{8,24},{12,28},{16,0},{20,4},{24,8},{28,12},{1,17},{... | collective-permute-start | bytes 159752 | tf_op jit(solution)/shard_map/ppermute | solution.py:559
  77.8 5.9 %collective-permute-start.12 = (bf16[208,128]{1,0:T(8,128)(2,1)S(1)}, bf16[208,128]{1,0:T(8,128)(2,1)S(1)}, u32[]{:S(2)}, u32[]{:S(2)}) collective-permute-start(bf16[208,128]{1,0:T(8,128)(2,1)S(1)} %get-tuple-element.139), channel_id=1, source_target_pairs={{0,24},{4,28},{8,16},{12,20},{16,8},{20,12},{24,0},{28,4},{1,25},{... | collective-permute-start | bytes 159752 | tf_op jit(solution)/shard_map/ppermute | solution.py:559
  (9 other events, 12.8 us)

commit v2 on v1

--- a/solution.py
+++ b/solution.py
@@ -310,9 +310,9 @@
 
 
 def early_kernel(
-    heads, count, every,
+    heads, every,
     low, total, y, gate, gg, gy, x, bc, scal, sin, cot, series, rim, slope,
-    normed, grad_gate, gp, gb, edge, keep, send, wide, stage,
+    normed, grad_gate, gp, gb, edge, sums, wide,
 ):
     length, width = y.shape
     depth = series.shape[1]
@@ -341,15 +341,10 @@
     normed[...] = (gated * cols[:, 0:1] * scal[GAIN : GAIN + 1, :]).astype(BF16)
     grad_gated = cols[:, 0:1] * gg[...] - gated * cols[:, 1:2]
     grad_gate[...] = (grad_gated * yv * (sig * (1.0 + g * (1.0 - sig)))).astype(BF16)
-    w_out = mm(cot[...], normed[...], TN).astype(BF16)
-    w_gate = mm(series[...], grad_gate[...], TN).astype(BF16)
-    w_c = (mm(series[...], gp[...], TN) + mm(rim[...], edge[...], TN)).astype(BF16)
-    piece = depth // count
-    for at in range(count):
-        stack_columns(stage, w_out, at, 0, piece)
-        stack_columns(stage, w_gate, at, 2, piece)
-        stack_columns(stage, w_c, at, 4, piece)
-    split_pair(low[0], stage, keep, send)
+    sums[:, 0:width] = mm(cot[...], normed[...], TN).astype(BF16)
+    sums[:, width : 2 * width] = mm(series[...], grad_gate[...], TN).astype(BF16)
+    w_c = mm(series[...], gp[...], TN) + mm(rim[...], edge[...], TN)
+    sums[:, 2 * width :] = w_c.astype(BF16)
 
 
 def beside_kernel(
@@ -480,25 +475,16 @@
     grad[...] = total[:, depth:]
 
 
-def early_sum_kernel(*refs):
-    *parts, w_out, others = refs
-    piece = w_out.shape[0]
-    total = sum_of(parts)
-    for q in range(2):
-        w_out[:, q * N : (q + 1) * N] = total[q * piece : (q + 1) * piece, :]
-    others[0 : 3 * piece, :] = total[2 * piece :, :]
-
-
 def total_kernel(early, *refs):
-    *parts, w_in, w_dt = refs
-    piece = w_in.shape[1]
+    *parts, w_in, w_dt, w_out = refs
+    piece, width = w_out.shape
+    w_out[...] = early[:, 0:width].astype(F32)
+    w_in[0] = early[:, width : 2 * width].astype(F32)
+    w_in[2, :, N:] = early[:, 2 * width :].astype(F32)
     late = sum_of(parts)
     for q in range(2):
-        cut = slice(q * N, (q + 1) * N)
-        w_in[0, :, cut] = early[q * piece : (q + 1) * piece, :]
-        w_in[1, :, cut] = late[q * piece : (q + 1) * piece, :]
+        w_in[1, :, q * N : (q + 1) * N] = late[q * piece : (q + 1) * piece, :]
     w_in[2, :, 0:N] = late[2 * piece : 3 * piece, :]
-    w_in[2, :, N:] = early[2 * piece : 3 * piece, :]
     w_dt[...] = late[3 * piece : 3 * piece + w_dt.shape[0], 0:piece]
 
 
@@ -665,28 +651,24 @@
         [((length, width), F32), state_msg, ((8, length), F32)],
         [sums, swapped(sums, "head", flip), y, gate, gg, bc, scal],
     )
-    early, late = 5 * piece, 3 * piece + LOGS
+    late = 3 * piece + LOGS
 
     def early_part(made):
         return run(
-            part(early_kernel, heads, count, every), "early",
+            part(early_kernel, heads, every), "early",
             [
                 ((length, width), BF16),
                 ((length, width), BF16),
                 ((length, N), BF16),
                 ((length, N), F32),
                 ((RIM, N), BF16),
-                ((hops, early, N), BF16),
-                ((hops, early, N), BF16),
+                ((depth, 2 * width + N), BF16),
             ],
             [
                 low, total, y, gate, gg, gy, x, bc, scal, sin, cotangent, series, rim, slope,
             ],
             (0,),
-            scratch=[
-                pltpu.VMEM((length + RIM + 8, N), F32),
-                pltpu.VMEM((count, early, N), BF16),
-            ],
+            scratch=[pltpu.VMEM((length + RIM + 8, N), F32)],
         )
 
     def beside_part(made):
@@ -702,9 +684,8 @@
         )
 
     behind, (firsts, (sg, held, yb)) = passed(msg, True, [early_part, beside_part])
-    edge_c, keep, send = firsts[4:]
-    early_parts = halved(keep, send, "tm", high, "halve_early")
-    early_parts = gathered(early_parts, "tm")
+    edge_c, early = firsts[4:]
+    early = lax.psum_scatter(early, "tm", scatter_dimension=0, tiled=True)
     back, gp, lead, edge = run(
         part(close_kernel, heads), "close",
         [
@@ -726,11 +707,6 @@
     late_parts = halved(keep, send, "tm", high, "halve_late")
     late_parts = gathered(late_parts, "tm")
     rows = length // parts
-    edge, early_parts = lax.optimization_barrier((edge, early_parts))
-    w_out_grad, early_total = run(
-        early_sum_kernel, "early_sum",
-        [((piece, width), F32), ((3 * piece, N), F32)], early_parts,
-    )
     keep, send = run(
         rows_kernel, "rows",
         [((parts // 2, rows, 2 * depth), BF16), ((parts // 2, rows, 2 * depth), BF16)],
@@ -742,9 +718,10 @@
         outputs_kernel, "outputs", [((rows, depth), BF16), ((rows, depth), F32)], both,
     )
     late_parts, layer_out = lax.optimization_barrier((late_parts, layer_out))
-    w_in_grad, w_dt_grad = run(
+    w_in_grad, w_dt_grad, w_out_grad = run(
         total_kernel, "total",
-        [((3, piece, width), F32), ((heads, piece), F32)], [early_total] + late_parts,
+        [((3, piece, width), F32), ((heads, piece), F32), ((piece, width), F32)],
+        [early] + late_parts,
     )
     return (layer_out, series_grad, w_in_grad.transpose(1, 0, 2), w_dt_grad.T, w_out_grad)
 

time: 84.9 us -> 119 us (1.40)
  waiting for transfers between devices: 24.2 us -> 53.2 us
  between operations: 0.93 us -> 14.3 us
  starting transfers between devices: 37.4 us -> 30.1 us
  Pallas kernels: 17.9 us -> 14.8 us
  local copies, waits for them, and re-layouts: 4.09 us -> 6.17 us
    reduce_scatter x0 -> x1, waiting for transfers between devices: none -> 25.7 us  [body(): early = lax.psum_scatter(early, 'tm', scatter_dimension=0, tiled=True)]
    ppermute x14 -> x10, starting transfers between devices: 19.1 us -> 11.7 us  [swapped(): lax.ppermute(block, axis, [(i, i ^ flip) for i in range(lax.axis_size(axi...]
    ppermute x6, waiting for transfers between devices: 9.05 us -> 14.3 us  [shifted(): return lax.ppermute(block, axis, route)]
    pallas_call x20 -> x18, Pallas kernels: 17.9 us -> 14.8 us  [run(): pl.pallas_call(whole if fetched else kernel, name=name, out_shape=[jax.Sh...]
    unnamed x26 -> x28, local copies, waits for them, and re-layouts: 3.37 us -> 5.45 us
    ppermute x14 -> x10, waiting for transfers between devices: 15.1 us -> 13.2 us  [swapped(): lax.ppermute(block, axis, [(i, i ^ flip) for i in range(lax.axis_size(axi...]
  transfers between devices with their start and end apart: 20 -> 17, of which waited for: 11 -> 11; matrix products, arithmetic and copies ran while one was open for 0% -> 0% of each run, Pallas kernels for 17% -> 10%
where the time goes in v2:
time: 119 us
  waiting for transfers between devices  53.2 us (45%)
  starting transfers between devices  30.1 us (25%)
  Pallas kernels  14.8 us (12%)
  between operations  14.3 us (12%)
  local copies, waits for them, and re-layouts  6.17 us (5%)
    reduce_scatter x1, waiting for transfers between devices, body(): early = lax.psum_scatter(early, 'tm', scatter_dimension=0, tiled=True)  25.7 us
    ppermute x6, starting transfers between devices, shifted(): return lax.ppermute(block, axis, route)  18.4 us
    pallas_call x18, Pallas kernels, run(): pl.pallas_call(whole if fetched else kernel, name=name, out_shape=[jax.Sh...  14.8 us
    ppermute x6, waiting for transfers between devices, shifted(): return lax.ppermute(block, axis, route)  14.3 us
    ppermute x10, waiting for transfers between devices, swapped(): lax.ppermute(block, axis, [(i, i ^ flip) for i in range(lax.axis_size(axi...  13.2 us
    ppermute x10, starting transfers between devices, swapped(): lax.ppermute(block, axis, [(i, i ^ flip) for i in range(lax.axis_size(axi...  11.7 us
    unnamed x28, local copies, waits for them, and re-layouts  5.45 us
  transfers between devices with their start and end apart: 17, of which 11 were waited for; matrix products, arithmetic and copies ran while one was open for 0% of the time, Pallas kernels for 10%

profile of v2, /device:TPU:0, one launch (start us, length us, event | category | flops | bytes accessed | tf_op | source)
XLA Modules:
  0.0 118.5 jit_solution(2001244803558823545)
XLA Ops:
  7.9 4.9 %collective-permute-start = (bf16[16,512]{1,0:T(8,128)(2,1)S(1)}, bf16[16,512]{1,0:T(8,128)(2,1)S(1)}, u32[]{:S(2)}, u32[]{:S(2)}) collective-permute-start(bf16[16,512]{1,0:T(8,128)(2,1)S(1)} %slice.3), channel_id=1, source_target_pairs={{0,4},{4,8},{8,12},{12,16},{16,20},{20,24},{24,28},{1,5},{5,9},{9,... | collective-permute-start | bytes 49160 | tf_op jit(solution)/shard_map/ppermute | solution.py:541
  12.8 2.3 %project.1 = (bf16[256,256]{1,0:T(8,128)(2,1)S(1)}, bf16[256,512]{1,0:T(8,128)(2,1)S(1)}, f32[32,256]{1,0:T(8,128)S(1)}, bf16[2,512,256]{2,1,0:T(8,128)(2,1)S(1)}) custom-call(bf16[256,512]{1,0:T(8,128)(2,1)} %series.3, bf16[3,512,256]{2,1,0:T(8,128)(2,1)} %bitcast.9, bf16[4,512]{1,0:T(4,128)(2,1)} %bitcast.12, f32[4]{0:T(128)} %refs_3_.1, f32[4]{0:T(128)} %refs_4_.1, ...), custom_call_target="tpu_custom_call" | custom-call | flops 1000000 | bytes 16384 | tf_op jit(solution)/shard_map/project/pallas_call | solution.py:526
  16.1 1.6 %collective-permute-start.1 = (bf16[272,128]{1,0:T(8,128)(2,1)S(1)}, bf16[272,128]{1,0:T(8,128)(2,1)S(1)}, u32[]{:S(2)}, u32[]{:S(2)}) collective-permute-start(bf16[272,128]{1,0:T(8,128)(2,1)S(1)} %get-tuple-element.80.mine), channel_id=1, source_target_pairs={{0,4},{4,0},{8,12},{12,8},{16,20},{20,16},{24,28},{28,24},{1,5},{5... | collective-permute-start | bytes 208904 | tf_op jit(solution)/shard_map/ppermute | solution.py:545
  18.5 1.9 %collective-permute-done.1.other.partner = bf16[272,128]{1,0:T(8,128)(2,1)S(1)} collective-permute-done((bf16[272,128]{1,0:T(8,128)(2,1)S(1)}, bf16[272,128]{1,0:T(8,128)(2,1)S(1)}, u32[]{:S(2)}, u32[]{:S(2)}) %collective-permute-start.1) | collective-permute-done | bytes 69664 | tf_op jit(solution)/shard_map/ppermute | solution.py:545
  20.5 4.2 %collective-permute-start.2 = (bf16[272,128]{1,0:T(8,128)(2,1)S(1)}, bf16[272,128]{1,0:T(8,128)(2,1)S(1)}, u32[]{:S(2)}, u32[]{:S(2)}) collective-permute-start(bf16[272,128]{1,0:T(8,128)(2,1)S(1)} %pair.2.nearer), channel_id=1, source_target_pairs={{0,8},{4,12},{8,16},{12,20},{16,24},{20,28},{1,9},{5,13},{9,17},{1... | collective-permute-start | bytes 208904 | tf_op jit(solution)/shard_map/ppermute | solution.py:541
  24.8 1.9 %collective-permute-done.2.farther = bf16[272,128]{1,0:T(8,128)(2,1)S(1)} collective-permute-done((bf16[272,128]{1,0:T(8,128)(2,1)S(1)}, bf16[272,128]{1,0:T(8,128)(2,1)S(1)}, u32[]{:S(2)}, u32[]{:S(2)}) %collective-permute-start.2) | collective-permute-done | bytes 69664 | tf_op jit(solution)/shard_map/ppermute | solution.py:541
  26.7 5.3 %collective-permute-start.3 = (bf16[272,128]{1,0:T(8,128)(2,1)S(1)}, bf16[272,128]{1,0:T(8,128)(2,1)S(1)}, u32[]{:S(2)}, u32[]{:S(2)}) collective-permute-start(bf16[272,128]{1,0:T(8,128)(2,1)S(1)} %get-tuple-element.89), channel_id=1, source_target_pairs={{0,16},{4,20},{8,24},{12,28},{1,17},{5,21},{9,25},{13,29},{2,18},{... | collective-permute-start | bytes 208904 | tf_op jit(solution)/shard_map/ppermute | solution.py:541
  32.0 1.9 %collective-permute-done.3.rest_0_ = bf16[272,128]{1,0:T(8,128)(2,1)S(1)} collective-permute-done((bf16[272,128]{1,0:T(8,128)(2,1)S(1)}, bf16[272,128]{1,0:T(8,128)(2,1)S(1)}, u32[]{:S(2)}, u32[]{:S(2)}) %collective-permute-start.3) | collective-permute-done | bytes 69664 | tf_op jit(solution)/shard_map/ppermute | solution.py:541
  36.0 1.5 %collective-permute-start.5 = (f32[8,256]{1,0:T(8,128)S(1)}, f32[8,256]{1,0:T(8,128)S(1)}, u32[]{:S(2)}, u32[]{:S(2)}) collective-permute-start(f32[8,256]{1,0:T(8,128)S(1)} %add.15.sums), channel_id=1, source_target_pairs={{0,2},{1,3},{2,0},{3,1},{4,6},{5,7},{6,4},{7,5},{8,10},{9,11},{10,... | collective-permute-start | bytes 24584 | tf_op jit(solution)/shard_map/ppermute | solution.py:545
  37.5 2.2 %collective-permute-done.5.other = f32[8,256]{1,0:T(8,128)S(1)} collective-permute-done((f32[8,256]{1,0:T(8,128)S(1)}, f32[8,256]{1,0:T(8,128)S(1)}, u32[]{:S(2)}, u32[]{:S(2)}) %collective-permute-start.5) | collective-permute-done | bytes 8224 | tf_op jit(solution)/shard_map/ppermute | solution.py:545
  41.2 2.2 %early.1 = (bf16[256,256]{1,0:T(8,128)(2,1)S(1)}, bf16[256,256]{1,0:T(8,128)(2,1)S(1)}, bf16[256,128]{1,0:T(8,128)(2,1)S(1)}, f32[256,128]{1,0:T(8,128)S(1)}, bf...) custom-call(s32[1]{0:T(128)} %bitcast.1.low, f32[8,256]{1,0:T(8,128)S(1)} %get-tuple-element.95.total, ...), custom_call_target="tpu_custom_call" | custom-call | flops 1000000 | bytes 16384 | tf_op jit(solution)/shard_map/early/pallas_call | solution.py:526
  45.5 1.4 %collective-permute-start.7 = (bf16[272,128]{1,0:T(8,128)(2,1)S(1)}, bf16[272,128]{1,0:T(8,128)(2,1)S(1)}, u32[]{:S(2)}, u32[]{:S(2)}) collective-permute-start(bf16[272,128]{1,0:T(8,128)(2,1)S(1)} %pair.3.nearer), channel_id=1, source_target_pairs={{8,0},{12,4},{16,8},{20,12},{24,16},{28,20},{9,1},{13,5},{17,9},{2... | collective-permute-start | bytes 208904 | tf_op jit(solution)/shard_map/ppermute | solution.py:541
  48.8 1.6 %beside.1 = (bf16[256,1024]{1,0:T(8,128)(2,1)S(1)}, f32[256,512]{1,0:T(8,128)S(1)}, f32[8,256]{1,0:T(8,128)S(1)}) custom-call(bf16[256,256]{1,0:T(8,128)(2,1)S(1)} %get-tuple-element.105.normed, bf16[256,256]{1,0:T(8,128)(2,1)S(1)} %copy-done.7, bf16[256,128]{1,0:T(8,128)(2,1)S(1)} %copy-done.12, f32[256,128]{1,0:T(8,128)S(1)} %copy-done.9, ...), custom_call_target="tpu_custom_call" | custom-call | flops 1000000 | bytes 16384 | tf_op jit(solution)/shard_map/beside/pallas_call | solution.py:526
  52.0 1.3 %collective-permute-start.8 = (bf16[272,128]{1,0:T(8,128)(2,1)S(1)}, bf16[272,128]{1,0:T(8,128)(2,1)S(1)}, u32[]{:S(2)}, u32[]{:S(2)}) collective-permute-start(bf16[272,128]{1,0:T(8,128)(2,1)S(1)} %get-tuple-element.115), channel_id=1, source_target_pairs={{16,0},{20,4},{24,8},{28,12},{17,1},{21,5},{25,9},{29,13},{18,2},{... | collective-permute-start | bytes 208904 | tf_op jit(solution)/shard_map/ppermute | solution.py:541
  53.3 7.5 %collective-permute-done.8.rest_0_ = bf16[272,128]{1,0:T(8,128)(2,1)S(1)} collective-permute-done((bf16[272,128]{1,0:T(8,128)(2,1)S(1)}, bf16[272,128]{1,0:T(8,128)(2,1)S(1)}, u32[]{:S(2)}, u32[]{:S(2)}) %collective-permute-start.8) | collective-permute-done | bytes 69664 | tf_op jit(solution)/shard_map/ppermute | solution.py:541
  61.7 1.3 %collective-permute-start.13 = (bf16[16,512]{1,0:T(8,128)(2,1)S(1)}, bf16[16,512]{1,0:T(8,128)(2,1)S(1)}, u32[]{:S(2)}, u32[]{:S(2)}) collective-permute-start(bf16[16,512]{1,0:T(8,128)(2,1)S(1)} %get-tuple-element.129), channel_id=1, source_target_pairs={{4,0},{8,4},{12,8},{16,12},{20,16},{24,20},{28,24},{5,1},{9,5},{13... | collective-permute-start | bytes 49160 | tf_op jit(solution)/shard_map/ppermute | solution.py:541
  63.0 2.1 %late.1 = (bf16[4,208,128]{2,1,0:T(8,128)(2,1)S(1)}, bf16[4,208,128]{2,1,0:T(8,128)(2,1)}, f32[8,256]{1,0:T(8,128)S(1)}) custom-call(s32[1]{0:T(128)} %bitcast.1.low, bf16[256,256]{1,0:T(8,128)(2,1)S(1)} %get-tuple-element.78.x, f32[32,256]{1,0:T(8,128)S(1)} %get-tuple-element.77.scal, f32[256,384]{1,0:T(8,128)S(1)} %get-tuple-element.117.back, ...), custom_call_target="tpu_custom_call" | custom-call | flops 1000000 | bytes 16384 | tf_op jit(solution)/shard_map/late/pallas_call | solution.py:526
  65.1 2.2 %collective-permute-done.13.edge = bf16[16,512]{1,0:T(8,128)(2,1)S(1)} collective-permute-done((bf16[16,512]{1,0:T(8,128)(2,1)S(1)}, bf16[16,512]{1,0:T(8,128)(2,1)S(1)}, u32[]{:S(2)}, u32[]{:S(2)}) %collective-permute-start.13) | collective-permute-done | bytes 16416 | tf_op jit(solution)/shard_map/ppermute | solution.py:541
  67.9 1.6 %collective-permute-start.9 = (bf16[4,208,128]{2,1,0:T(8,128)(2,1)}, bf16[4,208,128]{2,1,0:T(8,128)(2,1)S(1)}, u32[]{:S(2)}, u32[]{:S(2)}) collective-permute-start(bf16[4,208,128]{2,1,0:T(8,128)(2,1)} %get-tuple-element.122), channel_id=1, source_target_pairs={{0,4},{4,0},{8,12},{12,8},{16,20},{20,16},{24,28},{28,24},{1,5},{5... | collective-permute-start | bytes 638984 | tf_op jit(solution)/shard_map/ppermute | solution.py:545
  69.6 1.7 %collective-permute-start.15 = (bf16[64,1024]{1,0:T(8,128)(2,1)S(1)}, bf16[64,1024]{1,0:T(8,128)(2,1)S(1)}, u32[]{:S(2)}, u32[]{:S(2)}) collective-permute-start(bf16[64,1024]{1,0:T(8,128)(2,1)S(1)} %get-tuple-element.133), channel_id=1, source_target_pairs={{0,2},{1,3},{2,0},{3,1},{4,6},{5,7},{6,4},{7,5},{8,10},{9,11},{10,... | collective-permute-start | bytes 393224 | tf_op jit(solution)/shard_map/ppermute | solution.py:545
  71.3 5.0 %collective-permute-done.9.other = bf16[4,208,128]{2,1,0:T(8,128)(2,1)S(1)} collective-permute-done((bf16[4,208,128]{2,1,0:T(8,128)(2,1)}, bf16[4,208,128]{2,1,0:T(8,128)(2,1)S(1)}, u32[]{:S(2)}, u32[]{:S(2)}) %collective-permute-start.9) | collective-permute-done | bytes 213024 | tf_op jit(solution)/shard_map/ppermute | solution.py:545
  77.4 3.3 %collective-permute-start.12 = (bf16[208,128]{1,0:T(8,128)(2,1)S(1)}, bf16[208,128]{1,0:T(8,128)(2,1)S(1)}, u32[]{:S(2)}, u32[]{:S(2)}) collective-permute-start(bf16[208,128]{1,0:T(8,128)(2,1)S(1)} %get-tuple-element.126), channel_id=1, source_target_pairs={{0,24},{4,28},{8,16},{12,20},{16,8},{20,12},{24,0},{28,4},{1,25},{... | collective-permute-start | bytes 159752 | tf_op jit(solution)/shard_map/ppermute | solution.py:545
  81.5 2.9 %collective-permute-done.11.refs_2_ = bf16[208,128]{1,0:T(8,128)(2,1)S(1)} collective-permute-done((bf16[208,128]{1,0:T(8,128)(2,1)S(1)}, bf16[208,128]{1,0:T(8,128)(2,1)S(1)}, u32[]{:S(2)}, u32[]{:S(2)}) %collective-permute-start.11) | collective-permute-done | bytes 53280 | tf_op jit(solution)/shard_map/ppermute | solution.py:545
  84.4 25.7 %reduce-scatter.2.cloned.1.call-done.early = bf16[64,640]{1,0:T(8,128)(2,1)} async-done(((bf16[512,640]{1,0:T(8,128)(2,1)}), bf16[64,640]{1,0:T(8,128)(2,1)}) %reduce-scatter.2.cloned.1.call-update) | async-done | bytes 81936 | tf_op jit(solution)/shard_map/reduce_scatter | solution.py:688
  (59 shorter events, 16.7 us)
Async XLA Ops:
  7.2 102.9 %reduce-scatter.2.cloned.1.call-start = ((), (), s32[]{:S(2)}) async-start(), calls=%async_computation.1 | async-start | bytes 737280 | tf_op jit(solution)/shard_map/reduce_scatter | solution.py:688
  7.9 7.2 %collective-permute-start = (bf16[16,512]{1,0:T(8,128)(2,1)S(1)}, bf16[16,512]{1,0:T(8,128)(2,1)S(1)}, u32[]{:S(2)}, u32[]{:S(2)}) collective-permute-start(bf16[16,512]{1,0:T(8,128)(2,1)S(1)} %slice.3), channel_id=1, source_target_pairs={{0,4},{4,8},{8,12},{12,16},{16,20},{20,24},{24,28},{1,5},{5,9},{9,... | collective-permute-start | bytes 49160 | tf_op jit(solution)/shard_map/ppermute | solution.py:541
  15.1 2.6 %copy-start.2 = (bf16[256,512]{1,0:T(8,128)(2,1)S(1)}, bf16[256,512]{1,0:T(8,128)(2,1)}, u32[]{:S(2)}) copy-start(bf16[256,512]{1,0:T(8,128)(2,1)} %cot.3) | copy-start | bytes 786436
  15.1 2.6 %copy-start.3 = (bf16[512,256]{1,0:T(8,128)(2,1)S(1)}, bf16[512,256]{1,0:T(8,128)(2,1)}, u32[]{:S(2)}) copy-start(bf16[512,256]{1,0:T(8,128)(2,1)} %ow.3) | copy-start | bytes 786436
  16.1 4.4 %collective-permute-start.1 = (bf16[272,128]{1,0:T(8,128)(2,1)S(1)}, bf16[272,128]{1,0:T(8,128)(2,1)S(1)}, u32[]{:S(2)}, u32[]{:S(2)}) collective-permute-start(bf16[272,128]{1,0:T(8,128)(2,1)S(1)} %get-tuple-element.80.mine), channel_id=1, source_target_pairs={{0,4},{4,0},{8,12},{12,8},{16,20},{20,16},{24,28},{28,24},{1,5},{5... | collective-permute-start | bytes 208904 | tf_op jit(solution)/shard_map/ppermute | solution.py:545
  20.5 6.2 %collective-permute-start.2 = (bf16[272,128]{1,0:T(8,128)(2,1)S(1)}, bf16[272,128]{1,0:T(8,128)(2,1)S(1)}, u32[]{:S(2)}, u32[]{:S(2)}) collective-permute-start(bf16[272,128]{1,0:T(8,128)(2,1)S(1)} %pair.2.nearer), channel_id=1, source_target_pairs={{0,8},{4,12},{8,16},{12,20},{16,24},{20,28},{1,9},{5,13},{9,17},{1... | collective-permute-start | bytes 208904 | tf_op jit(solution)/shard_map/ppermute | solution.py:541
  26.7 7.2 %collective-permute-start.3 = (bf16[272,128]{1,0:T(8,128)(2,1)S(1)}, bf16[272,128]{1,0:T(8,128)(2,1)S(1)}, u32[]{:S(2)}, u32[]{:S(2)}) collective-permute-start(bf16[272,128]{1,0:T(8,128)(2,1)S(1)} %get-tuple-element.89), channel_id=1, source_target_pairs={{0,16},{4,20},{8,24},{12,28},{1,17},{5,21},{9,25},{13,29},{2,18},{... | collective-permute-start | bytes 208904 | tf_op jit(solution)/shard_map/ppermute | solution.py:541
  34.8 1.2 %collective-permute-start.4 = (f32[8,256]{1,0:T(8,128)S(1)}, f32[8,256]{1,0:T(8,128)S(1)}, u32[]{:S(2)}, u32[]{:S(2)}) collective-permute-start(f32[8,256]{1,0:T(8,128)S(1)} %get-tuple-element.91), channel_id=1, source_target_pairs={{0,1},{1,0},{2,3},{3,2},{4,5},{5,4},{6,7},{7,6},{8,9},{9,8},{10,11... | collective-permute-start | bytes 24584 | tf_op jit(solution)/shard_map/ppermute | solution.py:545
  36.0 3.7 %collective-permute-start.5 = (f32[8,256]{1,0:T(8,128)S(1)}, f32[8,256]{1,0:T(8,128)S(1)}, u32[]{:S(2)}, u32[]{:S(2)}) collective-permute-start(f32[8,256]{1,0:T(8,128)S(1)} %add.15.sums), channel_id=1, source_target_pairs={{0,2},{1,3},{2,0},{3,1},{4,6},{5,7},{6,4},{7,5},{8,10},{9,11},{10,... | collective-permute-start | bytes 24584 | tf_op jit(solution)/shard_map/ppermute | solution.py:545
  39.6 1.6 %copy-start.1 = (bf16[256,512]{1,0:T(8,128)(2,1)S(1)}, bf16[256,512]{1,0:T(8,128)(2,1)}, u32[]{:S(2)}) copy-start(bf16[256,512]{1,0:T(8,128)(2,1)} %series.3) | copy-start | bytes 786436
  40.4 5.0 %collective-permute-start.6 = (bf16[272,128]{1,0:T(8,128)(2,1)S(1)}, bf16[272,128]{1,0:T(8,128)(2,1)S(1)}, u32[]{:S(2)}, u32[]{:S(2)}) collective-permute-start(bf16[272,128]{1,0:T(8,128)(2,1)S(1)} %get-tuple-element.94.mine), channel_id=1, source_target_pairs={{0,4},{4,0},{8,12},{12,8},{16,20},{20,16},{24,28},{28,24},{1,5},{5... | collective-permute-start | bytes 208904 | tf_op jit(solution)/shard_map/ppermute | solution.py:545
  45.4 1.5 %copy-start = (bf16[512,3,256]{2,0,1:T(8,128)(2,1)S(1)}, bf16[512,3,256]{2,0,1:T(8,128)(2,1)}, u32[]{:S(2)}) copy-start(bf16[512,3,256]{2,0,1:T(8,128)(2,1)} %param.12) | copy-start | bytes 2359300
  45.4 1.5 %copy-start.12 = (bf16[256,128]{1,0:T(8,128)(2,1)S(1)}, bf16[256,128]{1,0:T(8,128)(2,1)}, u32[]{:S(2)}) copy-start(bf16[256,128]{1,0:T(8,128)(2,1)} %copy-done.11) | copy-start | bytes 196612
  45.5 6.4 %collective-permute-start.7 = (bf16[272,128]{1,0:T(8,128)(2,1)S(1)}, bf16[272,128]{1,0:T(8,128)(2,1)S(1)}, u32[]{:S(2)}, u32[]{:S(2)}) collective-permute-start(bf16[272,128]{1,0:T(8,128)(2,1)S(1)} %pair.3.nearer), channel_id=1, source_target_pairs={{8,0},{12,4},{16,8},{20,12},{24,16},{28,20},{9,1},{13,5},{17,9},{2... | collective-permute-start | bytes 208904 | tf_op jit(solution)/shard_map/ppermute | solution.py:541
  52.0 8.8 %collective-permute-start.8 = (bf16[272,128]{1,0:T(8,128)(2,1)S(1)}, bf16[272,128]{1,0:T(8,128)(2,1)S(1)}, u32[]{:S(2)}, u32[]{:S(2)}) collective-permute-start(bf16[272,128]{1,0:T(8,128)(2,1)S(1)} %get-tuple-element.115), channel_id=1, source_target_pairs={{16,0},{20,4},{24,8},{28,12},{17,1},{21,5},{25,9},{29,13},{18,2},{... | collective-permute-start | bytes 208904 | tf_op jit(solution)/shard_map/ppermute | solution.py:541
  61.7 5.7 %collective-permute-start.13 = (bf16[16,512]{1,0:T(8,128)(2,1)S(1)}, bf16[16,512]{1,0:T(8,128)(2,1)S(1)}, u32[]{:S(2)}, u32[]{:S(2)}) collective-permute-start(bf16[16,512]{1,0:T(8,128)(2,1)S(1)} %get-tuple-element.129), channel_id=1, source_target_pairs={{4,0},{8,4},{12,8},{16,12},{20,16},{24,20},{28,24},{5,1},{9,5},{13... | collective-permute-start | bytes 49160 | tf_op jit(solution)/shard_map/ppermute | solution.py:541
  63.0 4.4 %copy-start.5 = (bf16[256,1024]{1,0:T(8,128)(2,1)S(1)}, bf16[256,1024]{1,0:T(8,128)(2,1)}, u32[]{:S(2)}) copy-start(bf16[256,1024]{1,0:T(8,128)(2,1)} %copy-done.4) | copy-start | bytes 1572868
  63.0 4.4 %copy-start.13 = (bf16[512,4]{0,1:T(4,128)(2,1)S(1)}, bf16[512,4]{0,1:T(4,128)(2,1)}, u32[]{:S(2)}) copy-start(bf16[512,4]{0,1:T(4,128)(2,1)} %param.13) | copy-start | bytes 12292
  67.9 1.7 %collective-permute-start.14 = (bf16[2,64,1024]{2,1,0:T(8,128)(2,1)S(1)}, bf16[2,64,1024]{2,1,0:T(8,128)(2,1)S(1)}, u32[]{:S(2)}, u32[]{:S(2)}) collective-permute-start(bf16[2,64,1024]{2,1,0:T(8,128)(2,1)S(1)} %get-tuple-element.131), channel_id=1, source_target_pairs={{0,1},{1,0},{2,3},{3,2},{4,5},{5,4},{6,7},{7,6},{8,9},{9,8},{10,11... | collective-permute-start | bytes 786440 | tf_op jit(solution)/shard_map/ppermute | solution.py:545
  67.9 8.3 %collective-permute-start.9 = (bf16[4,208,128]{2,1,0:T(8,128)(2,1)}, bf16[4,208,128]{2,1,0:T(8,128)(2,1)S(1)}, u32[]{:S(2)}, u32[]{:S(2)}) collective-permute-start(bf16[4,208,128]{2,1,0:T(8,128)(2,1)} %get-tuple-element.122), channel_id=1, source_target_pairs={{0,4},{4,0},{8,12},{12,8},{16,20},{20,16},{24,28},{28,24},{1,5},{5... | collective-permute-start | bytes 638984 | tf_op jit(solution)/shard_map/ppermute | solution.py:545
  69.6 11.2 %collective-permute-start.15 = (bf16[64,1024]{1,0:T(8,128)(2,1)S(1)}, bf16[64,1024]{1,0:T(8,128)(2,1)S(1)}, u32[]{:S(2)}, u32[]{:S(2)}) collective-permute-start(bf16[64,1024]{1,0:T(8,128)(2,1)S(1)} %get-tuple-element.133), channel_id=1, source_target_pairs={{0,2},{1,3},{2,0},{3,1},{4,6},{5,7},{6,4},{7,5},{8,10},{9,11},{10,... | collective-permute-start | bytes 393224 | tf_op jit(solution)/shard_map/ppermute | solution.py:545
  76.3 5.2 %collective-permute-start.10 = (bf16[208,128]{1,0:T(8,128)(2,1)S(1)}, bf16[208,128]{1,0:T(8,128)(2,1)S(1)}, u32[]{:S(2)}, u32[]{:S(2)}) collective-permute-start(bf16[208,128]{1,0:T(8,128)(2,1)S(1)} %get-tuple-element.124), channel_id=1, source_target_pairs={{0,8},{4,12},{8,0},{12,4},{16,24},{20,28},{24,16},{28,20},{1,9},{5... | collective-permute-start | bytes 159752 | tf_op jit(solution)/shard_map/ppermute | solution.py:545
  77.3 7.1 %collective-permute-start.11 = (bf16[208,128]{1,0:T(8,128)(2,1)S(1)}, bf16[208,128]{1,0:T(8,128)(2,1)S(1)}, u32[]{:S(2)}, u32[]{:S(2)}) collective-permute-start(bf16[208,128]{1,0:T(8,128)(2,1)S(1)} %get-tuple-element.125), channel_id=1, source_target_pairs={{0,16},{4,20},{8,24},{12,28},{16,0},{20,4},{24,8},{28,12},{1,17},{... | collective-permute-start | bytes 159752 | tf_op jit(solution)/shard_map/ppermute | solution.py:545
  77.4 6.9 %collective-permute-start.12 = (bf16[208,128]{1,0:T(8,128)(2,1)S(1)}, bf16[208,128]{1,0:T(8,128)(2,1)S(1)}, u32[]{:S(2)}, u32[]{:S(2)}) collective-permute-start(bf16[208,128]{1,0:T(8,128)(2,1)S(1)} %get-tuple-element.126), channel_id=1, source_target_pairs={{0,24},{4,28},{8,16},{12,20},{16,8},{20,12},{24,0},{28,4},{1,25},{... | collective-permute-start | bytes 159752 | tf_op jit(solution)/shard_map/ppermute | solution.py:545
  (7 other events, 5.4 us)
Sparse Core Ops, SparseCore 0:
  45.5 64.4 reduce-scatter.1

commit v3 on v1

--- a/solution.py
+++ b/solution.py
@@ -384,15 +384,17 @@
     heads,
     low, x, bc, scal, gy, held, slope, edge_c, partner, *rest,
 ):
-    far, *near, back, gp, lead, edge, wide = rest
+    far, *near, ends, gp, lead, edge, wide = rest
     length, width = gy.shape
     state = carried(low[0] == 0, partner[...], far[...], near[0] if near else None, heads)
-    back[0:width, width:] = state
     running, step = scal[0:heads, :], scal[heads : 2 * heads, :]
     remain = jnp.exp(running[:, length - 1 : length] - running)
     cols = columns(jnp.concatenate([remain, step, remain * step], axis=0))
     grown = held[:, 0:width] + widen(cols, heads, width) * mm(bc[:, 0:N], state, NT)
-    back[0:length, 0:width] = grown
+    mask = head_mask(heads, width)
+    ends[0 : 2 * heads, :] = mm_exact(mask, x[...].astype(F32) * grown, NT)
+    whole = jnp.sum(mm_exact(mask, state * held[:, width + N :]), axis=1, keepdims=True)
+    ends[2 * heads :, :] = jnp.broadcast_to(whole, (2 * heads, length))
     grad_x = scal[SKIP : SKIP + 1, :] * gy[...] + widen(cols[:, heads:], heads, width) * grown
     grad_b = held[:, width : width + N] + mm(x[...].astype(F32) * widen(cols[:, 2 * heads :], heads, width), state)
     clear_ends(wide, length)
@@ -409,22 +411,21 @@
 
 def late_kernel(
     heads, count,
-    low, x, scal, back, gp, lead, yb, held, series, rim,
+    low, scal, ends, gp, lead, yb, series, rim,
     keep, send, graw, stage,
 ):
-    length, width = x.shape
-    depth = series.shape[1]
-    w_xb = (mm(series[...], gp[...], TN) + mm(rim[...], lead[...], TN)).astype(BF16)
+    depth = rim.shape[1]
     rows = scal[0 : 4 * heads, :]
     step = rows[heads : 2 * heads]
-    mask = head_mask(heads, width)
-    x_back = mm_exact(mask, x[...].astype(F32) * back[0:length, 0:width], NT)[0:heads]
-    ends = jnp.sum(mm_exact(mask, back[0:width, width:] * held[:, width + N :]), axis=1, keepdims=True)[0:heads]
-    grad_log = running_sum_back(yb[0:heads, :] - step * x_back) + ends
+    x_back = ends[0:heads, :]
+    grad_log = running_sum_back(yb[0:heads, :] - step * x_back)
+    grad_log = grad_log + ends[2 * heads : 3 * heads, :]
     grad_step = x_back - rows[3 * heads :] * grad_log
     grad_raw = grad_step * rows[2 * heads : 3 * heads]
     grad_raw = jnp.concatenate([grad_raw, jnp.zeros_like(grad_raw)], axis=0)
     graw[...] = grad_raw
+    series = series()
+    w_xb = (mm(series[...], gp[...], TN) + mm(rim[...], lead[...], TN)).astype(BF16)
     dt = mm(grad_raw, series[...])
     piece = depth // count
     blank = jnp.zeros((LOGS, N), F32)
@@ -507,7 +508,12 @@
 HBM = pl.BlockSpec(memory_space=pltpu.HBM)
 
 
-def run(kernel, name, outs, args, scalars=(), fetched=(), scratch=()):
+def waited(copy, ref):
+    copy.wait()
+    return ref
+
+
+def run(kernel, name, outs, args, scalars=(), fetched=(), lazy=False, scratch=()):
     args = [
         pltpu.with_memory_space_constraint(a, pltpu.HBM) if i in fetched else a
         for i, a in enumerate(args)
@@ -527,8 +533,11 @@
             refs[i] = held[k]
         for copy in copies:
             copy.start()
-        for copy in copies:
-            copy.wait()
+        for copy, i in zip(copies, fetched):
+            if lazy:
+                refs[i] = functools.partial(waited, copy, refs[i])
+            else:
+                copy.wait()
         kernel(*refs)
 
     holders = []
@@ -682,7 +691,7 @@
             [
                 low, total, y, gate, gg, gy, x, bc, scal, sin, cotangent, series, rim, slope,
             ],
-            (0,),
+            (0,), (10, 11),
             scratch=[
                 pltpu.VMEM((length + RIM + 8, N), F32),
                 pltpu.VMEM((count, early, N), BF16),
@@ -698,17 +707,17 @@
                 ((length, 2 * width), F32),
                 ((8, length), F32),
             ],
-            [normed, grad_gate, gp_c, gb, y, gy, x, bc, scal, sin, out_weight, w],
+            [normed, grad_gate, gp_c, gb, y, gy, x, bc, scal, sin, out_weight, w], (), (10, 11),
         )
 
     behind, (firsts, (sg, held, yb)) = passed(msg, True, [early_part, beside_part])
     edge_c, keep, send = firsts[4:]
     early_parts = halved(keep, send, "tm", high, "halve_early")
     early_parts = gathered(early_parts, "tm")
-    back, gp, lead, edge = run(
+    ends, gp, lead, edge = run(
         part(close_kernel, heads), "close",
         [
-            ((length, width + N), F32),
+            ((4 * heads, length), F32),
             ((length, width + N), BF16),
             ((RIM, width + N), BF16),
             ((RIM, 2 * width), BF16),
@@ -720,7 +729,7 @@
     keep, send, graw = run(
         part(late_kernel, heads, count), "late",
         [((hops, late, N), BF16), ((hops, late, N), BF16), ((2 * heads, length), F32)],
-        [low, x, scal, back, gp, lead, yb, held, series, rim], (0,),
+        [low, scal, ends, gp, lead, yb, series, rim], (0,), (6,), True,
         scratch=[pltpu.VMEM((count, late, N), BF16)],
     )
     late_parts = halved(keep, send, "tm", high, "halve_late")

time: 84.9 us -> 82.7 us (0.974)
  local copies, waits for them, and re-layouts: 4.09 us -> 2.93 us
  waiting for transfers between devices: 24.2 us -> 23.3 us
    ppermute x14, waiting for transfers between devices: 15.1 us -> 13.3 us  [swapped(): lax.ppermute(block, axis, [(i, i ^ flip) for i in range(lax.axis_size(axi...]
    unnamed x26 -> x16, local copies, waits for them, and re-layouts: 3.37 us -> 2.21 us
    ppermute x6, waiting for transfers between devices: 9.05 us -> 10.1 us  [shifted(): return lax.ppermute(block, axis, route)]
  transfers between devices with their start and end apart: 20 -> 20, of which waited for: 11 -> 12; matrix products, arithmetic and copies ran while one was open for 0% -> 0% of each run, Pallas kernels for 17% -> 18%
where the time goes in v3:
time: 82.7 us; the launch traced here: 82.3 us
  starting transfers between devices  36.7 us (44%)
  waiting for transfers between devices  23.3 us (28%)
  Pallas kernels  18.5 us (22%)
  local copies, waits for them, and re-layouts  2.93 us (4%)
  between operations  0.89 us (1%)
    pallas_call x20, Pallas kernels, run(): pl.pallas_call(whole if fetched else kernel, name=name, out_shape=[jax.Sh...  18.5 us
    ppermute x14, starting transfers between devices, swapped(): lax.ppermute(block, axis, [(i, i ^ flip) for i in range(lax.axis_size(axi...  18.4 us
    ppermute x6, starting transfers between devices, shifted(): return lax.ppermute(block, axis, route)  18.3 us
    ppermute x14, waiting for transfers between devices, swapped(): lax.ppermute(block, axis, [(i, i ^ flip) for i in range(lax.axis_size(axi...  13.3 us
    ppermute x6, waiting for transfers between devices, shifted(): return lax.ppermute(block, axis, route)  10.1 us
    unnamed x16, local copies, waits for them, and re-layouts  2.21 us
  transfers between devices with their start and end apart: 20, of which 12 were waited for; matrix products, arithmetic and copies ran while one was open for 0% of the time, Pallas kernels for 18%

profile of v3, /device:TPU:0, one launch (start us, length us, event | category | flops | bytes accessed | tf_op | source)
XLA Modules:
  0.0 82.3 jit_solution(3501478964697491816)
XLA Ops:
  1.4 4.9 %collective-permute-start = (bf16[16,512]{1,0:T(8,128)(2,1)S(1)}, bf16[16,512]{1,0:T(8,128)(2,1)S(1)}, u32[]{:S(2)}, u32[]{:S(2)}) collective-permute-start(bf16[16,512]{1,0:T(8,128)(2,1)S(1)} %slice.3), channel_id=1, source_target_pairs={{0,4},{4,8},{8,12},{12,16},{16,20},{20,24},{24,28},{1,5},{5,9},{9,... | collective-permute-start | bytes 49160 | tf_op jit(solution)/shard_map/ppermute | solution.py:564
  6.2 2.3 %project.1 = (bf16[256,256]{1,0:T(8,128)(2,1)S(1)}, bf16[256,512]{1,0:T(8,128)(2,1)S(1)}, f32[32,256]{1,0:T(8,128)S(1)}, bf16[2,512,256]{2,1,0:T(8,128)(2,1)S(1)}) custom-call(bf16[256,512]{1,0:T(8,128)(2,1)} %refs_6_.1, bf16[3,512,256]{2,1,0:T(8,128)(2,1)} %bitcast.9, bf16[4,512]{1,0:T(4,128)(2,1)} %bitcast.12, f32[4]{0:T(128)} %refs_3_.1, f32[4]{0:T(128)} %refs_4_.1, ...), custom_call_target="tpu_custom_call" | custom-call | flops 1000000 | bytes 16384 | tf_op jit(solution)/shard_map/project/pallas_call | solution.py:549
  9.5 1.6 %collective-permute-start.1 = (bf16[272,128]{1,0:T(8,128)(2,1)S(1)}, bf16[272,128]{1,0:T(8,128)(2,1)S(1)}, u32[]{:S(2)}, u32[]{:S(2)}) collective-permute-start(bf16[272,128]{1,0:T(8,128)(2,1)S(1)} %get-tuple-element.92.mine), channel_id=1, source_target_pairs={{0,4},{4,0},{8,12},{12,8},{16,20},{20,16},{24,28},{28,24},{1,5},{5... | collective-permute-start | bytes 208904 | tf_op jit(solution)/shard_map/ppermute | solution.py:568
  12.0 1.9 %collective-permute-done.1.other.partner = bf16[272,128]{1,0:T(8,128)(2,1)S(1)} collective-permute-done((bf16[272,128]{1,0:T(8,128)(2,1)S(1)}, bf16[272,128]{1,0:T(8,128)(2,1)S(1)}, u32[]{:S(2)}, u32[]{:S(2)}) %collective-permute-start.1) | collective-permute-done | bytes 69664 | tf_op jit(solution)/shard_map/ppermute | solution.py:568
  13.9 4.2 %collective-permute-start.2 = (bf16[272,128]{1,0:T(8,128)(2,1)S(1)}, bf16[272,128]{1,0:T(8,128)(2,1)S(1)}, u32[]{:S(2)}, u32[]{:S(2)}) collective-permute-start(bf16[272,128]{1,0:T(8,128)(2,1)S(1)} %pair.2.nearer), channel_id=1, source_target_pairs={{0,8},{4,12},{8,16},{12,20},{16,24},{20,28},{1,9},{5,13},{9,17},{1... | collective-permute-start | bytes 208904 | tf_op jit(solution)/shard_map/ppermute | solution.py:564
  18.2 1.9 %collective-permute-done.2.farther = bf16[272,128]{1,0:T(8,128)(2,1)S(1)} collective-permute-done((bf16[272,128]{1,0:T(8,128)(2,1)S(1)}, bf16[272,128]{1,0:T(8,128)(2,1)S(1)}, u32[]{:S(2)}, u32[]{:S(2)}) %collective-permute-start.2) | collective-permute-done | bytes 69664 | tf_op jit(solution)/shard_map/ppermute | solution.py:564
  20.2 5.3 %collective-permute-start.3 = (bf16[272,128]{1,0:T(8,128)(2,1)S(1)}, bf16[272,128]{1,0:T(8,128)(2,1)S(1)}, u32[]{:S(2)}, u32[]{:S(2)}) collective-permute-start(bf16[272,128]{1,0:T(8,128)(2,1)S(1)} %get-tuple-element.101), channel_id=1, source_target_pairs={{0,16},{4,20},{8,24},{12,28},{1,17},{5,21},{9,25},{13,29},{2,18},{... | collective-permute-start | bytes 208904 | tf_op jit(solution)/shard_map/ppermute | solution.py:564
  25.5 1.9 %collective-permute-done.3.rest_0_ = bf16[272,128]{1,0:T(8,128)(2,1)S(1)} collective-permute-done((bf16[272,128]{1,0:T(8,128)(2,1)S(1)}, bf16[272,128]{1,0:T(8,128)(2,1)S(1)}, u32[]{:S(2)}, u32[]{:S(2)}) %collective-permute-start.3) | collective-permute-done | bytes 69664 | tf_op jit(solution)/shard_map/ppermute | solution.py:564
  29.4 1.5 %collective-permute-start.5 = (f32[8,256]{1,0:T(8,128)S(1)}, f32[8,256]{1,0:T(8,128)S(1)}, u32[]{:S(2)}, u32[]{:S(2)}) collective-permute-start(f32[8,256]{1,0:T(8,128)S(1)} %add.13.sums), channel_id=1, source_target_pairs={{0,2},{1,3},{2,0},{3,1},{4,6},{5,7},{6,4},{7,5},{8,10},{9,11},{10,... | collective-permute-start | bytes 24584 | tf_op jit(solution)/shard_map/ppermute | solution.py:568
  30.9 2.2 %collective-permute-done.5.other = f32[8,256]{1,0:T(8,128)S(1)} collective-permute-done((f32[8,256]{1,0:T(8,128)S(1)}, f32[8,256]{1,0:T(8,128)S(1)}, u32[]{:S(2)}, u32[]{:S(2)}) %collective-permute-start.5) | collective-permute-done | bytes 8224 | tf_op jit(solution)/shard_map/ppermute | solution.py:568
  34.7 3.2 %early.1 = (bf16[256,256]{1,0:T(8,128)(2,1)S(1)}, bf16[256,256]{1,0:T(8,128)(2,1)S(1)}, bf16[256,128]{1,0:T(8,128)(2,1)S(1)}, f32[256,128]{1,0:T(8,128)S(1)}, bf...) custom-call(s32[1]{0:T(128)} %bitcast.1.low.refs_0_, ...), custom_call_target="tpu_custom_call" | custom-call | flops 1000000 | bytes 16384 | tf_op jit(solution)/shard_map/early/pallas_call | solution.py:549
  40.5 2.9 %beside.1 = (bf16[256,1024]{1,0:T(8,128)(2,1)S(1)}, f32[256,512]{1,0:T(8,128)S(1)}, f32[8,256]{1,0:T(8,128)S(1)}) custom-call(bf16[256,256]{1,0:T(8,128)(2,1)S(1)} %get-tuple-element.118.refs_0_, bf16[256,256]{1,0:T(8,128)(2,1)S(1)} %get-tuple-element.119.refs_1_, bf16[256,128]{1,0:T(8,128)(2,1)S(1)} %get-tuple-element.120.refs_2_, ...), custom_call_target="tpu_custom_call" | custom-call | flops 1000000 | bytes 16384 | tf_op jit(solution)/shard_map/beside/pallas_call | solution.py:549
  43.4 2.1 %collective-permute-done.7.farther = bf16[272,128]{1,0:T(8,128)(2,1)S(1)} collective-permute-done((bf16[272,128]{1,0:T(8,128)(2,1)S(1)}, bf16[272,128]{1,0:T(8,128)(2,1)S(1)}, u32[]{:S(2)}, u32[]{:S(2)}) %collective-permute-start.7) | collective-permute-done | bytes 69664 | tf_op jit(solution)/shard_map/ppermute | solution.py:564
  48.3 2.0 %collective-permute-start.15 = (bf16[320,128]{1,0:T(8,128)(2,1)}, bf16[320,128]{1,0:T(8,128)(2,1)S(1)}, u32[]{:S(2)}, u32[]{:S(2)}) collective-permute-start(bf16[320,128]{1,0:T(8,128)(2,1)} %get-tuple-element.146), channel_id=1, source_target_pairs={{0,8},{4,12},{8,0},{12,4},{16,24},{20,28},{24,16},{28,20},{1,9},{5... | collective-permute-start | bytes 245768 | tf_op jit(solution)/shard_map/ppermute | solution.py:568
  50.3 3.5 %collective-permute-start.16 = (bf16[320,128]{1,0:T(8,128)(2,1)}, bf16[320,128]{1,0:T(8,128)(2,1)S(1)}, u32[]{:S(2)}, u32[]{:S(2)}) collective-permute-start(bf16[320,128]{1,0:T(8,128)(2,1)} %get-tuple-element.147), channel_id=1, source_target_pairs={{0,16},{4,20},{8,24},{12,28},{16,0},{20,4},{24,8},{28,12},{1,17},{... | collective-permute-start | bytes 245768 | tf_op jit(solution)/shard_map/ppermute | solution.py:568
  56.5 1.7 %close.1 = (f32[16,256]{1,0:T(8,128)S(1)}, bf16[256,384]{1,0:T(8,128)(2,1)S(1)}, bf16[16,384]{1,0:T(8,128)(2,1)S(1)}, bf16[16,512]{1,0:T(8,128)(2,1)}) custom-call(s32[1]{0:T(128)} %bitcast.1.low.refs_0_, bf16[256,256]{1,0:T(8,128)(2,1)S(1)} %get-tuple-element.90.x.refs_6_, bf16[256,256]{1,0:T(8,128)(2,1)S(1)} %get-tuple-element.91.bc.refs_7_, ...), custom_call_target="tpu_custom_call" | custom-call | flops 1000000 | bytes 16384 | tf_op jit(solution)/shard_map/close/pallas_call | solution.py:549
  59.4 1.5 %late.1 = (bf16[4,208,128]{2,1,0:T(8,128)(2,1)S(1)}, bf16[4,208,128]{2,1,0:T(8,128)(2,1)S(1)}, f32[8,256]{1,0:T(8,128)S(1)}) custom-call(s32[1]{0:T(128)} %bitcast.1.low.refs_0_, f32[32,256]{1,0:T(8,128)S(1)} %get-tuple-element.87.scal.refs_8_.refs_1_, f32[16,256]{1,0:T(8,128)S(1)} %get-tuple-element.130.refs_2_, ...), custom_call_target="tpu_custom_call" | custom-call | flops 1000000 | bytes 16384 | tf_op jit(solution)/shard_map/late/pallas_call | solution.py:549
  61.0 3.0 %collective-permute-done.13.edge = bf16[16,512]{1,0:T(8,128)(2,1)S(1)} collective-permute-done((bf16[16,512]{1,0:T(8,128)(2,1)}, bf16[16,512]{1,0:T(8,128)(2,1)S(1)}, u32[]{:S(2)}, u32[]{:S(2)}) %collective-permute-start.13) | collective-permute-done | bytes 16416 | tf_op jit(solution)/shard_map/ppermute | solution.py:564
  64.6 1.9 %collective-permute-start.9 = (bf16[4,208,128]{2,1,0:T(8,128)(2,1)S(1)}, bf16[4,208,128]{2,1,0:T(8,128)(2,1)S(1)}, u32[]{:S(2)}, u32[]{:S(2)}) collective-permute-start(bf16[4,208,128]{2,1,0:T(8,128)(2,1)S(1)} %get-tuple-element.135), channel_id=1, source_target_pairs={{0,4},{4,0},{8,12},{12,8},{16,20},{20,16},{24,28},{28,24},{1,5},{5... | collective-permute-start | bytes 638984 | tf_op jit(solution)/shard_map/ppermute | solution.py:568
  66.5 1.6 %collective-permute-start.19 = (bf16[64,1024]{1,0:T(8,128)(2,1)S(1)}, bf16[64,1024]{1,0:T(8,128)(2,1)S(1)}, u32[]{:S(2)}, u32[]{:S(2)}) collective-permute-start(bf16[64,1024]{1,0:T(8,128)(2,1)S(1)} %get-tuple-element.153), channel_id=1, source_target_pairs={{0,2},{1,3},{2,0},{3,1},{4,6},{5,7},{6,4},{7,5},{8,10},{9,11},{10,... | collective-permute-start | bytes 393224 | tf_op jit(solution)/shard_map/ppermute | solution.py:568
  68.1 4.2 %collective-permute-done.9.other = bf16[4,208,128]{2,1,0:T(8,128)(2,1)S(1)} collective-permute-done((bf16[4,208,128]{2,1,0:T(8,128)(2,1)S(1)}, bf16[4,208,128]{2,1,0:T(8,128)(2,1)S(1)}, u32[]{:S(2)}, u32[]{:S(2)}) %collective-permute-start.9) | collective-permute-done | bytes 213024 | tf_op jit(solution)/shard_map/ppermute | solution.py:568
  73.0 2.6 %collective-permute-start.11 = (bf16[208,128]{1,0:T(8,128)(2,1)S(1)}, bf16[208,128]{1,0:T(8,128)(2,1)S(1)}, u32[]{:S(2)}, u32[]{:S(2)}) collective-permute-start(bf16[208,128]{1,0:T(8,128)(2,1)S(1)} %get-tuple-element.138), channel_id=1, source_target_pairs={{0,16},{4,20},{8,24},{12,28},{16,0},{20,4},{24,8},{28,12},{1,17},{... | collective-permute-start | bytes 159752 | tf_op jit(solution)/shard_map/ppermute | solution.py:568
  78.2 1.7 %collective-permute-done.11.refs_2_ = bf16[208,128]{1,0:T(8,128)(2,1)S(1)} collective-permute-done((bf16[208,128]{1,0:T(8,128)(2,1)S(1)}, bf16[208,128]{1,0:T(8,128)(2,1)S(1)}, u32[]{:S(2)}, u32[]{:S(2)}) %collective-permute-start.11) | collective-permute-done | bytes 53280 | tf_op jit(solution)/shard_map/ppermute | solution.py:568
  79.8 1.7 %collective-permute-done.12.refs_3_ = bf16[208,128]{1,0:T(8,128)(2,1)S(1)} collective-permute-done((bf16[208,128]{1,0:T(8,128)(2,1)S(1)}, bf16[208,128]{1,0:T(8,128)(2,1)S(1)}, u32[]{:S(2)}, u32[]{:S(2)}) %collective-permute-start.12) | collective-permute-done | bytes 53280 | tf_op jit(solution)/shard_map/ppermute | solution.py:568
  (54 shorter events, 20.1 us)
Async XLA Ops:
  1.4 7.2 %collective-permute-start = (bf16[16,512]{1,0:T(8,128)(2,1)S(1)}, bf16[16,512]{1,0:T(8,128)(2,1)S(1)}, u32[]{:S(2)}, u32[]{:S(2)}) collective-permute-start(bf16[16,512]{1,0:T(8,128)(2,1)S(1)} %slice.3), channel_id=1, source_target_pairs={{0,4},{4,8},{8,12},{12,16},{16,20},{20,24},{24,28},{1,5},{5,9},{9,... | collective-permute-start | bytes 49160 | tf_op jit(solution)/shard_map/ppermute | solution.py:564
  8.5 2.6 %copy-start.1 = (bf16[256,512]{1,0:T(8,128)(2,1)S(1)}, bf16[256,512]{1,0:T(8,128)(2,1)}, u32[]{:S(2)}) copy-start(bf16[256,512]{1,0:T(8,128)(2,1)} %refs_10_.2) | copy-start | bytes 786436
  9.5 4.4 %collective-permute-start.1 = (bf16[272,128]{1,0:T(8,128)(2,1)S(1)}, bf16[272,128]{1,0:T(8,128)(2,1)S(1)}, u32[]{:S(2)}, u32[]{:S(2)}) collective-permute-start(bf16[272,128]{1,0:T(8,128)(2,1)S(1)} %get-tuple-element.92.mine), channel_id=1, source_target_pairs={{0,4},{4,0},{8,12},{12,8},{16,20},{20,16},{24,28},{28,24},{1,5},{5... | collective-permute-start | bytes 208904 | tf_op jit(solution)/shard_map/ppermute | solution.py:568
  13.9 6.2 %collective-permute-start.2 = (bf16[272,128]{1,0:T(8,128)(2,1)S(1)}, bf16[272,128]{1,0:T(8,128)(2,1)S(1)}, u32[]{:S(2)}, u32[]{:S(2)}) collective-permute-start(bf16[272,128]{1,0:T(8,128)(2,1)S(1)} %pair.2.nearer), channel_id=1, source_target_pairs={{0,8},{4,12},{8,16},{12,20},{16,24},{20,28},{1,9},{5,13},{9,17},{1... | collective-permute-start | bytes 208904 | tf_op jit(solution)/shard_map/ppermute | solution.py:564
  20.2 7.2 %collective-permute-start.3 = (bf16[272,128]{1,0:T(8,128)(2,1)S(1)}, bf16[272,128]{1,0:T(8,128)(2,1)S(1)}, u32[]{:S(2)}, u32[]{:S(2)}) collective-permute-start(bf16[272,128]{1,0:T(8,128)(2,1)S(1)} %get-tuple-element.101), channel_id=1, source_target_pairs={{0,16},{4,20},{8,24},{12,28},{1,17},{5,21},{9,25},{13,29},{2,18},{... | collective-permute-start | bytes 208904 | tf_op jit(solution)/shard_map/ppermute | solution.py:564
  28.2 1.2 %collective-permute-start.4 = (f32[8,256]{1,0:T(8,128)S(1)}, f32[8,256]{1,0:T(8,128)S(1)}, u32[]{:S(2)}, u32[]{:S(2)}) collective-permute-start(f32[8,256]{1,0:T(8,128)S(1)} %get-tuple-element.103), channel_id=1, source_target_pairs={{0,1},{1,0},{2,3},{3,2},{4,5},{5,4},{6,7},{7,6},{8,9},{9,8},{10,11... | collective-permute-start | bytes 24584 | tf_op jit(solution)/shard_map/ppermute | solution.py:568
  29.4 3.7 %collective-permute-start.5 = (f32[8,256]{1,0:T(8,128)S(1)}, f32[8,256]{1,0:T(8,128)S(1)}, u32[]{:S(2)}, u32[]{:S(2)}) collective-permute-start(f32[8,256]{1,0:T(8,128)S(1)} %add.13.sums), channel_id=1, source_target_pairs={{0,2},{1,3},{2,0},{3,1},{4,6},{5,7},{6,4},{7,5},{8,10},{9,11},{10,... | collective-permute-start | bytes 24584 | tf_op jit(solution)/shard_map/ppermute | solution.py:568
  33.8 4.4 %collective-permute-start.6 = (bf16[272,128]{1,0:T(8,128)(2,1)S(1)}, bf16[272,128]{1,0:T(8,128)(2,1)S(1)}, u32[]{:S(2)}, u32[]{:S(2)}) collective-permute-start(bf16[272,128]{1,0:T(8,128)(2,1)S(1)} %get-tuple-element.106.mine), channel_id=1, source_target_pairs={{0,4},{4,0},{8,12},{12,8},{16,20},{20,16},{24,28},{28,24},{1,5},{5... | collective-permute-start | bytes 208904 | tf_op jit(solution)/shard_map/ppermute | solution.py:568
  38.2 8.7 %collective-permute-start.14 = (bf16[4,320,128]{2,1,0:T(8,128)(2,1)}, bf16[4,320,128]{2,1,0:T(8,128)(2,1)S(1)}, u32[]{:S(2)}, u32[]{:S(2)}) collective-permute-start(bf16[4,320,128]{2,1,0:T(8,128)(2,1)} %get-tuple-element.144), channel_id=1, source_target_pairs={{0,4},{4,0},{8,12},{12,8},{16,20},{20,16},{24,28},{28,24},{1,5},{5... | collective-permute-start | bytes 983048 | tf_op jit(solution)/shard_map/ppermute | solution.py:568
  39.2 6.3 %collective-permute-start.7 = (bf16[272,128]{1,0:T(8,128)(2,1)S(1)}, bf16[272,128]{1,0:T(8,128)(2,1)S(1)}, u32[]{:S(2)}, u32[]{:S(2)}) collective-permute-start(bf16[272,128]{1,0:T(8,128)(2,1)S(1)} %pair.3.nearer), channel_id=1, source_target_pairs={{8,0},{12,4},{16,8},{20,12},{24,16},{28,20},{9,1},{13,5},{17,9},{2... | collective-permute-start | bytes 208904 | tf_op jit(solution)/shard_map/ppermute | solution.py:564
  45.6 9.4 %collective-permute-start.8 = (bf16[272,128]{1,0:T(8,128)(2,1)S(1)}, bf16[272,128]{1,0:T(8,128)(2,1)S(1)}, u32[]{:S(2)}, u32[]{:S(2)}) collective-permute-start(bf16[272,128]{1,0:T(8,128)(2,1)S(1)} %get-tuple-element.128), channel_id=1, source_target_pairs={{16,0},{20,4},{24,8},{28,12},{17,1},{21,5},{25,9},{29,13},{18,2},{... | collective-permute-start | bytes 208904 | tf_op jit(solution)/shard_map/ppermute | solution.py:564
  48.3 15.7 %collective-permute-start.15 = (bf16[320,128]{1,0:T(8,128)(2,1)}, bf16[320,128]{1,0:T(8,128)(2,1)S(1)}, u32[]{:S(2)}, u32[]{:S(2)}) collective-permute-start(bf16[320,128]{1,0:T(8,128)(2,1)} %get-tuple-element.146), channel_id=1, source_target_pairs={{0,8},{4,12},{8,0},{12,4},{16,24},{20,28},{24,16},{28,20},{1,9},{5... | collective-permute-start | bytes 245768 | tf_op jit(solution)/shard_map/ppermute | solution.py:568
  50.3 13.7 %collective-permute-start.16 = (bf16[320,128]{1,0:T(8,128)(2,1)}, bf16[320,128]{1,0:T(8,128)(2,1)S(1)}, u32[]{:S(2)}, u32[]{:S(2)}) collective-permute-start(bf16[320,128]{1,0:T(8,128)(2,1)} %get-tuple-element.147), channel_id=1, source_target_pairs={{0,16},{4,20},{8,24},{12,28},{16,0},{20,4},{24,8},{28,12},{1,17},{... | collective-permute-start | bytes 245768 | tf_op jit(solution)/shard_map/ppermute | solution.py:568
  53.8 10.2 %collective-permute-start.17 = (bf16[320,128]{1,0:T(8,128)(2,1)}, bf16[320,128]{1,0:T(8,128)(2,1)S(1)}, u32[]{:S(2)}, u32[]{:S(2)}) collective-permute-start(bf16[320,128]{1,0:T(8,128)(2,1)} %get-tuple-element.148), channel_id=1, source_target_pairs={{0,24},{4,28},{8,16},{12,20},{16,8},{20,12},{24,0},{28,4},{1,25},{... | collective-permute-start | bytes 245768 | tf_op jit(solution)/shard_map/ppermute | solution.py:568
  56.5 7.5 %copy-start = (bf16[512,3,256]{2,0,1:T(8,128)(2,1)S(1)}, bf16[512,3,256]{2,0,1:T(8,128)(2,1)}, u32[]{:S(2)}) copy-start(bf16[512,3,256]{2,0,1:T(8,128)(2,1)} %param.12) | copy-start | bytes 2359300
  58.1 5.8 %collective-permute-start.13 = (bf16[16,512]{1,0:T(8,128)(2,1)}, bf16[16,512]{1,0:T(8,128)(2,1)S(1)}, u32[]{:S(2)}, u32[]{:S(2)}) collective-permute-start(bf16[16,512]{1,0:T(8,128)(2,1)} %get-tuple-element.142), channel_id=1, source_target_pairs={{4,0},{8,4},{12,8},{16,12},{20,16},{24,20},{28,24},{5,1},{9,5},{13... | collective-permute-start | bytes 49160 | tf_op jit(solution)/shard_map/ppermute | solution.py:564
  61.0 3.0 %copy-start.7 = (bf16[512,4]{0,1:T(4,128)(2,1)S(1)}, bf16[512,4]{0,1:T(4,128)(2,1)}, u32[]{:S(2)}) copy-start(bf16[512,4]{0,1:T(4,128)(2,1)} %param.13) | copy-start | bytes 12292
  64.5 2.0 %collective-permute-start.18 = (bf16[2,64,1024]{2,1,0:T(8,128)(2,1)S(1)}, bf16[2,64,1024]{2,1,0:T(8,128)(2,1)S(1)}, u32[]{:S(2)}, u32[]{:S(2)}) collective-permute-start(bf16[2,64,1024]{2,1,0:T(8,128)(2,1)S(1)} %get-tuple-element.151), channel_id=1, source_target_pairs={{0,1},{1,0},{2,3},{3,2},{4,5},{5,4},{6,7},{7,6},{8,9},{9,8},{10,11... | collective-permute-start | bytes 786440 | tf_op jit(solution)/shard_map/ppermute | solution.py:568
  64.6 7.7 %collective-permute-start.9 = (bf16[4,208,128]{2,1,0:T(8,128)(2,1)S(1)}, bf16[4,208,128]{2,1,0:T(8,128)(2,1)S(1)}, u32[]{:S(2)}, u32[]{:S(2)}) collective-permute-start(bf16[4,208,128]{2,1,0:T(8,128)(2,1)S(1)} %get-tuple-element.135), channel_id=1, source_target_pairs={{0,4},{4,0},{8,12},{12,8},{16,20},{20,16},{24,28},{28,24},{1,5},{5... | collective-permute-start | bytes 638984 | tf_op jit(solution)/shard_map/ppermute | solution.py:568
  66.5 10.9 %collective-permute-start.19 = (bf16[64,1024]{1,0:T(8,128)(2,1)S(1)}, bf16[64,1024]{1,0:T(8,128)(2,1)S(1)}, u32[]{:S(2)}, u32[]{:S(2)}) collective-permute-start(bf16[64,1024]{1,0:T(8,128)(2,1)S(1)} %get-tuple-element.153), channel_id=1, source_target_pairs={{0,2},{1,3},{2,0},{3,1},{4,6},{5,7},{6,4},{7,5},{8,10},{9,11},{10,... | collective-permute-start | bytes 393224 | tf_op jit(solution)/shard_map/ppermute | solution.py:568
  72.3 4.5 %copy-start.4 = (f32[320,128]{1,0:T(8,128)S(1)}, f32[320,128]{1,0:T(8,128)}, u32[]{:S(2)}) copy-start(f32[320,128]{1,0:T(8,128)} %copy-done.3) | copy-start | bytes 491524
  72.4 5.8 %collective-permute-start.10 = (bf16[208,128]{1,0:T(8,128)(2,1)S(1)}, bf16[208,128]{1,0:T(8,128)(2,1)S(1)}, u32[]{:S(2)}, u32[]{:S(2)}) collective-permute-start(bf16[208,128]{1,0:T(8,128)(2,1)S(1)} %get-tuple-element.137), channel_id=1, source_target_pairs={{0,8},{4,12},{8,0},{12,4},{16,24},{20,28},{24,16},{28,20},{1,9},{5... | collective-permute-start | bytes 159752 | tf_op jit(solution)/shard_map/ppermute | solution.py:568
  73.0 6.8 %collective-permute-start.11 = (bf16[208,128]{1,0:T(8,128)(2,1)S(1)}, bf16[208,128]{1,0:T(8,128)(2,1)S(1)}, u32[]{:S(2)}, u32[]{:S(2)}) collective-permute-start(bf16[208,128]{1,0:T(8,128)(2,1)S(1)} %get-tuple-element.138), channel_id=1, source_target_pairs={{0,16},{4,20},{8,24},{12,28},{16,0},{20,4},{24,8},{28,12},{1,17},{... | collective-permute-start | bytes 159752 | tf_op jit(solution)/shard_map/ppermute | solution.py:568
  75.6 5.9 %collective-permute-start.12 = (bf16[208,128]{1,0:T(8,128)(2,1)S(1)}, bf16[208,128]{1,0:T(8,128)(2,1)S(1)}, u32[]{:S(2)}, u32[]{:S(2)}) collective-permute-start(bf16[208,128]{1,0:T(8,128)(2,1)S(1)} %get-tuple-element.139), channel_id=1, source_target_pairs={{0,24},{4,28},{8,16},{12,20},{16,8},{20,12},{24,0},{28,4},{1,25},{... | collective-permute-start | bytes 159752 | tf_op jit(solution)/shard_map/ppermute | solution.py:568
  (4 other events, 4.7 us)

commit v4 on v3

--- a/solution.py
+++ b/solution.py
@@ -447,7 +447,8 @@
         part[...] = (keep[at].astype(F32) + other[at].astype(F32)).astype(BF16)
 
 
-def rows_kernel(low, sg, gp, graw, edge, w, dtw, keep, send, stage):
+def rows_kernel(spot, sg, gp, graw, edge, w, dtw, *rest):
+    *parts, stage = rest
     length, depth = sg.shape[0], sg.shape[1] // 2
     width = w.shape[2]
     heads = dtw.shape[0]
@@ -457,28 +458,18 @@
     stage[:, 0:depth] = sg[:, 0:depth]
     stage[:, depth:] = total.astype(BF16)
     stage[length - RIM :, depth:] = (total[length - RIM :, :] + late).astype(BF16)
-    piece = keep.shape[1]
-    for at in range(send.shape[0]):
-        start = pl.multiple_of((2 * at + low[0]) * piece, piece)
-        keep[at] = stage[pl.ds(start, piece), :]
-        start = pl.multiple_of((2 * at + 1 - low[0]) * piece, piece)
-        send[at] = stage[pl.ds(start, piece), :]
+    piece = parts[0].shape[0]
+    for k, part in enumerate(parts):
+        start = pl.multiple_of((spot[0] ^ k) * piece, piece)
+        part[...] = stage[pl.ds(start, piece), :]
 
 
 def sum_of(parts):
     rows = parts[-1].shape[0]
-    total = parts[0][0:rows, :]
+    total = parts[0][0:rows, :].astype(F32)
     for part in parts[1:]:
         total = total + part[...].astype(F32)
     return total
-
-
-def outputs_kernel(*refs):
-    *parts, layer, grad = refs
-    depth = layer.shape[1]
-    total = sum_of(parts)
-    layer[...] = total[:, 0:depth].astype(BF16)
-    grad[...] = total[:, depth:]
 
 
 def early_sum_kernel(*refs):
@@ -490,8 +481,13 @@
     others[0 : 3 * piece, :] = total[2 * piece :, :]
 
 
-def total_kernel(early, *refs):
-    *parts, w_in, w_dt = refs
+def final_kernel(hops, early, *refs):
+    *blocks, layer, grad, w_in, w_dt = refs
+    parts, blocks = blocks[:hops], blocks[hops:]
+    depth = layer.shape[1]
+    total = sum_of(blocks)
+    layer[...] = total[:, 0:depth].astype(BF16)
+    grad[...] = total[:, depth:]
     piece = w_in.shape[1]
     late = sum_of(parts)
     for q in range(2):
@@ -597,7 +593,6 @@
     position = lax.axis_index("tm").astype(jnp.int32)
     spot = lax.axis_index("head").astype(jnp.int32)
     low, high = (position % 2).reshape(1), (position // 2).reshape(1)
-    low_spot, high_spot = (spot % 2).reshape(1), (spot // 2).reshape(1)
     rim = shifted(series[length - RIM :], "tm", 1)
     state_msg = ((width + LOGS, N), BF16)
 
@@ -735,25 +730,26 @@
     late_parts = halved(keep, send, "tm", high, "halve_late")
     late_parts = gathered(late_parts, "tm")
     rows = length // parts
-    edge, early_parts = lax.optimization_barrier((edge, early_parts))
     w_out_grad, early_total = run(
         early_sum_kernel, "early_sum",
         [((piece, width), F32), ((3 * piece, N), F32)], early_parts,
     )
-    keep, send = run(
+    blocks = run(
         rows_kernel, "rows",
-        [((parts // 2, rows, 2 * depth), BF16), ((parts // 2, rows, 2 * depth), BF16)],
-        [low_spot, sg, gp, graw, edge, w, dtw], (0,),
+        [((rows, 2 * depth), BF16)] * parts,
+        [spot.reshape(1), sg, gp, graw, edge, w, dtw], (0,),
         scratch=[pltpu.VMEM((length, 2 * depth), BF16)],
     )
-    both = gathered(halved(keep, send, "head", high_spot, "halve_rows"), "head")
-    layer_out, series_grad = run(
-        outputs_kernel, "outputs", [((rows, depth), BF16), ((rows, depth), F32)], both,
-    )
-    late_parts, layer_out = lax.optimization_barrier((late_parts, layer_out))
-    w_in_grad, w_dt_grad = run(
-        total_kernel, "total",
-        [((3, piece, width), F32), ((heads, piece), F32)], [early_total] + late_parts,
+    blocks = [blocks[0]] + [swapped(blocks[k], "head", k) for k in range(1, parts)]
+    layer_out, series_grad, w_in_grad, w_dt_grad = run(
+        part(final_kernel, hops), "final",
+        [
+            ((rows, depth), BF16),
+            ((rows, depth), F32),
+            ((3, piece, width), F32),
+            ((heads, piece), F32),
+        ],
+        [early_total] + late_parts + blocks,
     )
     return (layer_out, series_grad, w_in_grad.transpose(1, 0, 2), w_dt_grad.T, w_out_grad)
 

time: 82.7 us -> 81.7 us (0.988)
  waiting for transfers between devices: 23.3 us -> 29.8 us
  starting transfers between devices: 36.7 us -> 32.8 us
  Pallas kernels: 18.5 us -> 16.5 us
  local copies, waits for them, and re-layouts: 2.93 us -> 1.4 us
    ppermute x6, waiting for transfers between devices: 10.1 us -> 15.3 us  [shifted(): return lax.ppermute(block, axis, route)]
    ppermute x14 -> x15, starting transfers between devices: 18.4 us -> 14.4 us  [swapped(): lax.ppermute(block, axis, [(i, i ^ flip) for i in range(lax.axis_size(axi...]
    pallas_call x20 -> x18, Pallas kernels: 18.5 us -> 16.5 us  [run(): pl.pallas_call(whole if fetched else kernel, name=name, out_shape=[jax.Sh...]
    unnamed x16 -> x12, local copies, waits for them, and re-layouts: 2.21 us -> 0.68 us
    ppermute x14 -> x15, waiting for transfers between devices: 13.3 us -> 14.5 us  [swapped(): lax.ppermute(block, axis, [(i, i ^ flip) for i in range(lax.axis_size(axi...]
  transfers between devices with their start and end apart: 20 -> 21, of which waited for: 12 -> 11; matrix products, arithmetic and copies ran while one was open for 0% -> 0% of each run, Pallas kernels for 18% -> 16%
where the time goes in v4:
time: 81.7 us; the launch traced here: 81.3 us
  starting transfers between devices  32.8 us (40%)
  waiting for transfers between devices  29.8 us (36%)
  Pallas kernels  16.5 us (20%)
  local copies, waits for them, and re-layouts  1.4 us (2%)
  between operations  0.84 us (1%)
    ppermute x6, starting transfers between devices, shifted(): return lax.ppermute(block, axis, route)  18.4 us
    pallas_call x18, Pallas kernels, run(): pl.pallas_call(whole if fetched else kernel, name=name, out_shape=[jax.Sh...  16.5 us
    ppermute x6, waiting for transfers between devices, shifted(): return lax.ppermute(block, axis, route)  15.3 us
    ppermute x15, waiting for transfers between devices, swapped(): lax.ppermute(block, axis, [(i, i ^ flip) for i in range(lax.axis_size(axi...  14.5 us
    ppermute x15, starting transfers between devices, swapped(): lax.ppermute(block, axis, [(i, i ^ flip) for i in range(lax.axis_size(axi...  14.4 us
  transfers between devices with their start and end apart: 21, of which 11 were waited for; matrix products, arithmetic and copies ran while one was open for 0% of the time, Pallas kernels for 16%

profile of v4, /device:TPU:0, one launch (start us, length us, event | category | flops | bytes accessed | tf_op | source)
XLA Modules:
  0.0 81.3 jit_solution(1510853886230706208)
XLA Ops:
  1.4 4.9 %collective-permute-start = (bf16[16,512]{1,0:T(8,128)(2,1)S(1)}, bf16[16,512]{1,0:T(8,128)(2,1)S(1)}, u32[]{:S(2)}, u32[]{:S(2)}) collective-permute-start(bf16[16,512]{1,0:T(8,128)(2,1)S(1)} %slice.3), channel_id=1, source_target_pairs={{0,4},{4,8},{8,12},{12,16},{16,20},{20,24},{24,28},{1,5},{5,9},{9,... | collective-permute-start | bytes 49160 | tf_op jit(solution)/shard_map/ppermute | solution.py:560
  6.2 2.3 %project.1 = (bf16[256,256]{1,0:T(8,128)(2,1)S(1)}, bf16[256,512]{1,0:T(8,128)(2,1)S(1)}, f32[32,256]{1,0:T(8,128)S(1)}, bf16[2,512,256]{2,1,0:T(8,128)(2,1)S(1)}) custom-call(bf16[256,512]{1,0:T(8,128)(2,1)} %refs_6_.1, bf16[3,512,256]{2,1,0:T(8,128)(2,1)} %bitcast.8, bf16[4,512]{1,0:T(4,128)(2,1)} %bitcast.11, f32[4]{0:T(128)} %refs_3_.1, f32[4]{0:T(128)} %refs_4_.1, ...), custom_call_target="tpu_custom_call" | custom-call | flops 1000000 | bytes 16384 | tf_op jit(solution)/shard_map/project/pallas_call | solution.py:545
  9.5 1.6 %collective-permute-start.1 = (bf16[272,128]{1,0:T(8,128)(2,1)S(1)}, bf16[272,128]{1,0:T(8,128)(2,1)S(1)}, u32[]{:S(2)}, u32[]{:S(2)}) collective-permute-start(bf16[272,128]{1,0:T(8,128)(2,1)S(1)} %get-tuple-element.80.mine), channel_id=1, source_target_pairs={{0,4},{4,0},{8,12},{12,8},{16,20},{20,16},{24,28},{28,24},{1,5},{5... | collective-permute-start | bytes 208904 | tf_op jit(solution)/shard_map/ppermute | solution.py:564
  12.0 1.9 %collective-permute-done.1.other.partner = bf16[272,128]{1,0:T(8,128)(2,1)S(1)} collective-permute-done((bf16[272,128]{1,0:T(8,128)(2,1)S(1)}, bf16[272,128]{1,0:T(8,128)(2,1)S(1)}, u32[]{:S(2)}, u32[]{:S(2)}) %collective-permute-start.1) | collective-permute-done | bytes 69664 | tf_op jit(solution)/shard_map/ppermute | solution.py:564
  13.9 4.2 %collective-permute-start.2 = (bf16[272,128]{1,0:T(8,128)(2,1)S(1)}, bf16[272,128]{1,0:T(8,128)(2,1)S(1)}, u32[]{:S(2)}, u32[]{:S(2)}) collective-permute-start(bf16[272,128]{1,0:T(8,128)(2,1)S(1)} %pair.2.nearer), channel_id=1, source_target_pairs={{0,8},{4,12},{8,16},{12,20},{16,24},{20,28},{1,9},{5,13},{9,17},{1... | collective-permute-start | bytes 208904 | tf_op jit(solution)/shard_map/ppermute | solution.py:560
  18.2 1.9 %collective-permute-done.2.farther = bf16[272,128]{1,0:T(8,128)(2,1)S(1)} collective-permute-done((bf16[272,128]{1,0:T(8,128)(2,1)S(1)}, bf16[272,128]{1,0:T(8,128)(2,1)S(1)}, u32[]{:S(2)}, u32[]{:S(2)}) %collective-permute-start.2) | collective-permute-done | bytes 69664 | tf_op jit(solution)/shard_map/ppermute | solution.py:560
  20.2 5.3 %collective-permute-start.3 = (bf16[272,128]{1,0:T(8,128)(2,1)S(1)}, bf16[272,128]{1,0:T(8,128)(2,1)S(1)}, u32[]{:S(2)}, u32[]{:S(2)}) collective-permute-start(bf16[272,128]{1,0:T(8,128)(2,1)S(1)} %get-tuple-element.91), channel_id=1, source_target_pairs={{0,16},{4,20},{8,24},{12,28},{1,17},{5,21},{9,25},{13,29},{2,18},{... | collective-permute-start | bytes 208904 | tf_op jit(solution)/shard_map/ppermute | solution.py:560
  25.5 1.9 %collective-permute-done.3.rest_0_ = bf16[272,128]{1,0:T(8,128)(2,1)S(1)} collective-permute-done((bf16[272,128]{1,0:T(8,128)(2,1)S(1)}, bf16[272,128]{1,0:T(8,128)(2,1)S(1)}, u32[]{:S(2)}, u32[]{:S(2)}) %collective-permute-start.3) | collective-permute-done | bytes 69664 | tf_op jit(solution)/shard_map/ppermute | solution.py:560
  29.4 1.5 %collective-permute-start.5 = (f32[8,256]{1,0:T(8,128)S(1)}, f32[8,256]{1,0:T(8,128)S(1)}, u32[]{:S(2)}, u32[]{:S(2)}) collective-permute-start(f32[8,256]{1,0:T(8,128)S(1)} %add.9.sums), channel_id=1, source_target_pairs={{0,2},{1,3},{2,0},{3,1},{4,6},{5,7},{6,4},{7,5},{8,10},{9,11},{10,... | collective-permute-start | bytes 24584 | tf_op jit(solution)/shard_map/ppermute | solution.py:564
  30.9 2.2 %collective-permute-done.5.other = f32[8,256]{1,0:T(8,128)S(1)} collective-permute-done((f32[8,256]{1,0:T(8,128)S(1)}, f32[8,256]{1,0:T(8,128)S(1)}, u32[]{:S(2)}, u32[]{:S(2)}) %collective-permute-start.5) | collective-permute-done | bytes 8224 | tf_op jit(solution)/shard_map/ppermute | solution.py:564
  34.7 2.5 %early.1 = (bf16[256,256]{1,0:T(8,128)(2,1)S(1)}, bf16[256,256]{1,0:T(8,128)(2,1)S(1)}, bf16[256,128]{1,0:T(8,128)(2,1)S(1)}, f32[256,128]{1,0:T(8,128)S(1)}, bf...) custom-call(s32[1]{0:T(128)} %bitcast.1.low.refs_0_, ...), custom_call_target="tpu_custom_call" | custom-call | flops 1000000 | bytes 16384 | tf_op jit(solution)/shard_map/early/pallas_call | solution.py:545
  38.2 1.3 %collective-permute-start.11 = (bf16[272,128]{1,0:T(8,128)(2,1)S(1)}, bf16[272,128]{1,0:T(8,128)(2,1)S(1)}, u32[]{:S(2)}, u32[]{:S(2)}) collective-permute-start(bf16[272,128]{1,0:T(8,128)(2,1)S(1)} %pair.3.nearer), channel_id=1, source_target_pairs={{8,0},{12,4},{16,8},{20,12},{24,16},{28,20},{9,1},{13,5},{17,9},{2... | collective-permute-start | bytes 208904 | tf_op jit(solution)/shard_map/ppermute | solution.py:560
  40.4 2.9 %beside.1 = (bf16[256,1024]{1,0:T(8,128)(2,1)S(1)}, f32[256,512]{1,0:T(8,128)S(1)}, f32[8,256]{1,0:T(8,128)S(1)}) custom-call(bf16[256,256]{1,0:T(8,128)(2,1)S(1)} %get-tuple-element.115.refs_0_, bf16[256,256]{1,0:T(8,128)(2,1)S(1)} %get-tuple-element.116.refs_1_, bf16[256,128]{1,0:T(8,128)(2,1)S(1)} %get-tuple-element.117.refs_2_, ...), custom_call_target="tpu_custom_call" | custom-call | flops 1000000 | bytes 16384 | tf_op jit(solution)/shard_map/beside/pallas_call | solution.py:545
  44.6 1.3 %collective-permute-start.12 = (bf16[272,128]{1,0:T(8,128)(2,1)S(1)}, bf16[272,128]{1,0:T(8,128)(2,1)S(1)}, u32[]{:S(2)}, u32[]{:S(2)}) collective-permute-start(bf16[272,128]{1,0:T(8,128)(2,1)S(1)} %get-tuple-element.125), channel_id=1, source_target_pairs={{16,0},{20,4},{24,8},{28,12},{17,1},{21,5},{25,9},{29,13},{18,2},{... | collective-permute-start | bytes 208904 | tf_op jit(solution)/shard_map/ppermute | solution.py:560
  45.9 5.8 %collective-permute-done.12.rest_0_ = bf16[272,128]{1,0:T(8,128)(2,1)S(1)} collective-permute-done((bf16[272,128]{1,0:T(8,128)(2,1)S(1)}, bf16[272,128]{1,0:T(8,128)(2,1)S(1)}, u32[]{:S(2)}, u32[]{:S(2)}) %collective-permute-start.12) | collective-permute-done | bytes 69664 | tf_op jit(solution)/shard_map/ppermute | solution.py:560
  52.8 1.5 %late.1 = (bf16[4,208,128]{2,1,0:T(8,128)(2,1)S(1)}, bf16[4,208,128]{2,1,0:T(8,128)(2,1)S(1)}, f32[8,256]{1,0:T(8,128)S(1)}) custom-call(s32[1]{0:T(128)} %bitcast.1.low.refs_0_, f32[32,256]{1,0:T(8,128)S(1)} %get-tuple-element.79.scal.refs_8_.refs_1_, f32[16,256]{1,0:T(8,128)S(1)} %get-tuple-element.127.refs_2_, ...), custom_call_target="tpu_custom_call" | custom-call | flops 1000000 | bytes 16384 | tf_op jit(solution)/shard_map/late/pallas_call | solution.py:545
  55.2 1.4 %collective-permute-start.17 = (bf16[16,512]{1,0:T(8,128)(2,1)S(1)}, bf16[16,512]{1,0:T(8,128)(2,1)S(1)}, u32[]{:S(2)}, u32[]{:S(2)}) collective-permute-start(bf16[16,512]{1,0:T(8,128)(2,1)S(1)} %get-tuple-element.139), channel_id=1, source_target_pairs={{4,0},{8,4},{12,8},{16,12},{20,16},{24,20},{28,24},{5,1},{9,5},{13... | collective-permute-start | bytes 49160 | tf_op jit(solution)/shard_map/ppermute | solution.py:560
  56.6 4.3 %collective-permute-done.17.edge = bf16[16,512]{1,0:T(8,128)(2,1)S(1)} collective-permute-done((bf16[16,512]{1,0:T(8,128)(2,1)S(1)}, bf16[16,512]{1,0:T(8,128)(2,1)S(1)}, u32[]{:S(2)}, u32[]{:S(2)}) %collective-permute-start.17) | collective-permute-done | bytes 16416 | tf_op jit(solution)/shard_map/ppermute | solution.py:560
  62.8 2.1 %collective-permute-start.8 = (bf16[320,128]{1,0:T(8,128)(2,1)S(1)}, bf16[320,128]{1,0:T(8,128)(2,1)S(1)}, u32[]{:S(2)}, u32[]{:S(2)}) collective-permute-start(bf16[320,128]{1,0:T(8,128)(2,1)S(1)} %get-tuple-element.110), channel_id=1, source_target_pairs={{0,8},{4,12},{8,0},{12,4},{16,24},{20,28},{24,16},{28,20},{1,9},{5... | collective-permute-start | bytes 245768 | tf_op jit(solution)/shard_map/ppermute | solution.py:564
  64.9 2.4 %collective-permute-start.10 = (bf16[320,128]{1,0:T(8,128)(2,1)S(1)}, bf16[320,128]{1,0:T(8,128)(2,1)S(1)}, u32[]{:S(2)}, u32[]{:S(2)}) collective-permute-start(bf16[320,128]{1,0:T(8,128)(2,1)S(1)} %get-tuple-element.112), channel_id=1, source_target_pairs={{0,24},{4,28},{8,16},{12,20},{16,8},{20,12},{24,0},{28,4},{1,25},{... | collective-permute-start | bytes 245768 | tf_op jit(solution)/shard_map/ppermute | solution.py:564
  67.4 1.5 %collective-permute-start.19 = (bf16[64,1024]{1,0:T(8,128)(2,1)S(1)}, bf16[64,1024]{1,0:T(8,128)(2,1)S(1)}, u32[]{:S(2)}, u32[]{:S(2)}) collective-permute-start(bf16[64,1024]{1,0:T(8,128)(2,1)S(1)} %copy-done.5), channel_id=1, source_target_pairs={{0,2},{1,3},{2,0},{3,1},{4,6},{5,7},{6,4},{7,5},{8,10},{9,11},{10,... | collective-permute-start | bytes 393224 | tf_op jit(solution)/shard_map/ppermute | solution.py:564
  70.2 4.1 %collective-permute-done.9.refs_2_ = bf16[320,128]{1,0:T(8,128)(2,1)S(1)} collective-permute-done((bf16[320,128]{1,0:T(8,128)(2,1)S(1)}, bf16[320,128]{1,0:T(8,128)(2,1)S(1)}, u32[]{:S(2)}, u32[]{:S(2)}) %collective-permute-start.9) | collective-permute-done | bytes 81952 | tf_op jit(solution)/shard_map/ppermute | solution.py:564
  74.3 1.6 %collective-permute-start.16 = (bf16[208,128]{1,0:T(8,128)(2,1)S(1)}, bf16[208,128]{1,0:T(8,128)(2,1)S(1)}, u32[]{:S(2)}, u32[]{:S(2)}) collective-permute-start(bf16[208,128]{1,0:T(8,128)(2,1)S(1)} %get-tuple-element.136), channel_id=1, source_target_pairs={{0,24},{4,28},{8,16},{12,20},{16,8},{20,12},{24,0},{28,4},{1,25},{... | collective-permute-start | bytes 159752 | tf_op jit(solution)/shard_map/ppermute | solution.py:564
  76.5 4.0 %collective-permute-done.15.refs_2_ = bf16[208,128]{1,0:T(8,128)(2,1)S(1)} collective-permute-done((bf16[208,128]{1,0:T(8,128)(2,1)S(1)}, bf16[208,128]{1,0:T(8,128)(2,1)S(1)}, u32[]{:S(2)}, u32[]{:S(2)}) %collective-permute-start.15) | collective-permute-done | bytes 53280 | tf_op jit(solution)/shard_map/ppermute | solution.py:564
  (50 shorter events, 16.1 us)
Async XLA Ops:
  1.4 7.2 %collective-permute-start = (bf16[16,512]{1,0:T(8,128)(2,1)S(1)}, bf16[16,512]{1,0:T(8,128)(2,1)S(1)}, u32[]{:S(2)}, u32[]{:S(2)}) collective-permute-start(bf16[16,512]{1,0:T(8,128)(2,1)S(1)} %slice.3), channel_id=1, source_target_pairs={{0,4},{4,8},{8,12},{12,16},{16,20},{20,24},{24,28},{1,5},{5,9},{9,... | collective-permute-start | bytes 49160 | tf_op jit(solution)/shard_map/ppermute | solution.py:560
  9.5 4.4 %collective-permute-start.1 = (bf16[272,128]{1,0:T(8,128)(2,1)S(1)}, bf16[272,128]{1,0:T(8,128)(2,1)S(1)}, u32[]{:S(2)}, u32[]{:S(2)}) collective-permute-start(bf16[272,128]{1,0:T(8,128)(2,1)S(1)} %get-tuple-element.80.mine), channel_id=1, source_target_pairs={{0,4},{4,0},{8,12},{12,8},{16,20},{20,16},{24,28},{28,24},{1,5},{5... | collective-permute-start | bytes 208904 | tf_op jit(solution)/shard_map/ppermute | solution.py:564
  13.9 6.2 %collective-permute-start.2 = (bf16[272,128]{1,0:T(8,128)(2,1)S(1)}, bf16[272,128]{1,0:T(8,128)(2,1)S(1)}, u32[]{:S(2)}, u32[]{:S(2)}) collective-permute-start(bf16[272,128]{1,0:T(8,128)(2,1)S(1)} %pair.2.nearer), channel_id=1, source_target_pairs={{0,8},{4,12},{8,16},{12,20},{16,24},{20,28},{1,9},{5,13},{9,17},{1... | collective-permute-start | bytes 208904 | tf_op jit(solution)/shard_map/ppermute | solution.py:560
  20.2 7.2 %collective-permute-start.3 = (bf16[272,128]{1,0:T(8,128)(2,1)S(1)}, bf16[272,128]{1,0:T(8,128)(2,1)S(1)}, u32[]{:S(2)}, u32[]{:S(2)}) collective-permute-start(bf16[272,128]{1,0:T(8,128)(2,1)S(1)} %get-tuple-element.91), channel_id=1, source_target_pairs={{0,16},{4,20},{8,24},{12,28},{1,17},{5,21},{9,25},{13,29},{2,18},{... | collective-permute-start | bytes 208904 | tf_op jit(solution)/shard_map/ppermute | solution.py:560
  28.2 1.2 %collective-permute-start.4 = (f32[8,256]{1,0:T(8,128)S(1)}, f32[8,256]{1,0:T(8,128)S(1)}, u32[]{:S(2)}, u32[]{:S(2)}) collective-permute-start(f32[8,256]{1,0:T(8,128)S(1)} %get-tuple-element.93), channel_id=1, source_target_pairs={{0,1},{1,0},{2,3},{3,2},{4,5},{5,4},{6,7},{7,6},{8,9},{9,8},{10,11... | collective-permute-start | bytes 24584 | tf_op jit(solution)/shard_map/ppermute | solution.py:564
  29.4 3.7 %collective-permute-start.5 = (f32[8,256]{1,0:T(8,128)S(1)}, f32[8,256]{1,0:T(8,128)S(1)}, u32[]{:S(2)}, u32[]{:S(2)}) collective-permute-start(f32[8,256]{1,0:T(8,128)S(1)} %add.9.sums), channel_id=1, source_target_pairs={{0,2},{1,3},{2,0},{3,1},{4,6},{5,7},{6,4},{7,5},{8,10},{9,11},{10,... | collective-permute-start | bytes 24584 | tf_op jit(solution)/shard_map/ppermute | solution.py:564
  33.8 4.4 %collective-permute-start.6 = (bf16[272,128]{1,0:T(8,128)(2,1)S(1)}, bf16[272,128]{1,0:T(8,128)(2,1)S(1)}, u32[]{:S(2)}, u32[]{:S(2)}) collective-permute-start(bf16[272,128]{1,0:T(8,128)(2,1)S(1)} %get-tuple-element.95.mine), channel_id=1, source_target_pairs={{0,4},{4,0},{8,12},{12,8},{16,20},{20,16},{24,28},{28,24},{1,5},{5... | collective-permute-start | bytes 208904 | tf_op jit(solution)/shard_map/ppermute | solution.py:564
  38.2 6.3 %collective-permute-start.11 = (bf16[272,128]{1,0:T(8,128)(2,1)S(1)}, bf16[272,128]{1,0:T(8,128)(2,1)S(1)}, u32[]{:S(2)}, u32[]{:S(2)}) collective-permute-start(bf16[272,128]{1,0:T(8,128)(2,1)S(1)} %pair.3.nearer), channel_id=1, source_target_pairs={{8,0},{12,4},{16,8},{20,12},{24,16},{28,20},{9,1},{13,5},{17,9},{2... | collective-permute-start | bytes 208904 | tf_op jit(solution)/shard_map/ppermute | solution.py:560
  39.5 23.2 %collective-permute-start.7 = (bf16[4,320,128]{2,1,0:T(8,128)(2,1)S(1)}, bf16[4,320,128]{2,1,0:T(8,128)(2,1)S(1)}, u32[]{:S(2)}, u32[]{:S(2)}) collective-permute-start(bf16[4,320,128]{2,1,0:T(8,128)(2,1)S(1)} %get-tuple-element.108), channel_id=1, source_target_pairs={{0,4},{4,0},{8,12},{12,8},{16,20},{20,16},{24,28},{28,24},{1,5},{5... | collective-permute-start | bytes 983048 | tf_op jit(solution)/shard_map/ppermute | solution.py:564
  44.6 7.1 %collective-permute-start.12 = (bf16[272,128]{1,0:T(8,128)(2,1)S(1)}, bf16[272,128]{1,0:T(8,128)(2,1)S(1)}, u32[]{:S(2)}, u32[]{:S(2)}) collective-permute-start(bf16[272,128]{1,0:T(8,128)(2,1)S(1)} %get-tuple-element.125), channel_id=1, source_target_pairs={{16,0},{20,4},{24,8},{28,12},{17,1},{21,5},{25,9},{29,13},{18,2},{... | collective-permute-start | bytes 208904 | tf_op jit(solution)/shard_map/ppermute | solution.py:560
  51.7 9.2 %copy-start = (bf16[512,3,256]{2,0,1:T(8,128)(2,1)S(1)}, bf16[512,3,256]{2,0,1:T(8,128)(2,1)}, u32[]{:S(2)}) copy-start(bf16[512,3,256]{2,0,1:T(8,128)(2,1)} %param.12) | copy-start | bytes 2359300
  54.3 14.5 %collective-permute-start.13 = (bf16[4,208,128]{2,1,0:T(8,128)(2,1)S(1)}, bf16[4,208,128]{2,1,0:T(8,128)(2,1)S(1)}, u32[]{:S(2)}, u32[]{:S(2)}) collective-permute-start(bf16[4,208,128]{2,1,0:T(8,128)(2,1)S(1)} %get-tuple-element.132), channel_id=1, source_target_pairs={{0,4},{4,0},{8,12},{12,8},{16,20},{20,16},{24,28},{28,24},{1,5},{5... | collective-permute-start | bytes 638984 | tf_op jit(solution)/shard_map/ppermute | solution.py:564
  55.2 5.8 %copy-start.3 = (bf16[512,4]{0,1:T(4,128)(2,1)S(1)}, bf16[512,4]{0,1:T(4,128)(2,1)}, u32[]{:S(2)}) copy-start(bf16[512,4]{0,1:T(4,128)(2,1)} %param.13) | copy-start | bytes 12292
  55.2 5.8 %collective-permute-start.17 = (bf16[16,512]{1,0:T(8,128)(2,1)S(1)}, bf16[16,512]{1,0:T(8,128)(2,1)S(1)}, u32[]{:S(2)}, u32[]{:S(2)}) collective-permute-start(bf16[16,512]{1,0:T(8,128)(2,1)S(1)} %get-tuple-element.139), channel_id=1, source_target_pairs={{4,0},{8,4},{12,8},{16,12},{20,16},{24,20},{28,24},{5,1},{9,5},{13... | collective-permute-start | bytes 49160 | tf_op jit(solution)/shard_map/ppermute | solution.py:560
  62.7 4.6 %collective-permute-start.18 = (bf16[64,1024]{1,0:T(8,128)(2,1)}, bf16[64,1024]{1,0:T(8,128)(2,1)S(1)}, u32[]{:S(2)}, u32[]{:S(2)}) collective-permute-start(bf16[64,1024]{1,0:T(8,128)(2,1)} %get-tuple-element.141), channel_id=1, source_target_pairs={{0,1},{1,0},{2,3},{3,2},{4,5},{5,4},{6,7},{7,6},{8,9},{9,8},{10,11... | collective-permute-start | bytes 393224 | tf_op jit(solution)/shard_map/ppermute | solution.py:564
  62.7 4.6 %copy-start.5 = (bf16[64,1024]{1,0:T(8,128)(2,1)S(1)}, bf16[64,1024]{1,0:T(8,128)(2,1)}, u32[]{:S(2)}) copy-start(bf16[64,1024]{1,0:T(8,128)(2,1)} %copy-done.4) | copy-start | bytes 393220
  62.8 6.1 %collective-permute-start.8 = (bf16[320,128]{1,0:T(8,128)(2,1)S(1)}, bf16[320,128]{1,0:T(8,128)(2,1)S(1)}, u32[]{:S(2)}, u32[]{:S(2)}) collective-permute-start(bf16[320,128]{1,0:T(8,128)(2,1)S(1)} %get-tuple-element.110), channel_id=1, source_target_pairs={{0,8},{4,12},{8,0},{12,4},{16,24},{20,28},{24,16},{28,20},{1,9},{5... | collective-permute-start | bytes 245768 | tf_op jit(solution)/shard_map/ppermute | solution.py:564
  64.9 9.3 %collective-permute-start.9 = (bf16[320,128]{1,0:T(8,128)(2,1)S(1)}, bf16[320,128]{1,0:T(8,128)(2,1)S(1)}, u32[]{:S(2)}, u32[]{:S(2)}) collective-permute-start(bf16[320,128]{1,0:T(8,128)(2,1)S(1)} %get-tuple-element.111), channel_id=1, source_target_pairs={{0,16},{4,20},{8,24},{12,28},{16,0},{20,4},{24,8},{28,12},{1,17},{... | collective-permute-start | bytes 245768 | tf_op jit(solution)/shard_map/ppermute | solution.py:564
  64.9 9.3 %collective-permute-start.10 = (bf16[320,128]{1,0:T(8,128)(2,1)S(1)}, bf16[320,128]{1,0:T(8,128)(2,1)S(1)}, u32[]{:S(2)}, u32[]{:S(2)}) collective-permute-start(bf16[320,128]{1,0:T(8,128)(2,1)S(1)} %get-tuple-element.112), channel_id=1, source_target_pairs={{0,24},{4,28},{8,16},{12,20},{16,8},{20,12},{24,0},{28,4},{1,25},{... | collective-permute-start | bytes 245768 | tf_op jit(solution)/shard_map/ppermute | solution.py:564
  67.4 9.1 %collective-permute-start.19 = (bf16[64,1024]{1,0:T(8,128)(2,1)S(1)}, bf16[64,1024]{1,0:T(8,128)(2,1)S(1)}, u32[]{:S(2)}, u32[]{:S(2)}) collective-permute-start(bf16[64,1024]{1,0:T(8,128)(2,1)S(1)} %copy-done.5), channel_id=1, source_target_pairs={{0,2},{1,3},{2,0},{3,1},{4,6},{5,7},{6,4},{7,5},{8,10},{9,11},{10,... | collective-permute-start | bytes 393224 | tf_op jit(solution)/shard_map/ppermute | solution.py:564
  68.9 7.6 %collective-permute-start.20 = (bf16[64,1024]{1,0:T(8,128)(2,1)S(1)}, bf16[64,1024]{1,0:T(8,128)(2,1)S(1)}, u32[]{:S(2)}, u32[]{:S(2)}) collective-permute-start(bf16[64,1024]{1,0:T(8,128)(2,1)S(1)} %get-tuple-element.143), channel_id=1, source_target_pairs={{0,3},{1,2},{2,1},{3,0},{4,7},{5,6},{6,5},{7,4},{8,11},{9,10},{10,... | collective-permute-start | bytes 393224 | tf_op jit(solution)/shard_map/ppermute | solution.py:564
  68.9 7.6 %collective-permute-start.14 = (bf16[208,128]{1,0:T(8,128)(2,1)S(1)}, bf16[208,128]{1,0:T(8,128)(2,1)S(1)}, u32[]{:S(2)}, u32[]{:S(2)}) collective-permute-start(bf16[208,128]{1,0:T(8,128)(2,1)S(1)} %get-tuple-element.134), channel_id=1, source_target_pairs={{0,8},{4,12},{8,0},{12,4},{16,24},{20,28},{24,16},{28,20},{1,9},{5... | collective-permute-start | bytes 159752 | tf_op jit(solution)/shard_map/ppermute | solution.py:564
  74.2 6.2 %collective-permute-start.15 = (bf16[208,128]{1,0:T(8,128)(2,1)S(1)}, bf16[208,128]{1,0:T(8,128)(2,1)S(1)}, u32[]{:S(2)}, u32[]{:S(2)}) collective-permute-start(bf16[208,128]{1,0:T(8,128)(2,1)S(1)} %get-tuple-element.135), channel_id=1, source_target_pairs={{0,16},{4,20},{8,24},{12,28},{16,0},{20,4},{24,8},{28,12},{1,17},{... | collective-permute-start | bytes 159752 | tf_op jit(solution)/shard_map/ppermute | solution.py:564
  74.3 6.2 %collective-permute-start.16 = (bf16[208,128]{1,0:T(8,128)(2,1)S(1)}, bf16[208,128]{1,0:T(8,128)(2,1)S(1)}, u32[]{:S(2)}, u32[]{:S(2)}) collective-permute-start(bf16[208,128]{1,0:T(8,128)(2,1)S(1)} %get-tuple-element.136), channel_id=1, source_target_pairs={{0,24},{4,28},{8,16},{12,20},{16,8},{20,12},{24,0},{28,4},{1,25},{... | collective-permute-start | bytes 159752 | tf_op jit(solution)/shard_map/ppermute | solution.py:564
  (3 other events, 5.8 us)
